TPU v7x, 32 devices: a whole 2x2x4 slice. The times are simulated.
32 devices in a mesh: ctx: 8 (over z, y), head: 4 (over x, core).
Axes of the slice: x: 2, y: 2, z: 4, core: 2. Of those that a mesh axis runs over, the one named last changes fastest.
Arguments:
- queries: bfloat16 [2048, 2048], P('ctx', 'head'), may hold values from -32 to 32
- keys: bfloat16 [2048, 1024], P('ctx', 'head'), may hold values from -32 to 32
- values: bfloat16 [2048, 1024], P('ctx', 'head'), may hold values from -6 to 6
- doc_ids: int32 [16], replicated, may hold values from 0 to 2, as said below
- out_weight: bfloat16 [2048, 5376], P('head'), may hold values from -1 to 1
Outputs:
- projected: bfloat16 [2048, 5376], P(('ctx', 'head'))
Inputs may be any that keep to these rules, and one draw needn't show every extreme that they name: doc_ids is non-decreasing along the sequence and starts at 0; the first document spans exactly 12 blocks, every other one 1 or more blocks.
All inputs are finite; a program needn't handle non-finite values.
Results may differ from a plain program's by a relative error of at most 0.015.
Values may be sent and summed in bfloat16 or wider, within the bound.
No kernel may reach another device: no remote copies, remote signals or barrier semaphores. Data moves between devices by JAX's collectives and lax.ppermute only.
A program may use at most 64 MiB of HBM per device.

v0:
```python
import functools

import jax
import jax.numpy as jnp
from jax import lax
from jax.experimental import pallas as pl
from jax.experimental.pallas import tpu as pltpu
from jax.sharding import PartitionSpec as P

HEAD_SIZE = 128
BLOCK = 128
SCALE = 168.0 ** (-0.5)
LOG2E = 1.4426950408889634
NEG = -1e30
VMEM = pl.BlockSpec(memory_space=pltpu.VMEM)
SMEM = pl.BlockSpec(memory_space=pltpu.SMEM)
HBM = pl.BlockSpec(memory_space=pltpu.HBM)
LIMIT = pltpu.CompilerParams(vmem_limit_bytes=32 * 1024 * 1024)


def hop(block, axis, pairs):
    return lax.ppermute(block, axis, pairs)


def describe(position, place, doc_ids, n_ctx):
    first = n_ctx * 3 // 4
    in_first = position < first
    chunks = [
        (position, position >= 0),
        (position ^ 1, position % 2 == 1),
        (position - 2, in_first & (position >= 2)),
        (position - 4, in_first & (position >= 4)),
        ((position - 2) ^ 1, in_first & (position >= 2)),
        ((position - 4) ^ 1, in_first & (position >= 4)),
    ]
    numbers = [position, place]
    for source, there in chunks:
        numbers += [jnp.where(there, source, 0), there.astype(jnp.int32)]
    return jnp.concatenate([jnp.stack(numbers), doc_ids])


CHUNKS = 6
BESIDE = ((0, 1), (2, 3), (4, 5), (6, 7))
BY_TWO = ((0, 2, 4), (1, 3, 5), (6, 7))
BY_FOUR = ((0, 4, 2), (1, 5, 3), (6, 7))


def after(x, state):
    return lax.optimization_barrier((x, state[0]))[0]


def cycles(rings):
    return [(ring[i], ring[(i + 1) % len(ring)]) for ring in rings for i in range(len(ring))]


def score_blocks(info, q, a, h, chunks, numbers):
    docs = 2 + 2 * CHUNKS
    position = info[0]
    rows = q.shape[0]
    n_query = chunks[0][0].shape[0]
    q_blocks = n_query // BLOCK
    doc = info[docs + position * q_blocks + a]
    row = lax.broadcasted_iota(jnp.int32, (rows, BLOCK), 0) % BLOCK
    col = lax.broadcasted_iota(jnp.int32, (rows, BLOCK), 1)
    scores = []
    for (keys, _), c in zip(chunks, numbers):
        count = (a + 1) * BLOCK if c == 0 else n_query
        k = keys[:count, h * HEAD_SIZE : (h + 1) * HEAD_SIZE]
        s = lax.dot_general(q, k, (((1,), (1,)), ((), ())), preferred_element_type=jnp.float32)
        source, there = info[2 + 2 * c], info[3 + 2 * c]
        for b in range(count // BLOCK):
            part = s[:, b * BLOCK : (b + 1) * BLOCK]
            if c == 0 and b == a:
                part = jnp.where(row >= col, part, NEG)
            else:
                seen = (info[docs + source * q_blocks + b] == doc) & (there == 1)
                part = part + jnp.where(seen, 0.0, NEG)
            scores.append(part)
    return scores


def weigh(scores, peak, factor, a, h, chunks, numbers):
    n_query = chunks[0][0].shape[0]
    total = added = None
    scores = list(scores)
    for (_, values), c in zip(chunks, numbers):
        count = (a + 1) * BLOCK if c == 0 else n_query
        parts = []
        for b in range(count // BLOCK):
            w = jnp.exp2(scores.pop(0) * factor - peak)
            total = w if total is None else total + w
            parts.append(w.astype(jnp.bfloat16))
        w = jnp.concatenate(parts, axis=1) if len(parts) > 1 else parts[0]
        v = values[:count, h * HEAD_SIZE : (h + 1) * HEAD_SIZE]
        term = jnp.dot(w, v, preferred_element_type=jnp.float32)
        added = term if added is None else added + term
    return total, added


def head_slices(queries, keys, h):
    group = queries.shape[1] // keys.shape[1]
    return [slice((h * group + g) * HEAD_SIZE, (h * group + g + 1) * HEAD_SIZE) for g in range(group)]


def absorb(numbers, info, queries, chunks, before, after):
    n_query = queries.shape[0]
    factor = SCALE * LOG2E
    at = 0
    for a in range(n_query // BLOCK):
        for h in range(chunks[0][0].shape[1] // HEAD_SIZE):
            heads = head_slices(queries, chunks[0][0], h)
            q = jnp.concatenate([queries[a * BLOCK : (a + 1) * BLOCK, s] for s in heads], axis=0)
            scores = score_blocks(info, q, a, h, chunks, numbers)
            rows = slice(at, at + q.shape[0])
            at += q.shape[0]
            peak = functools.reduce(jnp.maximum, scores)
            peak = jnp.max(peak, axis=1, keepdims=True) * factor
            if before is None:
                total, added = weigh(scores, peak, factor, a, h, chunks, numbers)
                peak = jnp.broadcast_to(peak, (q.shape[0], HEAD_SIZE))
            else:
                last = before[0][rows, :]
                peak = jnp.maximum(last, peak)
                shrink = jnp.exp2(last - peak)
                total, added = weigh(scores, peak, factor, a, h, chunks, numbers)
                total = total + before[1][rows, :] * shrink
                added = added + before[2][rows, :] * shrink
            after(a, heads, rows, peak, total, added)


def store_state(state):
    def after(a, heads, rows, *parts):
        for ref, part in zip(state, parts):
            ref[rows, :] = part

    return after


def pairs_of(refs):
    return list(zip(refs[0::2], refs[1::2]))


def first_kernel(numbers, info, queries_in, keys_in, values_in, weight_in, *refs):
    pairs = 2 * len(numbers) - 2
    *state, queries, weight, keys, values, sems = refs[pairs:]
    chunks = [(keys, values)] + pairs_of(refs[:pairs])
    places = ((queries_in, queries), (keys_in, keys), (values_in, values), (weight_in, weight))
    fetches = [pltpu.make_async_copy(a, b, sems.at[i]) for i, (a, b) in enumerate(places)]
    for fetch in fetches:
        fetch.start()
    for fetch in fetches[:3]:
        fetch.wait()
    absorb(numbers, info, queries, chunks, None, store_state(state))
    fetches[3].wait()


def next_kernel(numbers, info, queries, *refs):
    pairs = 2 * len(numbers)
    absorb(numbers, info, queries, pairs_of(refs[3 : 3 + pairs]), refs[:3], store_state(refs[3 + pairs :]))


def attend_cost(queries, numbers, fetched=0):
    n_query, width = queries.shape
    count = len(numbers) * n_query
    return pl.CostEstimate(
        flops=4 * n_query * width * count,
        bytes_accessed=fetched,
        transcendentals=n_query * count * width // HEAD_SIZE,
    )


def state_shapes(queries):
    rows = queries.size // HEAD_SIZE
    return (pltpu.VMEM((rows, HEAD_SIZE), jnp.float32),) * 3


def attend_first(info, queries, keys, values, weight, chunks, numbers):
    return pl.pallas_call(
        functools.partial(first_kernel, numbers),
        out_shape=state_shapes(queries)
        + (pltpu.VMEM(queries.shape, queries.dtype), pltpu.VMEM(weight.shape, weight.dtype)),
        in_specs=[SMEM, HBM, HBM, HBM, HBM] + [VMEM] * (2 * len(chunks)),
        out_specs=(VMEM,) * 5,
        scratch_shapes=[
            pltpu.VMEM(keys.shape, keys.dtype),
            pltpu.VMEM(values.shape, values.dtype),
            pltpu.SemaphoreType.DMA((4,)),
        ],
        compiler_params=LIMIT,
        cost_estimate=attend_cost(queries, numbers, 2 * weight.size),
        name="attend_first",
    )(
        info,
        *[pltpu.with_memory_space_constraint(x, pltpu.HBM) for x in (queries, keys, values, weight)],
        *[x for pair in chunks for x in pair],
    )


def attend_next(info, queries, state, chunks, numbers):
    return pl.pallas_call(
        functools.partial(next_kernel, numbers),
        out_shape=state_shapes(queries),
        in_specs=[SMEM] + [VMEM] * (4 + 2 * len(chunks)),
        out_specs=(VMEM,) * 3,
        compiler_params=LIMIT,
        cost_estimate=attend_cost(queries, numbers),
        name="attend_next",
    )(info, queries, *state, *[x for pair in chunks for x in pair])


def last_kernel(numbers, columns, info, queries, weight, *refs):
    pairs = 2 * len(numbers)
    chunks = pairs_of(refs[3 : 3 + pairs])
    far, near, mine, send, attended = refs[3 + pairs :]

    def after(a, heads, rows, peak, total, added):
        result = (added / jnp.sum(total, axis=1, keepdims=True)).astype(jnp.bfloat16)
        for g, head in enumerate(heads):
            attended[a * BLOCK : (a + 1) * BLOCK, head] = result[g * BLOCK : (g + 1) * BLOCK]

    absorb(numbers, info, queries, chunks, refs[:3], after)
    place = info[1]
    share = queries.shape[0] // 4
    for half, owners in ((far, (place ^ 2, place ^ 3)), (near, (place, place ^ 1))):
        for i, owner in enumerate(owners):
            source = pl.ds(pl.multiple_of(owner * share, share), share)
            half[i * share : (i + 1) * share, :] = attended[source, :]
    project_columns(far, weight, mine, (send,), *columns)


def attend_last(info, queries, weight, state, chunks, numbers, columns):
    n_query, width = queries.shape
    half = jax.ShapeDtypeStruct((n_query // 2, width), jnp.bfloat16)
    return pl.pallas_call(
        functools.partial(last_kernel, numbers, columns),
        out_shape=(half, half) + project_shapes(n_query // 4, columns[1] - columns[0]),
        in_specs=[SMEM] + [VMEM] * (5 + 2 * len(numbers)),
        out_specs=(VMEM,) * 4,
        scratch_shapes=[pltpu.VMEM(queries.shape, jnp.bfloat16)],
        compiler_params=LIMIT,
        cost_estimate=attend_cost(queries, numbers),
        name="attend_last",
    )(info, queries, weight, *state, *[x for pair in chunks for x in pair])


def project_shapes(rows, count, sends=1):
    send = jax.ShapeDtypeStruct((rows, count // sends), jnp.bfloat16)
    return (jax.ShapeDtypeStruct((rows, count), jnp.float32),) + (send,) * sends


def project_columns(rows, weight, mine, sends, start, end):
    share = rows.shape[0] // 2
    width = sends[0].shape[1]
    for at in range(start, end, width):
        for left in range(at, at + width, 768):
            right = min(left + 768, at + width)
            product = jnp.dot(rows[...], weight[:, left:right], preferred_element_type=jnp.float32)
            mine[:, left - start : right - start] = product[:share]
            send = sends[(at - start) // width]
            send[:, left - at : right - at] = product[share:].astype(send.dtype)


def project_kernel(columns, rows, weight, mine, *sends):
    project_columns(rows, weight, mine, sends, *columns)


def project(rows, weight, columns, sends=1):
    count = columns[1] - columns[0]
    return pl.pallas_call(
        functools.partial(project_kernel, columns),
        out_shape=project_shapes(rows.shape[0] // 2, count, sends),
        in_specs=[VMEM, VMEM],
        out_specs=(VMEM,) * (1 + sends),
        compiler_params=LIMIT,
        cost_estimate=pl.CostEstimate(
            flops=2 * rows.shape[0] * rows.shape[1] * count, bytes_accessed=0, transcendentals=0
        ),
        name="project",
    )(rows, weight)


def add_kernel(mine, theirs, out):
    out[...] = (mine[...] + theirs[...].astype(jnp.float32)).astype(out.dtype)


def add_up(mine, theirs):
    return pl.pallas_call(
        add_kernel,
        out_shape=jax.ShapeDtypeStruct(theirs.shape, theirs.dtype),
        in_specs=[VMEM, VMEM],
        out_specs=VMEM,
        compiler_params=LIMIT,
        cost_estimate=pl.CostEstimate(flops=theirs.size, bytes_accessed=0, transcendentals=0),
        name="add_up",
    )(mine, theirs)


def combine_kernel(counts, mine, *refs):
    out = refs[-1]
    ends = []
    for part in (refs[: counts[0]], refs[counts[0] : -1]):
        at, pieces = 0, []
        for ref in part:
            pieces.append((at, at + ref.shape[1], ref))
            at += ref.shape[1]
        ends.append(pieces)
    for low, high, beside in ends[0]:
        for start, stop, across in ends[1]:
            left, right = max(low, start), min(high, stop)
            if left < right:
                total = mine[:, left:right] + beside[:, left - low : right - low].astype(jnp.float32)
                total += across[:, left - start : right - start].astype(jnp.float32)
                out[:, left:right] = total.astype(out.dtype)


def combine(mine, beside, across):
    return pl.pallas_call(
        functools.partial(combine_kernel, (len(beside), len(across))),
        out_shape=jax.ShapeDtypeStruct(mine.shape, across[0].dtype),
        in_specs=[VMEM] * (1 + len(beside) + len(across)),
        out_specs=VMEM,
        compiler_params=LIMIT,
        name="combine",
    )(mine, *beside, *across)


def from_behind(block, axis, distance):
    devices = range(lax.axis_size(axis))
    route = [(i - distance, i) for i in devices if i - distance in devices]
    return lax.ppermute(block, axis, route)


def token_docs(doc_ids, start, count):
    blocks = (start + jnp.arange(count, dtype=jnp.int32)) // BLOCK
    table = blocks[:, None] == jnp.arange(doc_ids.shape[0], dtype=jnp.int32)[None, :]
    return jnp.sum(jnp.where(table, doc_ids[None, :], 0), axis=1)


def attend(carry, queries, q_docs, q_start, k_piece, v_piece, k_docs, k_start):
    peak, totals, accum = carry
    n_query = queries.shape[0]
    n_key = k_piece.shape[0]
    kv_heads = k_piece.shape[1] // HEAD_SIZE
    query_group = queries.shape[1] // k_piece.shape[1]
    q_heads = queries.reshape(n_query, kv_heads, query_group, HEAD_SIZE)
    k_heads = k_piece.reshape(n_key, kv_heads, HEAD_SIZE)
    v_heads = v_piece.reshape(n_key, kv_heads, HEAD_SIZE)
    scores = (
        jnp.einsum("qkgd,skd->kgqs", q_heads, k_heads, preferred_element_type=jnp.float32) * SCALE
    )
    q_pos = q_start + jnp.arange(n_query, dtype=jnp.int32)
    k_pos = k_start + jnp.arange(n_key, dtype=jnp.int32)
    allowed = (q_docs[:, None] == k_docs[None, :]) & (q_pos[:, None] >= k_pos[None, :])
    scores = jnp.where(allowed, scores, NEG)
    new_peak = jnp.maximum(peak, jnp.max(scores, axis=-1))
    shrink = jnp.exp(peak - new_peak)
    weights = jnp.exp(scores - new_peak[..., None])
    totals = totals * shrink + jnp.sum(weights, axis=-1)
    rounded = weights.astype(jnp.bfloat16)
    added = jnp.einsum("kgqs,skd->kgqd", rounded, v_heads, preferred_element_type=jnp.float32)
    accum = accum * shrink[..., None] + added
    return (new_peak, totals, accum)


def absorb_block(carry, queries, q_docs, q_start, k_piece, v_piece, k_start, doc_ids, flag):
    n_key = k_piece.shape[0]
    k_docs = token_docs(doc_ids, k_start, n_key)
    fresh = attend(carry, queries, q_docs, q_start, k_piece, v_piece, k_docs, k_start)
    return jax.tree.map(lambda new, old: jnp.where(flag, new, old), fresh, carry)


def ring_attention(queries, keys, values, doc_ids, n_ctx, position):
    n_query = queries.shape[0]
    q_start = position * n_query
    q_docs = token_docs(doc_ids, q_start, n_query)
    kv_heads = keys.shape[1] // HEAD_SIZE
    query_group = queries.shape[1] // keys.shape[1]
    carry = (
        jnp.full((kv_heads, query_group, n_query), NEG, jnp.float32),
        jnp.zeros((kv_heads, query_group, n_query), jnp.float32),
        jnp.zeros((kv_heads, query_group, n_query, HEAD_SIZE), jnp.float32),
    )
    always = jnp.array(True)
    carry = absorb_block(carry, queries, q_docs, q_start, keys, values, q_start, doc_ids, always)

    def turn_one(step, state):
        inner_state, moving = state
        moving = from_behind(moving, "ctx", 1)
        start = ((position - step) % n_ctx) * n_query
        inner_state = absorb_block(
            inner_state, queries, q_docs, q_start, moving[0], moving[1], start, doc_ids, always
        )
        return (inner_state, moving)

    _, totals, accum = lax.fori_loop(1, n_ctx, turn_one, (carry, jnp.stack((keys, values))))[0]
    result = accum / totals[..., None]
    return jnp.transpose(result, (2, 0, 1, 3)).reshape(queries.shape).astype(jnp.bfloat16)


def part_rows(attended, place):
    share = attended.shape[0] // 4
    rows = [lax.dynamic_slice_in_dim(attended, (place ^ flip) * share, share, 0) for flip in (2, 3, 0, 1)]
    return jnp.concatenate(rows[:2], axis=0), jnp.concatenate(rows[2:], axis=0)


def per_device(queries, keys, values, doc_ids, out_weight):
    n_ctx = lax.axis_size("ctx")
    heads = lax.axis_size("head")
    position = lax.axis_index("ctx")
    place = lax.axis_index("head")
    other_core = [(i, i ^ 1) for i in range(heads)]
    other_chip = [(i, i ^ 2) for i in range(heads)]
    columns = out_weight.shape[1]
    cut = columns * 4 // 7 // BLOCK * BLOCK

    if n_ctx == 8:
        by_two = [hop(x, "ctx", cycles(BY_TWO)) for x in (keys, values)]
        by_four = [hop(x, "ctx", cycles(BY_FOUR)) for x in (keys, values)]
        beside = [hop(x, "ctx", cycles(BESIDE)) for x in (keys, values)]
        info = describe(position, place, doc_ids, n_ctx)
        *state, fetched, weight = attend_first(
            info, queries, keys, values, out_weight, [beside], (0, 1)
        )
        by_two = [after(x, state) for x in by_two]
        swap_two = [hop(x, "ctx", cycles(BESIDE)) for x in by_two]
        state = attend_next(info, fetched, state, [by_two], (2,))
        by_four = [after(x, state) for x in by_four]
        swap_four = [hop(x, "ctx", cycles(BESIDE)) for x in by_four]
        state = attend_next(info, fetched, state, [by_four, swap_two], (3, 4))
        far, near, mine, send = attend_last(info, fetched, weight, state, [swap_four], (5,), (0, cut))
    else:
        weight = out_weight
        attended = ring_attention(queries, keys, values, doc_ids, n_ctx, position)
        far, near = part_rows(attended, place)
        mine, send = project(far, weight, (0, cut))
    theirs = hop(send, "head", other_core)
    later_mine, later_send = project(far, weight, (cut, columns))
    mine, later_mine = lax.optimization_barrier((mine, later_mine))
    first_sum = add_up(mine, theirs)
    first_part = hop(first_sum, "head", other_chip)
    later_theirs = hop(later_send, "head", other_core)
    later_mine, first_sum = lax.optimization_barrier((later_mine, first_sum))
    later_sum = add_up(later_mine, later_theirs)
    second_part = hop(later_sum, "head", other_chip)
    near, later_sum = lax.optimization_barrier((near, later_sum))
    mine, *sends = project(near, weight, (0, columns), 3)
    theirs = [hop(send, "head", other_core) for send in sends]
    return combine(mine, theirs, (first_part, second_part))


def solution(mesh):
    placed = (P("ctx", "head"), P("ctx", "head"), P("ctx", "head"), P(), P("head", None))
    return jax.shard_map(
        per_device, mesh=mesh, in_specs=placed, out_specs=P(("ctx", "head"), None), check_vma=False
    )
```

profile of v0, /device:TPU:30, one launch (start us, length us, event | category | flops | bytes accessed | tf_op | source)
XLA Modules:
  0.0 53.2 jit_solution(8974017558311075372)
XLA Ops:
  0.0 0.5 collective-permute-start
  0.5 1.5 %collective-permute-start.1 = (bf16[256,256]{1,0:T(8,128)(2,1)}, bf16[256,256]{1,0:T(8,128)(2,1)S(1)}, u32[]{:S(2)}, u32[]{:S(2)}) collective-permute-start(bf16[256,256]{1,0:T(8,128)(2,1)} %values_in.1), channel_id=1, source_target_pairs={{0,4},{4,0},{8,12},{12,8},{16,20},{20,16},{24,28},{28,24},{1,5},{5... | collective-permute-start | bytes 393224 | tf_op jit(solution)/shard_map/ppermute | solution.py:22
  2.0 0.5 collective-permute-start.2
  2.5 1.5 %collective-permute-start.3 = (bf16[256,256]{1,0:T(8,128)(2,1)}, bf16[256,256]{1,0:T(8,128)(2,1)S(1)}, u32[]{:S(2)}, u32[]{:S(2)}) collective-permute-start(bf16[256,256]{1,0:T(8,128)(2,1)} %values_in.1), channel_id=1, source_target_pairs={{0,8},{8,16},{16,0},{4,12},{12,20},{20,4},{24,28},{28,24},{1,9},{9... | collective-permute-start | bytes 393224 | tf_op jit(solution)/shard_map/ppermute | solution.py:22
  4.1 0.5 collective-permute-start.4
  4.6 2.0 %collective-permute-done.refs_0_ = bf16[256,256]{1,0:T(8,128)(2,1)S(1)} collective-permute-done((bf16[256,256]{1,0:T(8,128)(2,1)}, bf16[256,256]{1,0:T(8,128)(2,1)S(1)}, u32[]{:S(2)}, u32[]{:S(2)}) %collective-permute-start) | collective-permute-done | bytes 131104 | tf_op jit(solution)/shard_map/ppermute | solution.py:22
  6.6 0.5 collective-permute-start.5
  7.1 0.7 %concatenate.3.info = s32[30]{0:T(128)S(1)} concatenate(s32[1]{0:T(128)} %bitcast, s32[1]{0:T(128)} %bitcast.1, s32[1]{0:T(128)} %bitcast.2, s32[1]{0:T(128)} %bitcast.3, s32[1]{0:T(128)} %bitcast.4, s32[1]{0:T(128)} %bitcast.5, s32[1]{0:T(128)} %bitcast.6, s32[1]{0:T(128)} %bitcast.7, s32[1]{0:T(128)} %bitcast.8, s32[1]{0:T(128)} %bitcast.9, s32[1]{0:T(128)} %bitcast.10, ...), dimensions={0} | concatenate | bytes 240 | tf_op jit(solution)/shard_map/concatenate | solution.py:39
  7.8 1.6 %collective-permute-done.1.refs_1_ = bf16[256,256]{1,0:T(8,128)(2,1)S(1)} collective-permute-done((bf16[256,256]{1,0:T(8,128)(2,1)}, bf16[256,256]{1,0:T(8,128)(2,1)S(1)}, u32[]{:S(2)}, u32[]{:S(2)}) %collective-permute-start.1) | collective-permute-done | bytes 131104 | tf_op jit(solution)/shard_map/ppermute | solution.py:22
  9.4 3.4 %attend_first.1 = (f32[1024,128]{1,0:T(8,128)S(1)}, f32[1024,128]{1,0:T(8,128)S(1)}, f32[1024,128]{1,0:T(8,128)S(1)}, bf16[256,512]{1,0:T(8,128)(2,1)S(1)}, bf16[512,5376]{1,0:T(8,128)(2,1)S(1)}) custom-call(s32[30]{0:T(128)S(1)} %concatenate.3.info, bf16[256,512]{1,0:T(8,128)(2,1)} %queries_in.1, bf16[256,256]{1,0:T(8,128)(2,1)} %keys_in.1, ...), custom_call_target="tpu_custom_call" | custom-call | flops 268435456 | bytes 5505024 | tf_op jit(solution)/shard_map/attend_first/pallas_call | solution.py:178
  12.8 2.2 %collective-permute-done.3.refs_4_ = bf16[256,256]{1,0:T(8,128)(2,1)S(1)} collective-permute-done((bf16[256,256]{1,0:T(8,128)(2,1)}, bf16[256,256]{1,0:T(8,128)(2,1)S(1)}, u32[]{:S(2)}, u32[]{:S(2)}) %collective-permute-start.3) | collective-permute-done | bytes 131104 | tf_op jit(solution)/shard_map/ppermute | solution.py:22
  15.0 0.5 collective-permute-start.6
  15.5 1.5 %collective-permute-start.7 = (bf16[256,256]{1,0:T(8,128)(2,1)S(1)}, bf16[256,256]{1,0:T(8,128)(2,1)S(1)}, u32[]{:S(2)}, u32[]{:S(2)}) collective-permute-start(bf16[256,256]{1,0:T(8,128)(2,1)S(1)} %collective-permute-done.3.refs_4_), channel_id=1, source_target_pairs={{0,4},{4,0},{8,12},{12,8},{16,20},{20,16},{24,28},{28,24},{1,5},{5... | collective-permute-start | bytes 393224 | tf_op jit(solution)/shard_map/ppermute | solution.py:22
  17.0 1.4 %attend_next.2 = (f32[1024,128]{1,0:T(8,128)S(1)}, f32[1024,128]{1,0:T(8,128)S(1)}, f32[1024,128]{1,0:T(8,128)S(1)}) custom-call(s32[30]{0:T(128)S(1)} %concatenate.3.info, bf16[256,512]{1,0:T(8,128)(2,1)S(1)} %get-tuple-element.34.queries, f32[1024,128]{1,0:T(8,128)S(1)} %get-tuple-element.36.refs_0_, f32[1024,128]{1,0:T(8,128)S(1)} %get-tuple-element.37.refs_1_, ...), custom_call_target="tpu_custom_call" | custom-call | flops 134217728 | tf_op jit(solution)/shard_map/attend_next/pallas_call | solution.py:200
  18.5 2.2 %collective-permute-done.5.refs_4_ = bf16[256,256]{1,0:T(8,128)(2,1)S(1)} collective-permute-done((bf16[256,256]{1,0:T(8,128)(2,1)}, bf16[256,256]{1,0:T(8,128)(2,1)S(1)}, u32[]{:S(2)}, u32[]{:S(2)}) %collective-permute-start.5) | collective-permute-done | bytes 131104 | tf_op jit(solution)/shard_map/ppermute | solution.py:22
  20.6 0.5 collective-permute-start.8
  21.1 1.5 %collective-permute-start.9 = (bf16[256,256]{1,0:T(8,128)(2,1)S(1)}, bf16[256,256]{1,0:T(8,128)(2,1)S(1)}, u32[]{:S(2)}, u32[]{:S(2)}) collective-permute-start(bf16[256,256]{1,0:T(8,128)(2,1)S(1)} %collective-permute-done.5.refs_4_), channel_id=1, source_target_pairs={{0,4},{4,0},{8,12},{12,8},{16,20},{20,16},{24,28},{28,24},{1,5},{5... | collective-permute-start | bytes 393224 | tf_op jit(solution)/shard_map/ppermute | solution.py:22
  22.7 0.8 %collective-permute-done.6.refs_5_ = bf16[256,256]{1,0:T(8,128)(2,1)S(1)} collective-permute-done((bf16[256,256]{1,0:T(8,128)(2,1)S(1)}, bf16[256,256]{1,0:T(8,128)(2,1)S(1)}, u32[]{:S(2)}, u32[]{:S(2)}) %collective-permute-start.6) | collective-permute-done | bytes 131104 | tf_op jit(solution)/shard_map/ppermute | solution.py:22
  23.4 2.8 %collective-permute-done.7.refs_6_ = bf16[256,256]{1,0:T(8,128)(2,1)S(1)} collective-permute-done((bf16[256,256]{1,0:T(8,128)(2,1)S(1)}, bf16[256,256]{1,0:T(8,128)(2,1)S(1)}, u32[]{:S(2)}, u32[]{:S(2)}) %collective-permute-start.7) | collective-permute-done | bytes 131104 | tf_op jit(solution)/shard_map/ppermute | solution.py:22
  26.3 2.0 %attend_next.3 = (f32[1024,128]{1,0:T(8,128)S(1)}, f32[1024,128]{1,0:T(8,128)S(1)}, f32[1024,128]{1,0:T(8,128)S(1)}) custom-call(s32[30]{0:T(128)S(1)} %concatenate.3.info, bf16[256,512]{1,0:T(8,128)(2,1)S(1)} %get-tuple-element.34.queries, f32[1024,128]{1,0:T(8,128)S(1)} %get-tuple-element.41.refs_0_, f32[1024,128]{1,0:T(8,128)S(1)} %get-tuple-element.42.refs_1_, ...), custom_call_target="tpu_custom_call" | custom-call | flops 268435456 | tf_op jit(solution)/shard_map/attend_next/pallas_call | solution.py:200
  28.2 0.8 %collective-permute-done.8.refs_3_ = bf16[256,256]{1,0:T(8,128)(2,1)S(1)} collective-permute-done((bf16[256,256]{1,0:T(8,128)(2,1)S(1)}, bf16[256,256]{1,0:T(8,128)(2,1)S(1)}, u32[]{:S(2)}, u32[]{:S(2)}) %collective-permute-start.8) | collective-permute-done | bytes 131104 | tf_op jit(solution)/shard_map/ppermute | solution.py:22
  29.1 1.7 %collective-permute-done.9.refs_4_ = bf16[256,256]{1,0:T(8,128)(2,1)S(1)} collective-permute-done((bf16[256,256]{1,0:T(8,128)(2,1)S(1)}, bf16[256,256]{1,0:T(8,128)(2,1)S(1)}, u32[]{:S(2)}, u32[]{:S(2)}) %collective-permute-start.9) | collective-permute-done | bytes 131104 | tf_op jit(solution)/shard_map/ppermute | solution.py:22
  30.7 2.0 %attend_last.1 = (bf16[128,512]{1,0:T(8,128)(2,1)S(1)}, bf16[128,512]{1,0:T(8,128)(2,1)S(1)}, f32[64,3072]{1,0:T(8,128)S(1)}, bf16[64,3072]{1,0:T(8,128)(2,1)S(1)}) custom-call(s32[30]{0:T(128)S(1)} %concatenate.3.info, bf16[256,512]{1,0:T(8,128)(2,1)S(1)} %get-tuple-element.34.queries, bf16[512,5376]{1,0:T(8,128)(2,1)S(1)} %get-tuple-element.35.weight, ...), custom_call_target="tpu_custom_call" | custom-call | flops 134217728 | tf_op jit(solution)/shard_map/attend_last/pallas_call | solution.py:234
  33.3 0.6 %collective-permute-start.11 = (bf16[64,2304]{1,0:T(8,128)(2,1)S(1)}, bf16[64,2304]{1,0:T(8,128)(2,1)S(1)}, u32[]{:S(2)}, u32[]{:S(2)}) collective-permute-start(bf16[64,2304]{1,0:T(8,128)(2,1)S(1)} %get-tuple-element.57), channel_id=1, source_target_pairs={{0,1},{1,0},{2,3},{3,2},{4,5},{5,4},{6,7},{7,6},{8,9},{9,8},{10,11... | collective-permute-start | bytes 884744 | tf_op jit(solution)/shard_map/ppermute | solution.py:22
  33.8 0.7 %collective-permute-done.10.theirs = bf16[64,3072]{1,0:T(8,128)(2,1)S(1)} collective-permute-done((bf16[64,3072]{1,0:T(8,128)(2,1)S(1)}, bf16[64,3072]{1,0:T(8,128)(2,1)S(1)}, u32[]{:S(2)}, u32[]{:S(2)}) %collective-permute-start.10) | collective-permute-done | bytes 393248 | tf_op jit(solution)/shard_map/ppermute | solution.py:22
  34.6 0.6 %collective-permute-start.15 = (bf16[64,3072]{1,0:T(8,128)(2,1)S(1)}, bf16[64,3072]{1,0:T(8,128)(2,1)S(1)}, u32[]{:S(2)}, u32[]{:S(2)}) collective-permute-start(bf16[64,3072]{1,0:T(8,128)(2,1)S(1)} %add_up.2), channel_id=1, source_target_pairs={{0,2},{1,3},{2,0},{3,1},{4,6},{5,7},{6,4},{7,5},{8,10},{9,11},{10,... | collective-permute-start | bytes 1179656 | tf_op jit(solution)/shard_map/ppermute | solution.py:22
  35.3 1.6 %collective-permute-start.16 = (bf16[64,2304]{1,0:T(8,128)(2,1)S(1)}, bf16[64,2304]{1,0:T(8,128)(2,1)S(1)}, u32[]{:S(2)}, u32[]{:S(2)}) collective-permute-start(bf16[64,2304]{1,0:T(8,128)(2,1)S(1)} %add_up.3), channel_id=1, source_target_pairs={{0,2},{1,3},{2,0},{3,1},{4,6},{5,7},{6,4},{7,5},{8,10},{9,11},{10,... | collective-permute-start | bytes 884744 | tf_op jit(solution)/shard_map/ppermute | solution.py:22
  36.8 0.9 %project.3 = (f32[64,5376]{1,0:T(8,128)S(1)}, bf16[64,1792]{1,0:T(8,128)(2,1)S(1)}, bf16[64,1792]{1,0:T(8,128)(2,1)S(1)}, bf16[64,1792]{1,0:T(8,128)(2,1)S(1)}) custom-call(bf16[128,512]{1,0:T(8,128)(2,1)S(1)} %get-tuple-element.58.rows, bf16[512,5376]{1,0:T(8,128)(2,1)S(1)} %get-tuple-element.35.weight), custom_call_target="tpu_custom_call" | custom-call | flops 704643072 | tf_op jit(solution)/shard_map/project/pallas_call | solution.py:269
  37.8 0.5 collective-permute-start.13
  38.4 0.9 %collective-permute-done.12.refs_0_ = bf16[64,1792]{1,0:T(8,128)(2,1)S(1)} collective-permute-done((bf16[64,1792]{1,0:T(8,128)(2,1)S(1)}, bf16[64,1792]{1,0:T(8,128)(2,1)S(1)}, u32[]{:S(2)}, u32[]{:S(2)}) %collective-permute-start.12) | collective-permute-done | bytes 229408 | tf_op jit(solution)/shard_map/ppermute | solution.py:22
  39.9 12.2 %collective-permute-done.16.refs_4_ = bf16[64,2304]{1,0:T(8,128)(2,1)S(1)} collective-permute-done((bf16[64,2304]{1,0:T(8,128)(2,1)S(1)}, bf16[64,2304]{1,0:T(8,128)(2,1)S(1)}, u32[]{:S(2)}, u32[]{:S(2)}) %collective-permute-start.16) | collective-permute-done | bytes 294944 | tf_op jit(solution)/shard_map/ppermute | solution.py:22
  52.1 1.1 %combine.1 = bf16[64,5376]{1,0:T(8,128)(2,1)} custom-call(f32[64,5376]{1,0:T(8,128)S(1)} %get-tuple-element.59.mine, bf16[64,1792]{1,0:T(8,128)(2,1)S(1)} %collective-permute-done.12.refs_0_, bf16[64,1792]{1,0:T(8,128)(2,1)S(1)} %collective-permute-done.13.refs_1_, bf16[64,1792]{1,0:T(8,128)(2,1)S(1)} %collective-permute-done.14.refs_2_, ...), custom_call_target="tpu_custom_call" | custom-call | tf_op jit(solution)/shard_map/combine/pallas_call | solution.py:317
  (12 shorter events, 1.5 us)
Async XLA Ops:
  0.0 6.6 %collective-permute-start = (bf16[256,256]{1,0:T(8,128)(2,1)}, bf16[256,256]{1,0:T(8,128)(2,1)S(1)}, u32[]{:S(2)}, u32[]{:S(2)}) collective-permute-start(bf16[256,256]{1,0:T(8,128)(2,1)} %keys_in.1), channel_id=1, source_target_pairs={{0,4},{4,0},{8,12},{12,8},{16,20},{20,16},{24,28},{28,24},{1,5},{5... | collective-permute-start | bytes 393224 | tf_op jit(solution)/shard_map/ppermute | solution.py:22
  0.5 8.9 %collective-permute-start.1 = (bf16[256,256]{1,0:T(8,128)(2,1)}, bf16[256,256]{1,0:T(8,128)(2,1)S(1)}, u32[]{:S(2)}, u32[]{:S(2)}) collective-permute-start(bf16[256,256]{1,0:T(8,128)(2,1)} %values_in.1), channel_id=1, source_target_pairs={{0,4},{4,0},{8,12},{12,8},{16,20},{20,16},{24,28},{28,24},{1,5},{5... | collective-permute-start | bytes 393224 | tf_op jit(solution)/shard_map/ppermute | solution.py:22
  2.0 10.8 %collective-permute-start.2 = (bf16[256,256]{1,0:T(8,128)(2,1)}, bf16[256,256]{1,0:T(8,128)(2,1)S(1)}, u32[]{:S(2)}, u32[]{:S(2)}) collective-permute-start(bf16[256,256]{1,0:T(8,128)(2,1)} %keys_in.1), channel_id=1, source_target_pairs={{0,8},{8,16},{16,0},{4,12},{12,20},{20,4},{24,28},{28,24},{1,9},{9... | collective-permute-start | bytes 393224 | tf_op jit(solution)/shard_map/ppermute | solution.py:22
  2.5 12.5 %collective-permute-start.3 = (bf16[256,256]{1,0:T(8,128)(2,1)}, bf16[256,256]{1,0:T(8,128)(2,1)S(1)}, u32[]{:S(2)}, u32[]{:S(2)}) collective-permute-start(bf16[256,256]{1,0:T(8,128)(2,1)} %values_in.1), channel_id=1, source_target_pairs={{0,8},{8,16},{16,0},{4,12},{12,20},{20,4},{24,28},{28,24},{1,9},{9... | collective-permute-start | bytes 393224 | tf_op jit(solution)/shard_map/ppermute | solution.py:22
  4.1 14.4 %collective-permute-start.4 = (bf16[256,256]{1,0:T(8,128)(2,1)}, bf16[256,256]{1,0:T(8,128)(2,1)S(1)}, u32[]{:S(2)}, u32[]{:S(2)}) collective-permute-start(bf16[256,256]{1,0:T(8,128)(2,1)} %keys_in.1), channel_id=1, source_target_pairs={{0,16},{16,8},{8,0},{4,20},{20,12},{12,4},{24,28},{28,24},{1,17},{... | collective-permute-start | bytes 393224 | tf_op jit(solution)/shard_map/ppermute | solution.py:22
  6.6 14.0 %collective-permute-start.5 = (bf16[256,256]{1,0:T(8,128)(2,1)}, bf16[256,256]{1,0:T(8,128)(2,1)S(1)}, u32[]{:S(2)}, u32[]{:S(2)}) collective-permute-start(bf16[256,256]{1,0:T(8,128)(2,1)} %values_in.1), channel_id=1, source_target_pairs={{0,16},{16,8},{8,0},{4,20},{20,12},{12,4},{24,28},{28,24},{1,17},{... | collective-permute-start | bytes 393224 | tf_op jit(solution)/shard_map/ppermute | solution.py:22
  15.0 8.4 %collective-permute-start.6 = (bf16[256,256]{1,0:T(8,128)(2,1)S(1)}, bf16[256,256]{1,0:T(8,128)(2,1)S(1)}, u32[]{:S(2)}, u32[]{:S(2)}) collective-permute-start(bf16[256,256]{1,0:T(8,128)(2,1)S(1)} %collective-permute-done.2.refs_3_), channel_id=1, source_target_pairs={{0,4},{4,0},{8,12},{12,8},{16,20},{20,16},{24,28},{28,24},{1,5},{5... | collective-permute-start | bytes 393224 | tf_op jit(solution)/shard_map/ppermute | solution.py:22
  15.5 10.7 %collective-permute-start.7 = (bf16[256,256]{1,0:T(8,128)(2,1)S(1)}, bf16[256,256]{1,0:T(8,128)(2,1)S(1)}, u32[]{:S(2)}, u32[]{:S(2)}) collective-permute-start(bf16[256,256]{1,0:T(8,128)(2,1)S(1)} %collective-permute-done.3.refs_4_), channel_id=1, source_target_pairs={{0,4},{4,0},{8,12},{12,8},{16,20},{20,16},{24,28},{28,24},{1,5},{5... | collective-permute-start | bytes 393224 | tf_op jit(solution)/shard_map/ppermute | solution.py:22
  20.6 8.4 %collective-permute-start.8 = (bf16[256,256]{1,0:T(8,128)(2,1)S(1)}, bf16[256,256]{1,0:T(8,128)(2,1)S(1)}, u32[]{:S(2)}, u32[]{:S(2)}) collective-permute-start(bf16[256,256]{1,0:T(8,128)(2,1)S(1)} %collective-permute-done.4.refs_3_), channel_id=1, source_target_pairs={{0,4},{4,0},{8,12},{12,8},{16,20},{20,16},{24,28},{28,24},{1,5},{5... | collective-permute-start | bytes 393224 | tf_op jit(solution)/shard_map/ppermute | solution.py:22
  21.1 9.6 %collective-permute-start.9 = (bf16[256,256]{1,0:T(8,128)(2,1)S(1)}, bf16[256,256]{1,0:T(8,128)(2,1)S(1)}, u32[]{:S(2)}, u32[]{:S(2)}) collective-permute-start(bf16[256,256]{1,0:T(8,128)(2,1)S(1)} %collective-permute-done.5.refs_4_), channel_id=1, source_target_pairs={{0,4},{4,0},{8,12},{12,8},{16,20},{20,16},{24,28},{28,24},{1,5},{5... | collective-permute-start | bytes 393224 | tf_op jit(solution)/shard_map/ppermute | solution.py:22
  32.7 1.8 %collective-permute-start.10 = (bf16[64,3072]{1,0:T(8,128)(2,1)S(1)}, bf16[64,3072]{1,0:T(8,128)(2,1)S(1)}, u32[]{:S(2)}, u32[]{:S(2)}) collective-permute-start(bf16[64,3072]{1,0:T(8,128)(2,1)S(1)} %get-tuple-element.55), channel_id=1, source_target_pairs={{0,1},{1,0},{2,3},{3,2},{4,5},{5,4},{6,7},{7,6},{8,9},{9,8},{10,11... | collective-permute-start | bytes 1179656 | tf_op jit(solution)/shard_map/ppermute | solution.py:22
  33.3 1.9 %collective-permute-start.11 = (bf16[64,2304]{1,0:T(8,128)(2,1)S(1)}, bf16[64,2304]{1,0:T(8,128)(2,1)S(1)}, u32[]{:S(2)}, u32[]{:S(2)}) collective-permute-start(bf16[64,2304]{1,0:T(8,128)(2,1)S(1)} %get-tuple-element.57), channel_id=1, source_target_pairs={{0,1},{1,0},{2,3},{3,2},{4,5},{5,4},{6,7},{7,6},{8,9},{9,8},{10,11... | collective-permute-start | bytes 884744 | tf_op jit(solution)/shard_map/ppermute | solution.py:22
  34.6 17.5 %collective-permute-start.15 = (bf16[64,3072]{1,0:T(8,128)(2,1)S(1)}, bf16[64,3072]{1,0:T(8,128)(2,1)S(1)}, u32[]{:S(2)}, u32[]{:S(2)}) collective-permute-start(bf16[64,3072]{1,0:T(8,128)(2,1)S(1)} %add_up.2), channel_id=1, source_target_pairs={{0,2},{1,3},{2,0},{3,1},{4,6},{5,7},{6,4},{7,5},{8,10},{9,11},{10,... | collective-permute-start | bytes 1179656 | tf_op jit(solution)/shard_map/ppermute | solution.py:22
  35.3 16.9 %collective-permute-start.16 = (bf16[64,2304]{1,0:T(8,128)(2,1)S(1)}, bf16[64,2304]{1,0:T(8,128)(2,1)S(1)}, u32[]{:S(2)}, u32[]{:S(2)}) collective-permute-start(bf16[64,2304]{1,0:T(8,128)(2,1)S(1)} %add_up.3), channel_id=1, source_target_pairs={{0,2},{1,3},{2,0},{3,1},{4,6},{5,7},{6,4},{7,5},{8,10},{9,11},{10,... | collective-permute-start | bytes 884744 | tf_op jit(solution)/shard_map/ppermute | solution.py:22
  37.7 1.6 %collective-permute-start.12 = (bf16[64,1792]{1,0:T(8,128)(2,1)S(1)}, bf16[64,1792]{1,0:T(8,128)(2,1)S(1)}, u32[]{:S(2)}, u32[]{:S(2)}) collective-permute-start(bf16[64,1792]{1,0:T(8,128)(2,1)S(1)} %get-tuple-element.60), channel_id=1, source_target_pairs={{0,1},{1,0},{2,3},{3,2},{4,5},{5,4},{6,7},{7,6},{8,9},{9,8},{10,11... | collective-permute-start | bytes 688136 | tf_op jit(solution)/shard_map/ppermute | solution.py:22
  37.8 1.8 %collective-permute-start.13 = (bf16[64,1792]{1,0:T(8,128)(2,1)S(1)}, bf16[64,1792]{1,0:T(8,128)(2,1)S(1)}, u32[]{:S(2)}, u32[]{:S(2)}) collective-permute-start(bf16[64,1792]{1,0:T(8,128)(2,1)S(1)} %get-tuple-element.61), channel_id=1, source_target_pairs={{0,1},{1,0},{2,3},{3,2},{4,5},{5,4},{6,7},{7,6},{8,9},{9,8},{10,11... | collective-permute-start | bytes 688136 | tf_op jit(solution)/shard_map/ppermute | solution.py:22
  38.3 1.6 %collective-permute-start.14 = (bf16[64,1792]{1,0:T(8,128)(2,1)S(1)}, bf16[64,1792]{1,0:T(8,128)(2,1)S(1)}, u32[]{:S(2)}, u32[]{:S(2)}) collective-permute-start(bf16[64,1792]{1,0:T(8,128)(2,1)S(1)} %get-tuple-element.62), channel_id=1, source_target_pairs={{0,1},{1,0},{2,3},{3,2},{4,5},{5,4},{6,7},{7,6},{8,9},{9,8},{10,11... | collective-permute-start | bytes 688136 | tf_op jit(solution)/shard_map/ppermute | solution.py:22
where the time goes:
time: 53.3 us; the launch traced here: 53.2 us
  waiting for transfers between devices  28.5 us (53%)
  starting transfers between devices  12.6 us (24%)
  Pallas kernels  11.3 us (21%)
  local copies, waits for them, and re-layouts  0.74 us (1%)
    ppermute x17, waiting for transfers between devices, hop(): return lax.ppermute(block, axis, pairs)  28.5 us
    ppermute x17, starting transfers between devices, hop(): return lax.ppermute(block, axis, pairs)  12.6 us
    pallas_call x1, Pallas kernels, attend_first(): pl.pallas_call(functools.partial(first_kernel, numbers), out_shape=state_...  3.37 us
    pallas_call x2, Pallas kernels, attend_next(): pl.pallas_call(functools.partial(next_kernel, numbers), out_shape=state_s...  3.36 us
    pallas_call x1, Pallas kernels, attend_last(): pl.pallas_call(functools.partial(last_kernel, numbers, columns), out_shap...  1.99 us
    pallas_call x2, Pallas kernels, project(): pl.pallas_call(functools.partial(project_kernel, columns), out_shape=proj...  1.36 us
  transfers between devices with their start and end apart: 17, of which 13 were waited for; matrix products, arithmetic and copies ran while one was open for 1% of the time, Pallas kernels for 15%

commit v1 on v0

--- a/solution.py
+++ b/solution.py
@@ -41,12 +41,12 @@
 
 CHUNKS = 6
 BESIDE = ((0, 1), (2, 3), (4, 5), (6, 7))
-BY_TWO = ((0, 2, 4), (1, 3, 5), (6, 7))
-BY_FOUR = ((0, 4, 2), (1, 5, 3), (6, 7))
-
-
-def after(x, state):
-    return lax.optimization_barrier((x, state[0]))[0]
+BY_TWO = ((0, 2, 4, 6), (1, 3, 5, 7))
+BY_FOUR = ((0, 4, 6, 2), (1, 5, 7, 3))
+
+
+def after(x, event):
+    return lax.optimization_barrier((x, event))[0]
 
 
 def cycles(rings):
@@ -140,23 +140,32 @@
     return list(zip(refs[0::2], refs[1::2]))
 
 
-def first_kernel(numbers, info, queries_in, keys_in, values_in, weight_in, *refs):
-    pairs = 2 * len(numbers) - 2
-    *state, queries, weight, keys, values, sems = refs[pairs:]
-    chunks = [(keys, values)] + pairs_of(refs[:pairs])
-    places = ((queries_in, queries), (keys_in, keys), (values_in, values), (weight_in, weight))
+def first_kernel(numbers, cut, info, queries_in, keys_in, values_in, weight_in, *refs):
+    *state, queries, weight, keys, values, sems = refs
+    places = (
+        (queries_in, queries),
+        (keys_in, keys),
+        (values_in, values),
+        (weight_in.at[:, :cut], weight),
+    )
     fetches = [pltpu.make_async_copy(a, b, sems.at[i]) for i, (a, b) in enumerate(places)]
     for fetch in fetches:
         fetch.start()
     for fetch in fetches[:3]:
         fetch.wait()
-    absorb(numbers, info, queries, chunks, None, store_state(state))
+    absorb(numbers, info, queries, [(keys, values)], None, store_state(state))
     fetches[3].wait()
 
 
-def next_kernel(numbers, info, queries, *refs):
+def next_kernel(numbers, cut, info, queries, *refs):
+    if cut is not None:
+        weight_in, *refs, weight, sem = refs
+        fetch = pltpu.make_async_copy(weight_in.at[:, cut:], weight, sem)
+        fetch.start()
     pairs = 2 * len(numbers)
     absorb(numbers, info, queries, pairs_of(refs[3 : 3 + pairs]), refs[:3], store_state(refs[3 + pairs :]))
+    if cut is not None:
+        fetch.wait()
 
 
 def attend_cost(queries, numbers, fetched=0):
@@ -174,12 +183,12 @@
     return (pltpu.VMEM((rows, HEAD_SIZE), jnp.float32),) * 3
 
 
-def attend_first(info, queries, keys, values, weight, chunks, numbers):
-    return pl.pallas_call(
-        functools.partial(first_kernel, numbers),
-        out_shape=state_shapes(queries)
-        + (pltpu.VMEM(queries.shape, queries.dtype), pltpu.VMEM(weight.shape, weight.dtype)),
-        in_specs=[SMEM, HBM, HBM, HBM, HBM] + [VMEM] * (2 * len(chunks)),
+def attend_first(info, queries, keys, values, weight, cut):
+    part = pltpu.VMEM((weight.shape[0], cut), weight.dtype)
+    return pl.pallas_call(
+        functools.partial(first_kernel, (0,), cut),
+        out_shape=state_shapes(queries) + (pltpu.VMEM(queries.shape, queries.dtype), part),
+        in_specs=[SMEM, HBM, HBM, HBM, HBM],
         out_specs=(VMEM,) * 5,
         scratch_shapes=[
             pltpu.VMEM(keys.shape, keys.dtype),
@@ -187,28 +196,30 @@
             pltpu.SemaphoreType.DMA((4,)),
         ],
         compiler_params=LIMIT,
-        cost_estimate=attend_cost(queries, numbers, 2 * weight.size),
+        cost_estimate=attend_cost(queries, (0,), 2 * weight.size),
         name="attend_first",
-    )(
-        info,
-        *[pltpu.with_memory_space_constraint(x, pltpu.HBM) for x in (queries, keys, values, weight)],
-        *[x for pair in chunks for x in pair],
-    )
-
-
-def attend_next(info, queries, state, chunks, numbers):
-    return pl.pallas_call(
-        functools.partial(next_kernel, numbers),
-        out_shape=state_shapes(queries),
-        in_specs=[SMEM] + [VMEM] * (4 + 2 * len(chunks)),
-        out_specs=(VMEM,) * 3,
+    )(info, *[pltpu.with_memory_space_constraint(x, pltpu.HBM) for x in (queries, keys, values, weight)])
+
+
+def attend_next(info, queries, state, chunks, numbers, weight=None, cut=None):
+    fetched, shapes, scratch = [], state_shapes(queries), []
+    if cut is not None:
+        fetched = [pltpu.with_memory_space_constraint(weight, pltpu.HBM)]
+        shapes += (pltpu.VMEM((weight.shape[0], weight.shape[1] - cut), weight.dtype),)
+        scratch = [pltpu.SemaphoreType.DMA]
+    return pl.pallas_call(
+        functools.partial(next_kernel, numbers, cut),
+        out_shape=shapes,
+        in_specs=[SMEM, VMEM] + [HBM] * len(fetched) + [VMEM] * (3 + 2 * len(chunks)),
+        out_specs=(VMEM,) * len(shapes),
+        scratch_shapes=scratch,
         compiler_params=LIMIT,
         cost_estimate=attend_cost(queries, numbers),
         name="attend_next",
-    )(info, queries, *state, *[x for pair in chunks for x in pair])
-
-
-def last_kernel(numbers, columns, info, queries, weight, *refs):
+    )(info, queries, *fetched, *state, *[x for pair in chunks for x in pair])
+
+
+def last_kernel(numbers, info, queries, weight, *refs):
     pairs = 2 * len(numbers)
     chunks = pairs_of(refs[3 : 3 + pairs])
     far, near, mine, send, attended = refs[3 + pairs :]
@@ -225,15 +236,15 @@
         for i, owner in enumerate(owners):
             source = pl.ds(pl.multiple_of(owner * share, share), share)
             half[i * share : (i + 1) * share, :] = attended[source, :]
-    project_columns(far, weight, mine, (send,), *columns)
-
-
-def attend_last(info, queries, weight, state, chunks, numbers, columns):
+    project_columns(far, [weight], mine, (send,))
+
+
+def attend_last(info, queries, weight, state, chunks, numbers):
     n_query, width = queries.shape
     half = jax.ShapeDtypeStruct((n_query // 2, width), jnp.bfloat16)
     return pl.pallas_call(
-        functools.partial(last_kernel, numbers, columns),
-        out_shape=(half, half) + project_shapes(n_query // 4, columns[1] - columns[0]),
+        functools.partial(last_kernel, numbers),
+        out_shape=(half, half) + project_shapes(n_query // 4, weight.shape[1]),
         in_specs=[SMEM] + [VMEM] * (5 + 2 * len(numbers)),
         out_specs=(VMEM,) * 4,
         scratch_shapes=[pltpu.VMEM(queries.shape, jnp.bfloat16)],
@@ -248,35 +259,39 @@
     return (jax.ShapeDtypeStruct((rows, count), jnp.float32),) + (send,) * sends
 
 
-def project_columns(rows, weight, mine, sends, start, end):
+def project_columns(rows, weights, mine, sends):
     share = rows.shape[0] // 2
     width = sends[0].shape[1]
-    for at in range(start, end, width):
-        for left in range(at, at + width, 768):
-            right = min(left + 768, at + width)
-            product = jnp.dot(rows[...], weight[:, left:right], preferred_element_type=jnp.float32)
-            mine[:, left - start : right - start] = product[:share]
-            send = sends[(at - start) // width]
-            send[:, left - at : right - at] = product[share:].astype(send.dtype)
-
-
-def project_kernel(columns, rows, weight, mine, *sends):
-    project_columns(rows, weight, mine, sends, *columns)
-
-
-def project(rows, weight, columns, sends=1):
-    count = columns[1] - columns[0]
-    return pl.pallas_call(
-        functools.partial(project_kernel, columns),
-        out_shape=project_shapes(rows.shape[0] // 2, count, sends),
-        in_specs=[VMEM, VMEM],
+    ends = [0]
+    for weight in weights:
+        ends.append(ends[-1] + weight.shape[1])
+    stops = sorted(set(ends) | {i * width for i in range(len(sends) + 1)} | set(range(0, ends[-1], 768)))
+    for left, right in zip(stops[:-1], stops[1:]):
+        i = max(i for i in range(len(weights)) if ends[i] <= left)
+        columns = weights[i][:, left - ends[i] : right - ends[i]]
+        product = jnp.dot(rows[...], columns, preferred_element_type=jnp.float32)
+        mine[:, left:right] = product[:share]
+        send, at = sends[left // width], left // width * width
+        send[:, left - at : right - at] = product[share:].astype(send.dtype)
+
+
+def project_kernel(count, rows, *refs):
+    project_columns(rows, refs[:count], refs[count], refs[count + 1 :])
+
+
+def project(rows, weights, sends=1):
+    columns = sum(weight.shape[1] for weight in weights)
+    return pl.pallas_call(
+        functools.partial(project_kernel, len(weights)),
+        out_shape=project_shapes(rows.shape[0] // 2, columns, sends),
+        in_specs=[VMEM] * (1 + len(weights)),
         out_specs=(VMEM,) * (1 + sends),
         compiler_params=LIMIT,
         cost_estimate=pl.CostEstimate(
-            flops=2 * rows.shape[0] * rows.shape[1] * count, bytes_accessed=0, transcendentals=0
+            flops=2 * rows.shape[0] * rows.shape[1] * columns, bytes_accessed=0, transcendentals=0
         ),
         name="project",
-    )(rows, weight)
+    )(rows, *weights)
 
 
 def add_kernel(mine, theirs, out):
@@ -414,27 +429,29 @@
     cut = columns * 4 // 7 // BLOCK * BLOCK
 
     if n_ctx == 8:
+        info = describe(position, place, doc_ids, n_ctx)
         by_two = [hop(x, "ctx", cycles(BY_TWO)) for x in (keys, values)]
-        by_four = [hop(x, "ctx", cycles(BY_FOUR)) for x in (keys, values)]
         beside = [hop(x, "ctx", cycles(BESIDE)) for x in (keys, values)]
-        info = describe(position, place, doc_ids, n_ctx)
-        *state, fetched, weight = attend_first(
-            info, queries, keys, values, out_weight, [beside], (0, 1)
+        *state, fetched, weight_a = attend_first(info, queries, keys, values, out_weight, cut)
+        later = [after(keys, state[0]), after(values, by_two[1])]
+        by_four = [hop(x, "ctx", cycles(BY_FOUR)) for x in later]
+        swap_two = [hop(x, "ctx", cycles(BESIDE)) for x in by_two]
+        *state, weight_b = attend_next(
+            info, fetched, state, [beside, by_two], (1, 2), out_weight, cut
         )
-        by_two = [after(x, state) for x in by_two]
-        swap_two = [hop(x, "ctx", cycles(BESIDE)) for x in by_two]
-        state = attend_next(info, fetched, state, [by_two], (2,))
-        by_four = [after(x, state) for x in by_four]
-        swap_four = [hop(x, "ctx", cycles(BESIDE)) for x in by_four]
+        swap_four = [
+            hop(after(by_four[0], state[0]), "ctx", cycles(BESIDE)),
+            hop(after(beside[1], by_two[1]), "ctx", cycles(BY_FOUR)),
+        ]
         state = attend_next(info, fetched, state, [by_four, swap_two], (3, 4))
-        far, near, mine, send = attend_last(info, fetched, weight, state, [swap_four], (5,), (0, cut))
+        far, near, mine, send = attend_last(info, fetched, weight_a, state, [swap_four], (5,))
     else:
-        weight = out_weight
+        weight_a, weight_b = out_weight[:, :cut], out_weight[:, cut:]
         attended = ring_attention(queries, keys, values, doc_ids, n_ctx, position)
         far, near = part_rows(attended, place)
-        mine, send = project(far, weight, (0, cut))
+        mine, send = project(far, [weight_a])
     theirs = hop(send, "head", other_core)
-    later_mine, later_send = project(far, weight, (cut, columns))
+    later_mine, later_send = project(far, [weight_b])
     mine, later_mine = lax.optimization_barrier((mine, later_mine))
     first_sum = add_up(mine, theirs)
     first_part = hop(first_sum, "head", other_chip)
@@ -443,7 +460,7 @@
     later_sum = add_up(later_mine, later_theirs)
     second_part = hop(later_sum, "head", other_chip)
     near, later_sum = lax.optimization_barrier((near, later_sum))
-    mine, *sends = project(near, weight, (0, columns), 3)
+    mine, *sends = project(near, [weight_a, weight_b], 3)
     theirs = [hop(send, "head", other_core) for send in sends]
     return combine(mine, theirs, (first_part, second_part))
 

time: 53.3 us -> 47.2 us (0.89)
  the two profiles are of different devices: /device:TPU:30 before, /device:TPU:0 now
where the time goes in v1:
time: 47.2 us; the launch traced here: 47 us
  starting transfers between devices  18.2 us (39%)
  waiting for transfers between devices  15.7 us (33%)
  Pallas kernels  12.3 us (26%)
  local copies, waits for them, and re-layouts  0.74 us (2%)
    ppermute x17, starting transfers between devices, hop(): return lax.ppermute(block, axis, pairs)  18.2 us
    ppermute x17, waiting for transfers between devices, hop(): return lax.ppermute(block, axis, pairs)  15.7 us
    pallas_call x2, Pallas kernels, attend_next(): pl.pallas_call(functools.partial(next_kernel, numbers, cut), out_shape=sh...  4.96 us
    pallas_call x1, Pallas kernels, attend_first(): pl.pallas_call(functools.partial(first_kernel, (0,), cut), out_shape=stat...  2.7 us
    pallas_call x1, Pallas kernels, attend_last(): pl.pallas_call(functools.partial(last_kernel, numbers), out_shape=(half,...  2.02 us
    pallas_call x2, Pallas kernels, project(): pl.pallas_call(functools.partial(project_kernel, len(weights)), out_shape...  1.41 us
    pallas_call x1, Pallas kernels, combine(): pl.pallas_call(functools.partial(combine_kernel, (len(beside), len(across...  1.05 us
  transfers between devices with their start and end apart: 17, of which 6 were waited for; matrix products, arithmetic and copies ran while one was open for 2% of the time, Pallas kernels for 20%

profile of v1, /device:TPU:0, one launch (start us, length us, event | category | flops | bytes accessed | tf_op | source)
XLA Modules:
  0.0 47.0 jit_solution(6473826401564162380)
XLA Ops:
  0.0 3.0 %collective-permute-start.3 = (bf16[256,256]{1,0:T(8,128)(2,1)}, bf16[256,256]{1,0:T(8,128)(2,1)S(1)}, u32[]{:S(2)}, u32[]{:S(2)}) collective-permute-start(bf16[256,256]{1,0:T(8,128)(2,1)} %values_in.1), channel_id=1, source_target_pairs={{0,8},{8,16},{16,24},{24,0},{4,12},{12,20},{20,28},{28,4},{1,9},{9... | collective-permute-start | bytes 393224 | tf_op jit(solution)/shard_map/ppermute | solution.py:22
  3.0 1.5 %collective-permute-start = (bf16[256,256]{1,0:T(8,128)(2,1)}, bf16[256,256]{1,0:T(8,128)(2,1)S(1)}, u32[]{:S(2)}, u32[]{:S(2)}) collective-permute-start(bf16[256,256]{1,0:T(8,128)(2,1)} %keys_in.1), channel_id=1, source_target_pairs={{0,4},{4,0},{8,12},{12,8},{16,20},{20,16},{24,28},{28,24},{1,5},{5... | collective-permute-start | bytes 393224 | tf_op jit(solution)/shard_map/ppermute | solution.py:22
  4.5 1.6 %collective-permute-start.2 = (bf16[256,256]{1,0:T(8,128)(2,1)}, bf16[256,256]{1,0:T(8,128)(2,1)S(1)}, u32[]{:S(2)}, u32[]{:S(2)}) collective-permute-start(bf16[256,256]{1,0:T(8,128)(2,1)} %keys_in.1), channel_id=1, source_target_pairs={{0,8},{8,16},{16,24},{24,0},{4,12},{12,20},{20,28},{28,4},{1,9},{9... | collective-permute-start | bytes 393224 | tf_op jit(solution)/shard_map/ppermute | solution.py:22
  6.1 0.5 %collective-permute-start.1 = (bf16[256,256]{1,0:T(8,128)(2,1)}, bf16[256,256]{1,0:T(8,128)(2,1)S(1)}, u32[]{:S(2)}, u32[]{:S(2)}) collective-permute-start(bf16[256,256]{1,0:T(8,128)(2,1)} %values_in.1), channel_id=1, source_target_pairs={{0,4},{4,0},{8,12},{12,8},{16,20},{20,16},{24,28},{28,24},{1,5},{5... | collective-permute-start | bytes 393224 | tf_op jit(solution)/shard_map/ppermute | solution.py:22
  6.6 0.7 %concatenate.3.info = s32[30]{0:T(128)S(1)} concatenate(s32[1]{0:T(128)} %bitcast, s32[1]{0:T(128)} %bitcast.1, s32[1]{0:T(128)} %bitcast.2, s32[1]{0:T(128)} %bitcast.3, s32[1]{0:T(128)} %bitcast.4, s32[1]{0:T(128)} %bitcast.5, s32[1]{0:T(128)} %bitcast.6, s32[1]{0:T(128)} %bitcast.7, s32[1]{0:T(128)} %bitcast.8, s32[1]{0:T(128)} %bitcast.9, s32[1]{0:T(128)} %bitcast.10, ...), dimensions={0} | concatenate | bytes 240 | tf_op jit(solution)/shard_map/concatenate | solution.py:39
  7.4 2.7 %attend_first.1 = (f32[1024,128]{1,0:T(8,128)S(1)}, f32[1024,128]{1,0:T(8,128)S(1)}, f32[1024,128]{1,0:T(8,128)S(1)}, bf16[256,512]{1,0:T(8,128)(2,1)S(1)}, bf16[512,3072]{1,0:T(8,128)(2,1)S(1)}) custom-call(s32[30]{0:T(128)S(1)} %concatenate.3.info, bf16[256,512]{1,0:T(8,128)(2,1)} %queries_in.1, bf16[256,256]{1,0:T(8,128)(2,1)} %keys_in.1, ...), custom_call_target="tpu_custom_call" | custom-call | flops 134217728 | bytes 5505024 | tf_op jit(solution)/shard_map/attend_first/pallas_call | solution.py:188
  10.1 1.1 %collective-permute-start.4 = (bf16[256,256]{1,0:T(8,128)(2,1)S(1)}, bf16[256,256]{1,0:T(8,128)(2,1)S(1)}, u32[]{:S(2)}, u32[]{:S(2)}) collective-permute-start(bf16[256,256]{1,0:T(8,128)(2,1)S(1)} %copy-done), channel_id=1, source_target_pairs={{0,16},{16,24},{24,8},{8,0},{4,20},{20,28},{28,12},{12,4},{1,17},{... | collective-permute-start | bytes 393224 | tf_op jit(solution)/shard_map/ppermute | solution.py:22
  11.2 1.7 %collective-permute-start.5 = (bf16[256,256]{1,0:T(8,128)(2,1)S(1)}, bf16[256,256]{1,0:T(8,128)(2,1)S(1)}, u32[]{:S(2)}, u32[]{:S(2)}) collective-permute-start(bf16[256,256]{1,0:T(8,128)(2,1)S(1)} %copy-done.1), channel_id=1, source_target_pairs={{0,16},{16,24},{24,8},{8,0},{4,20},{20,28},{28,12},{12,4},{1,17},{... | collective-permute-start | bytes 393224 | tf_op jit(solution)/shard_map/ppermute | solution.py:22
  13.0 1.5 %collective-permute-start.7 = (bf16[256,256]{1,0:T(8,128)(2,1)S(1)}, bf16[256,256]{1,0:T(8,128)(2,1)S(1)}, u32[]{:S(2)}, u32[]{:S(2)}) collective-permute-start(bf16[256,256]{1,0:T(8,128)(2,1)S(1)} %collective-permute-done.3.refs_7_), channel_id=1, source_target_pairs={{0,4},{4,0},{8,12},{12,8},{16,20},{20,16},{24,28},{28,24},{1,5},{5... | collective-permute-start | bytes 393224 | tf_op jit(solution)/shard_map/ppermute | solution.py:22
  14.5 0.5 %collective-permute-start.6 = (bf16[256,256]{1,0:T(8,128)(2,1)S(1)}, bf16[256,256]{1,0:T(8,128)(2,1)S(1)}, u32[]{:S(2)}, u32[]{:S(2)}) collective-permute-start(bf16[256,256]{1,0:T(8,128)(2,1)S(1)} %collective-permute-done.2.refs_6_), channel_id=1, source_target_pairs={{0,4},{4,0},{8,12},{12,8},{16,20},{20,16},{24,28},{28,24},{1,5},{5... | collective-permute-start | bytes 393224 | tf_op jit(solution)/shard_map/ppermute | solution.py:22
  15.0 3.0 %attend_next.2 = (f32[1024,128]{1,0:T(8,128)S(1)}, f32[1024,128]{1,0:T(8,128)S(1)}, f32[1024,128]{1,0:T(8,128)S(1)}, bf16[512,2304]{1,0:T(8,128)(2,1)S(1)}) custom-call(s32[30]{0:T(128)S(1)} %concatenate.3.info, bf16[256,512]{1,0:T(8,128)(2,1)S(1)} %get-tuple-element.35.queries, bf16[512,5376]{1,0:T(8,128)(2,1)} %refs_0_.1, ...), custom_call_target="tpu_custom_call" | custom-call | flops 268435456 | tf_op jit(solution)/shard_map/attend_next/pallas_call | solution.py:210
  18.0 1.6 %collective-permute-start.8 = (bf16[256,256]{1,0:T(8,128)(2,1)S(1)}, bf16[256,256]{1,0:T(8,128)(2,1)S(1)}, u32[]{:S(2)}, u32[]{:S(2)}) collective-permute-start(bf16[256,256]{1,0:T(8,128)(2,1)S(1)} %collective-permute-done.4.refs_3_), channel_id=1, source_target_pairs={{0,4},{4,0},{8,12},{12,8},{16,20},{20,16},{24,28},{28,24},{1,5},{5... | collective-permute-start | bytes 393224 | tf_op jit(solution)/shard_map/ppermute | solution.py:22
  19.6 1.7 %collective-permute-start.9 = (bf16[256,256]{1,0:T(8,128)(2,1)S(1)}, bf16[256,256]{1,0:T(8,128)(2,1)S(1)}, u32[]{:S(2)}, u32[]{:S(2)}) collective-permute-start(bf16[256,256]{1,0:T(8,128)(2,1)S(1)} %collective-permute-done.1.refs_5_), channel_id=1, source_target_pairs={{0,16},{16,24},{24,8},{8,0},{4,20},{20,28},{28,12},{12,4},{1,17},{... | collective-permute-start | bytes 393224 | tf_op jit(solution)/shard_map/ppermute | solution.py:22
  21.3 2.0 %attend_next.3 = (f32[1024,128]{1,0:T(8,128)S(1)}, f32[1024,128]{1,0:T(8,128)S(1)}, f32[1024,128]{1,0:T(8,128)S(1)}) custom-call(s32[30]{0:T(128)S(1)} %concatenate.3.info, bf16[256,512]{1,0:T(8,128)(2,1)S(1)} %get-tuple-element.35.queries, f32[1024,128]{1,0:T(8,128)S(1)} %get-tuple-element.40.refs_0_, f32[1024,128]{1,0:T(8,128)S(1)} %get-tuple-element.41.refs_1_, ...), custom_call_target="tpu_custom_call" | custom-call | flops 268435456 | tf_op jit(solution)/shard_map/attend_next/pallas_call | solution.py:210
  23.3 1.3 %collective-permute-done.9.refs_4_ = bf16[256,256]{1,0:T(8,128)(2,1)S(1)} collective-permute-done((bf16[256,256]{1,0:T(8,128)(2,1)S(1)}, bf16[256,256]{1,0:T(8,128)(2,1)S(1)}, u32[]{:S(2)}, u32[]{:S(2)}) %collective-permute-start.9) | collective-permute-done | bytes 131104 | tf_op jit(solution)/shard_map/ppermute | solution.py:22
  24.6 2.0 %attend_last.1 = (bf16[128,512]{1,0:T(8,128)(2,1)S(1)}, bf16[128,512]{1,0:T(8,128)(2,1)S(1)}, f32[64,3072]{1,0:T(8,128)S(1)}, bf16[64,3072]{1,0:T(8,128)(2,1)S(1)}) custom-call(s32[30]{0:T(128)S(1)} %concatenate.3.info, bf16[256,512]{1,0:T(8,128)(2,1)S(1)} %get-tuple-element.35.queries, bf16[512,3072]{1,0:T(8,128)(2,1)S(1)} %get-tuple-element.36.weight.refs_0_, ...), custom_call_target="tpu_custom_call" | custom-call | flops 134217728 | tf_op jit(solution)/shard_map/attend_last/pallas_call | solution.py:245
  26.6 0.1 collective-permute-start.10
  26.7 0.5 %project.2 = (f32[64,2304]{1,0:T(8,128)S(1)}, bf16[64,2304]{1,0:T(8,128)(2,1)S(1)}) custom-call(bf16[128,512]{1,0:T(8,128)(2,1)S(1)} %get-tuple-element.52.rows, bf16[512,2304]{1,0:T(8,128)(2,1)S(1)} %get-tuple-element.53.refs_0_.refs_1_), custom_call_target="tpu_custom_call" | custom-call | flops 301989888 | tf_op jit(solution)/shard_map/project/pallas_call | solution.py:284
  27.2 0.6 %collective-permute-start.11 = (bf16[64,2304]{1,0:T(8,128)(2,1)S(1)}, bf16[64,2304]{1,0:T(8,128)(2,1)S(1)}, u32[]{:S(2)}, u32[]{:S(2)}) collective-permute-start(bf16[64,2304]{1,0:T(8,128)(2,1)S(1)} %get-tuple-element.59), channel_id=1, source_target_pairs={{0,1},{1,0},{2,3},{3,2},{4,5},{5,4},{6,7},{7,6},{8,9},{9,8},{10,11... | collective-permute-start | bytes 884744 | tf_op jit(solution)/shard_map/ppermute | solution.py:22
  27.7 0.7 %collective-permute-done.10.theirs = bf16[64,3072]{1,0:T(8,128)(2,1)S(1)} collective-permute-done((bf16[64,3072]{1,0:T(8,128)(2,1)S(1)}, bf16[64,3072]{1,0:T(8,128)(2,1)S(1)}, u32[]{:S(2)}, u32[]{:S(2)}) %collective-permute-start.10) | collective-permute-done | bytes 393248 | tf_op jit(solution)/shard_map/ppermute | solution.py:22
  28.4 0.1 add_up.2
  28.5 1.6 %collective-permute-start.15 = (bf16[64,3072]{1,0:T(8,128)(2,1)S(1)}, bf16[64,3072]{1,0:T(8,128)(2,1)S(1)}, u32[]{:S(2)}, u32[]{:S(2)}) collective-permute-start(bf16[64,3072]{1,0:T(8,128)(2,1)S(1)} %add_up.2), channel_id=1, source_target_pairs={{0,2},{1,3},{2,0},{3,1},{4,6},{5,7},{6,4},{7,5},{8,10},{9,11},{10,... | collective-permute-start | bytes 1179656 | tf_op jit(solution)/shard_map/ppermute | solution.py:22
  30.1 0.6 %collective-permute-start.16 = (bf16[64,2304]{1,0:T(8,128)(2,1)S(1)}, bf16[64,2304]{1,0:T(8,128)(2,1)S(1)}, u32[]{:S(2)}, u32[]{:S(2)}) collective-permute-start(bf16[64,2304]{1,0:T(8,128)(2,1)S(1)} %add_up.3), channel_id=1, source_target_pairs={{0,2},{1,3},{2,0},{3,1},{4,6},{5,7},{6,4},{7,5},{8,10},{9,11},{10,... | collective-permute-start | bytes 884744 | tf_op jit(solution)/shard_map/ppermute | solution.py:22
  30.7 0.9 %project.3 = (f32[64,5376]{1,0:T(8,128)S(1)}, bf16[64,1792]{1,0:T(8,128)(2,1)S(1)}, bf16[64,1792]{1,0:T(8,128)(2,1)S(1)}, bf16[64,1792]{1,0:T(8,128)(2,1)S(1)}) custom-call(bf16[128,512]{1,0:T(8,128)(2,1)S(1)} %get-tuple-element.60.rows, bf16[512,3072]{1,0:T(8,128)(2,1)S(1)} %get-tuple-element.36.weight.refs_0_, ...), custom_call_target="tpu_custom_call" | custom-call | flops 704643072 | tf_op jit(solution)/shard_map/project/pallas_call | solution.py:284
  31.6 0.1 collective-permute-start.12
  31.7 0.5 %collective-permute-start.13 = (bf16[64,1792]{1,0:T(8,128)(2,1)S(1)}, bf16[64,1792]{1,0:T(8,128)(2,1)S(1)}, u32[]{:S(2)}, u32[]{:S(2)}) collective-permute-start(bf16[64,1792]{1,0:T(8,128)(2,1)S(1)} %get-tuple-element.63), channel_id=1, source_target_pairs={{0,1},{1,0},{2,3},{3,2},{4,5},{5,4},{6,7},{7,6},{8,9},{9,8},{10,11... | collective-permute-start | bytes 688136 | tf_op jit(solution)/shard_map/ppermute | solution.py:22
  32.2 0.1 collective-permute-start.14
  32.3 0.9 %collective-permute-done.12.refs_0_ = bf16[64,1792]{1,0:T(8,128)(2,1)S(1)} collective-permute-done((bf16[64,1792]{1,0:T(8,128)(2,1)S(1)}, bf16[64,1792]{1,0:T(8,128)(2,1)S(1)}, u32[]{:S(2)}, u32[]{:S(2)}) %collective-permute-start.12) | collective-permute-done | bytes 229408 | tf_op jit(solution)/shard_map/ppermute | solution.py:22
  33.2 0.3 collective-permute-done.13.refs_1_
  33.5 0.3 collective-permute-done.14.refs_2_
  33.8 12.2 %collective-permute-done.16.refs_4_ = bf16[64,2304]{1,0:T(8,128)(2,1)S(1)} collective-permute-done((bf16[64,2304]{1,0:T(8,128)(2,1)S(1)}, bf16[64,2304]{1,0:T(8,128)(2,1)S(1)}, u32[]{:S(2)}, u32[]{:S(2)}) %collective-permute-start.16) | collective-permute-done | bytes 294944 | tf_op jit(solution)/shard_map/ppermute | solution.py:22
  46.0 1.1 %combine.1 = bf16[64,5376]{1,0:T(8,128)(2,1)} custom-call(f32[64,5376]{1,0:T(8,128)S(1)} %get-tuple-element.61.mine, bf16[64,1792]{1,0:T(8,128)(2,1)S(1)} %collective-permute-done.12.refs_0_, bf16[64,1792]{1,0:T(8,128)(2,1)S(1)} %collective-permute-done.13.refs_1_, bf16[64,1792]{1,0:T(8,128)(2,1)S(1)} %collective-permute-done.14.refs_2_, ...), custom_call_target="tpu_custom_call" | custom-call | tf_op jit(solution)/shard_map/combine/pallas_call | solution.py:332
  (16 shorter events, 0.1 us)
Async XLA Ops:
  0.0 11.2 %copy-start.1 = (bf16[256,256]{1,0:T(8,128)(2,1)S(1)}, bf16[256,256]{1,0:T(8,128)(2,1)}, u32[]{:S(2)}) copy-start(bf16[256,256]{1,0:T(8,128)(2,1)} %values_in.1) | copy-start | bytes 393220
  0.0 10.1 %copy-start = (bf16[256,256]{1,0:T(8,128)(2,1)S(1)}, bf16[256,256]{1,0:T(8,128)(2,1)}, u32[]{:S(2)}) copy-start(bf16[256,256]{1,0:T(8,128)(2,1)} %keys_in.1) | copy-start | bytes 393220
  0.0 11.2 %collective-permute-start.3 = (bf16[256,256]{1,0:T(8,128)(2,1)}, bf16[256,256]{1,0:T(8,128)(2,1)S(1)}, u32[]{:S(2)}, u32[]{:S(2)}) collective-permute-start(bf16[256,256]{1,0:T(8,128)(2,1)} %values_in.1), channel_id=1, source_target_pairs={{0,8},{8,16},{16,24},{24,0},{4,12},{12,20},{20,28},{28,4},{1,9},{9... | collective-permute-start | bytes 393224 | tf_op jit(solution)/shard_map/ppermute | solution.py:22
  3.0 9.9 %collective-permute-start = (bf16[256,256]{1,0:T(8,128)(2,1)}, bf16[256,256]{1,0:T(8,128)(2,1)S(1)}, u32[]{:S(2)}, u32[]{:S(2)}) collective-permute-start(bf16[256,256]{1,0:T(8,128)(2,1)} %keys_in.1), channel_id=1, source_target_pairs={{0,4},{4,0},{8,12},{12,8},{16,20},{20,16},{24,28},{28,24},{1,5},{5... | collective-permute-start | bytes 393224 | tf_op jit(solution)/shard_map/ppermute | solution.py:22
  4.5 9.9 %collective-permute-start.2 = (bf16[256,256]{1,0:T(8,128)(2,1)}, bf16[256,256]{1,0:T(8,128)(2,1)S(1)}, u32[]{:S(2)}, u32[]{:S(2)}) collective-permute-start(bf16[256,256]{1,0:T(8,128)(2,1)} %keys_in.1), channel_id=1, source_target_pairs={{0,8},{8,16},{16,24},{24,0},{4,12},{12,20},{20,28},{28,4},{1,9},{9... | collective-permute-start | bytes 393224 | tf_op jit(solution)/shard_map/ppermute | solution.py:22
  6.1 8.9 %collective-permute-start.1 = (bf16[256,256]{1,0:T(8,128)(2,1)}, bf16[256,256]{1,0:T(8,128)(2,1)S(1)}, u32[]{:S(2)}, u32[]{:S(2)}) collective-permute-start(bf16[256,256]{1,0:T(8,128)(2,1)} %values_in.1), channel_id=1, source_target_pairs={{0,4},{4,0},{8,12},{12,8},{16,20},{20,16},{24,28},{28,24},{1,5},{5... | collective-permute-start | bytes 393224 | tf_op jit(solution)/shard_map/ppermute | solution.py:22
  10.1 7.9 %collective-permute-start.4 = (bf16[256,256]{1,0:T(8,128)(2,1)S(1)}, bf16[256,256]{1,0:T(8,128)(2,1)S(1)}, u32[]{:S(2)}, u32[]{:S(2)}) collective-permute-start(bf16[256,256]{1,0:T(8,128)(2,1)S(1)} %copy-done), channel_id=1, source_target_pairs={{0,16},{16,24},{24,8},{8,0},{4,20},{20,28},{28,12},{12,4},{1,17},{... | collective-permute-start | bytes 393224 | tf_op jit(solution)/shard_map/ppermute | solution.py:22
  11.2 10.1 %collective-permute-start.5 = (bf16[256,256]{1,0:T(8,128)(2,1)S(1)}, bf16[256,256]{1,0:T(8,128)(2,1)S(1)}, u32[]{:S(2)}, u32[]{:S(2)}) collective-permute-start(bf16[256,256]{1,0:T(8,128)(2,1)S(1)} %copy-done.1), channel_id=1, source_target_pairs={{0,16},{16,24},{24,8},{8,0},{4,20},{20,28},{28,12},{12,4},{1,17},{... | collective-permute-start | bytes 393224 | tf_op jit(solution)/shard_map/ppermute | solution.py:22
  13.0 8.3 %collective-permute-start.7 = (bf16[256,256]{1,0:T(8,128)(2,1)S(1)}, bf16[256,256]{1,0:T(8,128)(2,1)S(1)}, u32[]{:S(2)}, u32[]{:S(2)}) collective-permute-start(bf16[256,256]{1,0:T(8,128)(2,1)S(1)} %collective-permute-done.3.refs_7_), channel_id=1, source_target_pairs={{0,4},{4,0},{8,12},{12,8},{16,20},{20,16},{24,28},{28,24},{1,5},{5... | collective-permute-start | bytes 393224 | tf_op jit(solution)/shard_map/ppermute | solution.py:22
  14.5 6.8 %collective-permute-start.6 = (bf16[256,256]{1,0:T(8,128)(2,1)S(1)}, bf16[256,256]{1,0:T(8,128)(2,1)S(1)}, u32[]{:S(2)}, u32[]{:S(2)}) collective-permute-start(bf16[256,256]{1,0:T(8,128)(2,1)S(1)} %collective-permute-done.2.refs_6_), channel_id=1, source_target_pairs={{0,4},{4,0},{8,12},{12,8},{16,20},{20,16},{24,28},{28,24},{1,5},{5... | collective-permute-start | bytes 393224 | tf_op jit(solution)/shard_map/ppermute | solution.py:22
  18.0 5.3 %collective-permute-start.8 = (bf16[256,256]{1,0:T(8,128)(2,1)S(1)}, bf16[256,256]{1,0:T(8,128)(2,1)S(1)}, u32[]{:S(2)}, u32[]{:S(2)}) collective-permute-start(bf16[256,256]{1,0:T(8,128)(2,1)S(1)} %collective-permute-done.4.refs_3_), channel_id=1, source_target_pairs={{0,4},{4,0},{8,12},{12,8},{16,20},{20,16},{24,28},{28,24},{1,5},{5... | collective-permute-start | bytes 393224 | tf_op jit(solution)/shard_map/ppermute | solution.py:22
  19.6 5.0 %collective-permute-start.9 = (bf16[256,256]{1,0:T(8,128)(2,1)S(1)}, bf16[256,256]{1,0:T(8,128)(2,1)S(1)}, u32[]{:S(2)}, u32[]{:S(2)}) collective-permute-start(bf16[256,256]{1,0:T(8,128)(2,1)S(1)} %collective-permute-done.1.refs_5_), channel_id=1, source_target_pairs={{0,16},{16,24},{24,8},{8,0},{4,20},{20,28},{28,12},{12,4},{1,17},{... | collective-permute-start | bytes 393224 | tf_op jit(solution)/shard_map/ppermute | solution.py:22
  26.6 1.8 %collective-permute-start.10 = (bf16[64,3072]{1,0:T(8,128)(2,1)S(1)}, bf16[64,3072]{1,0:T(8,128)(2,1)S(1)}, u32[]{:S(2)}, u32[]{:S(2)}) collective-permute-start(bf16[64,3072]{1,0:T(8,128)(2,1)S(1)} %get-tuple-element.57), channel_id=1, source_target_pairs={{0,1},{1,0},{2,3},{3,2},{4,5},{5,4},{6,7},{7,6},{8,9},{9,8},{10,11... | collective-permute-start | bytes 1179656 | tf_op jit(solution)/shard_map/ppermute | solution.py:22
  27.2 2.9 %collective-permute-start.11 = (bf16[64,2304]{1,0:T(8,128)(2,1)S(1)}, bf16[64,2304]{1,0:T(8,128)(2,1)S(1)}, u32[]{:S(2)}, u32[]{:S(2)}) collective-permute-start(bf16[64,2304]{1,0:T(8,128)(2,1)S(1)} %get-tuple-element.59), channel_id=1, source_target_pairs={{0,1},{1,0},{2,3},{3,2},{4,5},{5,4},{6,7},{7,6},{8,9},{9,8},{10,11... | collective-permute-start | bytes 884744 | tf_op jit(solution)/shard_map/ppermute | solution.py:22
  28.5 17.5 %collective-permute-start.15 = (bf16[64,3072]{1,0:T(8,128)(2,1)S(1)}, bf16[64,3072]{1,0:T(8,128)(2,1)S(1)}, u32[]{:S(2)}, u32[]{:S(2)}) collective-permute-start(bf16[64,3072]{1,0:T(8,128)(2,1)S(1)} %add_up.2), channel_id=1, source_target_pairs={{0,2},{1,3},{2,0},{3,1},{4,6},{5,7},{6,4},{7,5},{8,10},{9,11},{10,... | collective-permute-start | bytes 1179656 | tf_op jit(solution)/shard_map/ppermute | solution.py:22
  30.1 15.9 %collective-permute-start.16 = (bf16[64,2304]{1,0:T(8,128)(2,1)S(1)}, bf16[64,2304]{1,0:T(8,128)(2,1)S(1)}, u32[]{:S(2)}, u32[]{:S(2)}) collective-permute-start(bf16[64,2304]{1,0:T(8,128)(2,1)S(1)} %add_up.3), channel_id=1, source_target_pairs={{0,2},{1,3},{2,0},{3,1},{4,6},{5,7},{6,4},{7,5},{8,10},{9,11},{10,... | collective-permute-start | bytes 884744 | tf_op jit(solution)/shard_map/ppermute | solution.py:22
  31.6 1.6 %collective-permute-start.12 = (bf16[64,1792]{1,0:T(8,128)(2,1)S(1)}, bf16[64,1792]{1,0:T(8,128)(2,1)S(1)}, u32[]{:S(2)}, u32[]{:S(2)}) collective-permute-start(bf16[64,1792]{1,0:T(8,128)(2,1)S(1)} %get-tuple-element.62), channel_id=1, source_target_pairs={{0,1},{1,0},{2,3},{3,2},{4,5},{5,4},{6,7},{7,6},{8,9},{9,8},{10,11... | collective-permute-start | bytes 688136 | tf_op jit(solution)/shard_map/ppermute | solution.py:22
  31.7 1.8 %collective-permute-start.13 = (bf16[64,1792]{1,0:T(8,128)(2,1)S(1)}, bf16[64,1792]{1,0:T(8,128)(2,1)S(1)}, u32[]{:S(2)}, u32[]{:S(2)}) collective-permute-start(bf16[64,1792]{1,0:T(8,128)(2,1)S(1)} %get-tuple-element.63), channel_id=1, source_target_pairs={{0,1},{1,0},{2,3},{3,2},{4,5},{5,4},{6,7},{7,6},{8,9},{9,8},{10,11... | collective-permute-start | bytes 688136 | tf_op jit(solution)/shard_map/ppermute | solution.py:22
  32.2 1.6 %collective-permute-start.14 = (bf16[64,1792]{1,0:T(8,128)(2,1)S(1)}, bf16[64,1792]{1,0:T(8,128)(2,1)S(1)}, u32[]{:S(2)}, u32[]{:S(2)}) collective-permute-start(bf16[64,1792]{1,0:T(8,128)(2,1)S(1)} %get-tuple-element.64), channel_id=1, source_target_pairs={{0,1},{1,0},{2,3},{3,2},{4,5},{5,4},{6,7},{7,6},{8,9},{9,8},{10,11... | collective-permute-start | bytes 688136 | tf_op jit(solution)/shard_map/ppermute | solution.py:22

commit v2 on v1

--- a/solution.py
+++ b/solution.py
@@ -22,24 +22,19 @@
     return lax.ppermute(block, axis, pairs)
 
 
-def describe(position, place, doc_ids, n_ctx):
+def chunk_source(number, position, n_ctx):
     first = n_ctx * 3 // 4
     in_first = position < first
-    chunks = [
-        (position, position >= 0),
+    return (
+        (position, None),
         (position ^ 1, position % 2 == 1),
         (position - 2, in_first & (position >= 2)),
         (position - 4, in_first & (position >= 4)),
         ((position - 2) ^ 1, in_first & (position >= 2)),
         ((position - 4) ^ 1, in_first & (position >= 4)),
-    ]
-    numbers = [position, place]
-    for source, there in chunks:
-        numbers += [jnp.where(there, source, 0), there.astype(jnp.int32)]
-    return jnp.concatenate([jnp.stack(numbers), doc_ids])
-
-
-CHUNKS = 6
+    )[number]
+
+
 BESIDE = ((0, 1), (2, 3), (4, 5), (6, 7))
 BY_TWO = ((0, 2, 4, 6), (1, 3, 5, 7))
 BY_FOUR = ((0, 4, 6, 2), (1, 5, 7, 3))
@@ -53,27 +48,28 @@
     return [(ring[i], ring[(i + 1) % len(ring)]) for ring in rings for i in range(len(ring))]
 
 
-def score_blocks(info, q, a, h, chunks, numbers):
-    docs = 2 + 2 * CHUNKS
-    position = info[0]
-    rows = q.shape[0]
+def score_blocks(docs, q, a, h, chunks, numbers):
+    position = lax.axis_index("ctx")
+    n_ctx = lax.axis_size("ctx")
     n_query = chunks[0][0].shape[0]
     q_blocks = n_query // BLOCK
-    doc = info[docs + position * q_blocks + a]
-    row = lax.broadcasted_iota(jnp.int32, (rows, BLOCK), 0) % BLOCK
-    col = lax.broadcasted_iota(jnp.int32, (rows, BLOCK), 1)
+    doc = docs[position * q_blocks + a]
     scores = []
     for (keys, _), c in zip(chunks, numbers):
         count = (a + 1) * BLOCK if c == 0 else n_query
         k = keys[:count, h * HEAD_SIZE : (h + 1) * HEAD_SIZE]
         s = lax.dot_general(q, k, (((1,), (1,)), ((), ())), preferred_element_type=jnp.float32)
-        source, there = info[2 + 2 * c], info[3 + 2 * c]
+        source, there = chunk_source(c, position, n_ctx)
         for b in range(count // BLOCK):
             part = s[:, b * BLOCK : (b + 1) * BLOCK]
             if c == 0 and b == a:
+                row = lax.broadcasted_iota(jnp.int32, part.shape, 0) % BLOCK
+                col = lax.broadcasted_iota(jnp.int32, part.shape, 1)
                 part = jnp.where(row >= col, part, NEG)
             else:
-                seen = (info[docs + source * q_blocks + b] == doc) & (there == 1)
+                seen = docs[jnp.maximum(source, 0) * q_blocks + b] == doc
+                if there is not None:
+                    seen = seen & there
                 part = part + jnp.where(seen, 0.0, NEG)
             scores.append(part)
     return scores
@@ -102,36 +98,46 @@
     return [slice((h * group + g) * HEAD_SIZE, (h * group + g + 1) * HEAD_SIZE) for g in range(group)]
 
 
-def absorb(numbers, info, queries, chunks, before, after):
+def absorb(numbers, docs, queries, chunks, before, after):
     n_query = queries.shape[0]
     factor = SCALE * LOG2E
-    at = 0
+    parts = []
     for a in range(n_query // BLOCK):
         for h in range(chunks[0][0].shape[1] // HEAD_SIZE):
             heads = head_slices(queries, chunks[0][0], h)
-            q = jnp.concatenate([queries[a * BLOCK : (a + 1) * BLOCK, s] for s in heads], axis=0)
-            scores = score_blocks(info, q, a, h, chunks, numbers)
-            rows = slice(at, at + q.shape[0])
-            at += q.shape[0]
-            peak = functools.reduce(jnp.maximum, scores)
-            peak = jnp.max(peak, axis=1, keepdims=True) * factor
-            if before is None:
-                total, added = weigh(scores, peak, factor, a, h, chunks, numbers)
-                peak = jnp.broadcast_to(peak, (q.shape[0], HEAD_SIZE))
-            else:
-                last = before[0][rows, :]
-                peak = jnp.maximum(last, peak)
-                shrink = jnp.exp2(last - peak)
-                total, added = weigh(scores, peak, factor, a, h, chunks, numbers)
-                total = total + before[1][rows, :] * shrink
-                added = added + before[2][rows, :] * shrink
-            after(a, heads, rows, peak, total, added)
+            size = len(heads) * BLOCK
+            parts.append((a, h, heads, slice(len(parts) * size, (len(parts) + 1) * size)))
+    scores = []
+    for a, h, heads, _ in parts:
+        q = jnp.concatenate([queries[a * BLOCK : (a + 1) * BLOCK, s] for s in heads], axis=0)
+        scores.append(score_blocks(docs, q, a, h, chunks, numbers))
+    peaks = [functools.reduce(jnp.maximum, s) for s in scores]
+    peaks = [jnp.max(peak, axis=1, keepdims=True) * factor for peak in peaks]
+    shrinks = None
+    if before is None:
+        peaks = [jnp.broadcast_to(peak, (peak.shape[0], HEAD_SIZE)) for peak in peaks]
+    else:
+        lasts = [before[0][rows, :] for _, _, _, rows in parts]
+        peaks = [jnp.maximum(last, peak) for last, peak in zip(lasts, peaks)]
+        shrinks = [jnp.exp2(last - peak) for last, peak in zip(lasts, peaks)]
+    sums = [
+        weigh(s, peak, factor, a, h, chunks, numbers)
+        for s, peak, (a, h, _, _) in zip(scores, peaks, parts)
+    ]
+    for i, (a, h, heads, rows) in enumerate(parts):
+        total, added = sums[i]
+        if before is not None:
+            total = total + before[1][rows, :] * shrinks[i]
+            added = added + before[2][rows, :] * shrinks[i]
+        sums[i] = (total, added)
+    after(parts, peaks, sums)
 
 
 def store_state(state):
-    def after(a, heads, rows, *parts):
-        for ref, part in zip(state, parts):
-            ref[rows, :] = part
+    def after(parts, peaks, sums):
+        for (_, _, _, rows), peak, (total, added) in zip(parts, peaks, sums):
+            for ref, part in zip(state, (peak, total, added)):
+                ref[rows, :] = part
 
     return after
 
@@ -140,7 +146,7 @@
     return list(zip(refs[0::2], refs[1::2]))
 
 
-def first_kernel(numbers, cut, info, queries_in, keys_in, values_in, weight_in, *refs):
+def first_kernel(numbers, cut, docs, queries_in, keys_in, values_in, weight_in, *refs):
     *state, queries, weight, keys, values, sems = refs
     places = (
         (queries_in, queries),
@@ -153,17 +159,17 @@
         fetch.start()
     for fetch in fetches[:3]:
         fetch.wait()
-    absorb(numbers, info, queries, [(keys, values)], None, store_state(state))
+    absorb(numbers, docs, queries, [(keys, values)], None, store_state(state))
     fetches[3].wait()
 
 
-def next_kernel(numbers, cut, info, queries, *refs):
+def next_kernel(numbers, cut, docs, queries, *refs):
     if cut is not None:
         weight_in, *refs, weight, sem = refs
         fetch = pltpu.make_async_copy(weight_in.at[:, cut:], weight, sem)
         fetch.start()
     pairs = 2 * len(numbers)
-    absorb(numbers, info, queries, pairs_of(refs[3 : 3 + pairs]), refs[:3], store_state(refs[3 + pairs :]))
+    absorb(numbers, docs, queries, pairs_of(refs[3 : 3 + pairs]), refs[:3], store_state(refs[3 + pairs :]))
     if cut is not None:
         fetch.wait()
 
@@ -183,7 +189,7 @@
     return (pltpu.VMEM((rows, HEAD_SIZE), jnp.float32),) * 3
 
 
-def attend_first(info, queries, keys, values, weight, cut):
+def attend_first(docs, queries, keys, values, weight, cut):
     part = pltpu.VMEM((weight.shape[0], cut), weight.dtype)
     return pl.pallas_call(
         functools.partial(first_kernel, (0,), cut),
@@ -198,10 +204,10 @@
         compiler_params=LIMIT,
         cost_estimate=attend_cost(queries, (0,), 2 * weight.size),
         name="attend_first",
-    )(info, *[pltpu.with_memory_space_constraint(x, pltpu.HBM) for x in (queries, keys, values, weight)])
-
-
-def attend_next(info, queries, state, chunks, numbers, weight=None, cut=None):
+    )(docs, *[pltpu.with_memory_space_constraint(x, pltpu.HBM) for x in (queries, keys, values, weight)])
+
+
+def attend_next(docs, queries, state, chunks, numbers, weight=None, cut=None):
     fetched, shapes, scratch = [], state_shapes(queries), []
     if cut is not None:
         fetched = [pltpu.with_memory_space_constraint(weight, pltpu.HBM)]
@@ -216,21 +222,23 @@
         compiler_params=LIMIT,
         cost_estimate=attend_cost(queries, numbers),
         name="attend_next",
-    )(info, queries, *fetched, *state, *[x for pair in chunks for x in pair])
-
-
-def last_kernel(numbers, info, queries, weight, *refs):
+    )(docs, queries, *fetched, *state, *[x for pair in chunks for x in pair])
+
+
+def last_kernel(numbers, docs, queries, weight, *refs):
     pairs = 2 * len(numbers)
     chunks = pairs_of(refs[3 : 3 + pairs])
     far, near, mine, send, attended = refs[3 + pairs :]
 
-    def after(a, heads, rows, peak, total, added):
-        result = (added / jnp.sum(total, axis=1, keepdims=True)).astype(jnp.bfloat16)
-        for g, head in enumerate(heads):
-            attended[a * BLOCK : (a + 1) * BLOCK, head] = result[g * BLOCK : (g + 1) * BLOCK]
-
-    absorb(numbers, info, queries, chunks, refs[:3], after)
-    place = info[1]
+    def after(parts, peaks, sums):
+        inverses = [1.0 / jnp.sum(total, axis=1, keepdims=True) for total, _ in sums]
+        for (a, _, heads, _), inverse, (_, added) in zip(parts, inverses, sums):
+            result = (added * inverse).astype(jnp.bfloat16)
+            for g, head in enumerate(heads):
+                attended[a * BLOCK : (a + 1) * BLOCK, head] = result[g * BLOCK : (g + 1) * BLOCK]
+
+    absorb(numbers, docs, queries, chunks, refs[:3], after)
+    place = lax.axis_index("head")
     share = queries.shape[0] // 4
     for half, owners in ((far, (place ^ 2, place ^ 3)), (near, (place, place ^ 1))):
         for i, owner in enumerate(owners):
@@ -239,7 +247,7 @@
     project_columns(far, [weight], mine, (send,))
 
 
-def attend_last(info, queries, weight, state, chunks, numbers):
+def attend_last(docs, queries, weight, state, chunks, numbers):
     n_query, width = queries.shape
     half = jax.ShapeDtypeStruct((n_query // 2, width), jnp.bfloat16)
     return pl.pallas_call(
@@ -251,7 +259,7 @@
         compiler_params=LIMIT,
         cost_estimate=attend_cost(queries, numbers),
         name="attend_last",
-    )(info, queries, weight, *state, *[x for pair in chunks for x in pair])
+    )(docs, queries, weight, *state, *[x for pair in chunks for x in pair])
 
 
 def project_shapes(rows, count, sends=1):
@@ -310,33 +318,34 @@
     )(mine, theirs)
 
 
-def combine_kernel(counts, mine, *refs):
-    out = refs[-1]
-    ends = []
-    for part in (refs[: counts[0]], refs[counts[0] : -1]):
-        at, pieces = 0, []
-        for ref in part:
-            pieces.append((at, at + ref.shape[1], ref))
-            at += ref.shape[1]
-        ends.append(pieces)
-    for low, high, beside in ends[0]:
-        for start, stop, across in ends[1]:
-            left, right = max(low, start), min(high, stop)
-            if left < right:
-                total = mine[:, left:right] + beside[:, left - low : right - low].astype(jnp.float32)
-                total += across[:, left - start : right - start].astype(jnp.float32)
-                out[:, left:right] = total.astype(out.dtype)
-
-
-def combine(mine, beside, across):
-    return pl.pallas_call(
-        functools.partial(combine_kernel, (len(beside), len(across))),
-        out_shape=jax.ShapeDtypeStruct(mine.shape, across[0].dtype),
-        in_specs=[VMEM] * (1 + len(beside) + len(across)),
-        out_specs=VMEM,
+def combine_kernel(at, mine, across, *refs):
+    *beside, out, total, sem = refs
+    width = across.shape[1]
+    left = 0
+    for part in beside[: len(beside) - (at > 0)]:
+        low, high = max(left, at), min(left + part.shape[1], at + width)
+        if low < high:
+            piece = mine[:, low:high] + part[:, low - left : high - left].astype(jnp.float32)
+            piece += across[:, low - at : high - at].astype(jnp.float32)
+            total[:, low - at : high - at] = piece.astype(total.dtype)
+        left += part.shape[1]
+    copy = pltpu.make_async_copy(total, out.at[:, at : at + width], sem)
+    copy.start()
+    copy.wait()
+
+
+def combine(mine, beside, across, at=0, out=None):
+    outs = [] if out is None else [out]
+    return pl.pallas_call(
+        functools.partial(combine_kernel, at),
+        out_shape=jax.ShapeDtypeStruct(mine.shape, across.dtype),
+        in_specs=[VMEM] * (2 + len(beside)) + [HBM] * len(outs),
+        out_specs=HBM,
+        scratch_shapes=[pltpu.VMEM(across.shape, across.dtype), pltpu.SemaphoreType.DMA],
+        input_output_aliases={2 + len(beside): 0} if outs else {},
         compiler_params=LIMIT,
         name="combine",
-    )(mine, *beside, *across)
+    )(mine, across, *beside, *outs)
 
 
 def from_behind(block, axis, distance):
@@ -429,22 +438,26 @@
     cut = columns * 4 // 7 // BLOCK * BLOCK
 
     if n_ctx == 8:
-        info = describe(position, place, doc_ids, n_ctx)
         by_two = [hop(x, "ctx", cycles(BY_TWO)) for x in (keys, values)]
         beside = [hop(x, "ctx", cycles(BESIDE)) for x in (keys, values)]
-        *state, fetched, weight_a = attend_first(info, queries, keys, values, out_weight, cut)
-        later = [after(keys, state[0]), after(values, by_two[1])]
-        by_four = [hop(x, "ctx", cycles(BY_FOUR)) for x in later]
-        swap_two = [hop(x, "ctx", cycles(BESIDE)) for x in by_two]
+        *state, fetched, weight_a = attend_first(doc_ids, queries, keys, values, out_weight, cut)
+        swap_two = [hop(after(x, state[0]), "ctx", cycles(BESIDE)) for x in by_two]
+        four_keys = hop(keys, "ctx", cycles(BY_FOUR))
+        four_values = hop(after(values, by_two[0]), "ctx", cycles(BY_FOUR))
+        swap_four = [
+            hop(four_keys, "ctx", cycles(BESIDE)),
+            hop(after(beside[1], four_keys), "ctx", cycles(BY_FOUR)),
+        ]
         *state, weight_b = attend_next(
-            info, fetched, state, [beside, by_two], (1, 2), out_weight, cut
+            doc_ids,
+            fetched,
+            state,
+            [beside, by_two, (four_keys, four_values), swap_two],
+            (1, 2, 3, 4),
+            out_weight,
+            cut,
         )
-        swap_four = [
-            hop(after(by_four[0], state[0]), "ctx", cycles(BESIDE)),
-            hop(after(beside[1], by_two[1]), "ctx", cycles(BY_FOUR)),
-        ]
-        state = attend_next(info, fetched, state, [by_four, swap_two], (3, 4))
-        far, near, mine, send = attend_last(info, fetched, weight_a, state, [swap_four], (5,))
+        far, near, mine, send = attend_last(doc_ids, fetched, weight_a, state, [swap_four], (5,))
     else:
         weight_a, weight_b = out_weight[:, :cut], out_weight[:, cut:]
         attended = ring_attention(queries, keys, values, doc_ids, n_ctx, position)
@@ -462,7 +475,8 @@
     near, later_sum = lax.optimization_barrier((near, later_sum))
     mine, *sends = project(near, [weight_a, weight_b], 3)
     theirs = [hop(send, "head", other_core) for send in sends]
-    return combine(mine, theirs, (first_part, second_part))
+    out = combine(mine, theirs, first_part)
+    return combine(mine, theirs, second_part, cut, out)
 
 
 def solution(mesh):

time: 47.2 us -> 46.7 us (0.989)
  starting transfers between devices: 18.2 us -> 20.1 us
  waiting for transfers between devices: 15.7 us -> 14.1 us
  Pallas kernels: 12.3 us -> 11.6 us
    ppermute x17, starting transfers between devices: 18.2 us -> 20.1 us  [hop(): return lax.ppermute(block, axis, pairs)]
    ppermute x17, waiting for transfers between devices: 15.7 us -> 14.1 us  [hop(): return lax.ppermute(block, axis, pairs)]
    pallas_call x2 -> x1, Pallas kernels: 4.96 us -> 3.74 us  [attend_next(): pl.pallas_call(functools.partial(next_kernel, numbers, cut), out_shape=sh...]
    concatenate x1 -> x0, local copies, waits for them, and re-layouts: 0.74 us -> none  [describe(): return jnp.concatenate([jnp.stack(numbers), doc_ids])]
    unnamed x4, local copies, waits for them, and re-layouts: 0.01 us -> 0.66 us
    pallas_call x1 -> x2, Pallas kernels: 1.05 us -> 1.68 us  [combine(): pl.pallas_call(functools.partial(combine_kernel, at), out_shape=jax.Shape...]
  transfers between devices with their start and end apart: 17 -> 17, of which waited for: 6 -> 7; matrix products, arithmetic and copies ran while one was open for 2% -> 0% of each run, Pallas kernels for 20% -> 19%
where the time goes in v2:
time: 46.7 us; the launch traced here: 46.6 us
  starting transfers between devices  20.1 us (43%)
  waiting for transfers between devices  14.1 us (30%)
  Pallas kernels  11.6 us (25%)
  local copies, waits for them, and re-layouts  0.66 us (1%)
    ppermute x17, starting transfers between devices, hop(): return lax.ppermute(block, axis, pairs)  20.1 us
    ppermute x17, waiting for transfers between devices, hop(): return lax.ppermute(block, axis, pairs)  14.1 us
    pallas_call x1, Pallas kernels, attend_next(): pl.pallas_call(functools.partial(next_kernel, numbers, cut), out_shape=sh...  3.74 us
    pallas_call x1, Pallas kernels, attend_first(): pl.pallas_call(functools.partial(first_kernel, (0,), cut), out_shape=stat...  2.69 us
    pallas_call x1, Pallas kernels, attend_last(): pl.pallas_call(functools.partial(last_kernel, numbers), out_shape=(half,...  1.89 us
    pallas_call x2, Pallas kernels, combine(): pl.pallas_call(functools.partial(combine_kernel, at), out_shape=jax.Shape...  1.68 us
    pallas_call x2, Pallas kernels, project(): pl.pallas_call(functools.partial(project_kernel, len(weights)), out_shape...  1.41 us
  transfers between devices with their start and end apart: 17, of which 7 were waited for; matrix products, arithmetic and copies ran while one was open for 0% of the time, Pallas kernels for 19%

profile of v2, /device:TPU:0, one launch (start us, length us, event | category | flops | bytes accessed | tf_op | source)
XLA Modules:
  0.0 46.6 jit_solution(16456262832275978669)
XLA Ops:
  0.0 3.0 %collective-permute-start.2 = (bf16[256,256]{1,0:T(8,128)(2,1)}, bf16[256,256]{1,0:T(8,128)(2,1)S(1)}, u32[]{:S(2)}, u32[]{:S(2)}) collective-permute-start(bf16[256,256]{1,0:T(8,128)(2,1)} %keys_in.1), channel_id=1, source_target_pairs={{0,8},{8,16},{16,24},{24,0},{4,12},{12,20},{20,28},{28,4},{1,9},{9... | collective-permute-start | bytes 393224 | tf_op jit(solution)/shard_map/ppermute | solution.py:22
  3.0 1.6 %collective-permute-start.3 = (bf16[256,256]{1,0:T(8,128)(2,1)}, bf16[256,256]{1,0:T(8,128)(2,1)S(1)}, u32[]{:S(2)}, u32[]{:S(2)}) collective-permute-start(bf16[256,256]{1,0:T(8,128)(2,1)} %values_in.1), channel_id=1, source_target_pairs={{0,8},{8,16},{16,24},{24,0},{4,12},{12,20},{20,28},{28,4},{1,9},{9... | collective-permute-start | bytes 393224 | tf_op jit(solution)/shard_map/ppermute | solution.py:22
  4.6 1.5 %collective-permute-start.1 = (bf16[256,256]{1,0:T(8,128)(2,1)}, bf16[256,256]{1,0:T(8,128)(2,1)S(1)}, u32[]{:S(2)}, u32[]{:S(2)}) collective-permute-start(bf16[256,256]{1,0:T(8,128)(2,1)} %values_in.1), channel_id=1, source_target_pairs={{0,4},{4,0},{8,12},{12,8},{16,20},{20,16},{24,28},{28,24},{1,5},{5... | collective-permute-start | bytes 393224 | tf_op jit(solution)/shard_map/ppermute | solution.py:22
  6.1 1.2 %collective-permute-start.4 = (bf16[256,256]{1,0:T(8,128)(2,1)}, bf16[256,256]{1,0:T(8,128)(2,1)S(1)}, u32[]{:S(2)}, u32[]{:S(2)}) collective-permute-start(bf16[256,256]{1,0:T(8,128)(2,1)} %keys_in.1), channel_id=1, source_target_pairs={{0,16},{16,24},{24,8},{8,0},{4,20},{20,28},{28,12},{12,4},{1,17},{... | collective-permute-start | bytes 393224 | tf_op jit(solution)/shard_map/ppermute | solution.py:22
  7.4 0.3 collective-permute-start
  7.7 0.7 %copy-done = s32[16]{0:T(128)S(1)} copy-done((s32[16]{0:T(128)S(1)}, s32[16]{0:T(128)}, u32[]{:S(2)}) %copy-start) | copy-done | bytes 88
  8.3 2.7 %attend_first.1 = (f32[1024,128]{1,0:T(8,128)S(1)}, f32[1024,128]{1,0:T(8,128)S(1)}, f32[1024,128]{1,0:T(8,128)S(1)}, bf16[256,512]{1,0:T(8,128)(2,1)S(1)}, bf16[512,3072]{1,0:T(8,128)(2,1)S(1)}) custom-call(s32[16]{0:T(128)S(1)} %copy-done, bf16[256,512]{1,0:T(8,128)(2,1)} %queries_in.1, bf16[256,256]{1,0:T(8,128)(2,1)} %keys_in.1, ...), custom_call_target="tpu_custom_call" | custom-call | flops 134217728 | bytes 5505024 | tf_op jit(solution)/shard_map/attend_first/pallas_call | solution.py:194
  11.1 1.8 %collective-permute-start.5 = (bf16[256,256]{1,0:T(8,128)(2,1)S(1)}, bf16[256,256]{1,0:T(8,128)(2,1)S(1)}, u32[]{:S(2)}, u32[]{:S(2)}) collective-permute-start(bf16[256,256]{1,0:T(8,128)(2,1)S(1)} %copy-done.1), channel_id=1, source_target_pairs={{0,16},{16,24},{24,8},{8,0},{4,20},{20,28},{28,12},{12,4},{1,17},{... | collective-permute-start | bytes 393224 | tf_op jit(solution)/shard_map/ppermute | solution.py:22
  12.9 1.5 %collective-permute-start.6 = (bf16[256,256]{1,0:T(8,128)(2,1)S(1)}, bf16[256,256]{1,0:T(8,128)(2,1)S(1)}, u32[]{:S(2)}, u32[]{:S(2)}) collective-permute-start(bf16[256,256]{1,0:T(8,128)(2,1)S(1)} %collective-permute-done.2.refs_6_), channel_id=1, source_target_pairs={{0,4},{4,0},{8,12},{12,8},{16,20},{20,16},{24,28},{28,24},{1,5},{5... | collective-permute-start | bytes 393224 | tf_op jit(solution)/shard_map/ppermute | solution.py:22
  14.4 0.5 %collective-permute-start.7 = (bf16[256,256]{1,0:T(8,128)(2,1)S(1)}, bf16[256,256]{1,0:T(8,128)(2,1)S(1)}, u32[]{:S(2)}, u32[]{:S(2)}) collective-permute-start(bf16[256,256]{1,0:T(8,128)(2,1)S(1)} %collective-permute-done.3.refs_7_), channel_id=1, source_target_pairs={{0,4},{4,0},{8,12},{12,8},{16,20},{20,16},{24,28},{28,24},{1,5},{5... | collective-permute-start | bytes 393224 | tf_op jit(solution)/shard_map/ppermute | solution.py:22
  14.9 1.5 %collective-permute-start.8 = (bf16[256,256]{1,0:T(8,128)(2,1)S(1)}, bf16[256,256]{1,0:T(8,128)(2,1)S(1)}, u32[]{:S(2)}, u32[]{:S(2)}) collective-permute-start(bf16[256,256]{1,0:T(8,128)(2,1)S(1)} %collective-permute-done.4.refs_8_), channel_id=1, source_target_pairs={{0,4},{4,0},{8,12},{12,8},{16,20},{20,16},{24,28},{28,24},{1,5},{5... | collective-permute-start | bytes 393224 | tf_op jit(solution)/shard_map/ppermute | solution.py:22
  16.4 3.6 %collective-permute-start.9 = (bf16[256,256]{1,0:T(8,128)(2,1)S(1)}, bf16[256,256]{1,0:T(8,128)(2,1)S(1)}, u32[]{:S(2)}, u32[]{:S(2)}) collective-permute-start(bf16[256,256]{1,0:T(8,128)(2,1)S(1)} %collective-permute-done.1.refs_5_), channel_id=1, source_target_pairs={{0,16},{16,24},{24,8},{8,0},{4,20},{20,28},{28,12},{12,4},{1,17},{... | collective-permute-start | bytes 393224 | tf_op jit(solution)/shard_map/ppermute | solution.py:22
  20.1 0.6 %collective-permute-done.7.refs_11_ = bf16[256,256]{1,0:T(8,128)(2,1)S(1)} collective-permute-done((bf16[256,256]{1,0:T(8,128)(2,1)S(1)}, bf16[256,256]{1,0:T(8,128)(2,1)S(1)}, u32[]{:S(2)}, u32[]{:S(2)}) %collective-permute-start.7) | collective-permute-done | bytes 131104 | tf_op jit(solution)/shard_map/ppermute | solution.py:22
  20.7 3.7 %attend_next.1 = (f32[1024,128]{1,0:T(8,128)S(1)}, f32[1024,128]{1,0:T(8,128)S(1)}, f32[1024,128]{1,0:T(8,128)S(1)}, bf16[512,2304]{1,0:T(8,128)(2,1)S(1)}) custom-call(s32[16]{0:T(128)S(1)} %copy-done, bf16[256,512]{1,0:T(8,128)(2,1)S(1)} %get-tuple-element.32.queries, bf16[512,5376]{1,0:T(8,128)(2,1)} %refs_0_.1, ...), custom_call_target="tpu_custom_call" | custom-call | flops 536870912 | tf_op jit(solution)/shard_map/attend_next/pallas_call | solution.py:216
  24.4 1.9 %attend_last.1 = (bf16[128,512]{1,0:T(8,128)(2,1)S(1)}, bf16[128,512]{1,0:T(8,128)(2,1)S(1)}, f32[64,3072]{1,0:T(8,128)S(1)}, bf16[64,3072]{1,0:T(8,128)(2,1)S(1)}) custom-call(s32[16]{0:T(128)S(1)} %copy-done, bf16[256,512]{1,0:T(8,128)(2,1)S(1)} %get-tuple-element.32.queries, bf16[512,3072]{1,0:T(8,128)(2,1)S(1)} %get-tuple-element.33.weight.refs_0_, ...), custom_call_target="tpu_custom_call" | custom-call | flops 134217728 | tf_op jit(solution)/shard_map/attend_last/pallas_call | solution.py:253
  26.3 0.1 collective-permute-start.10
  26.4 0.5 %project.2 = (f32[64,2304]{1,0:T(8,128)S(1)}, bf16[64,2304]{1,0:T(8,128)(2,1)S(1)}) custom-call(bf16[128,512]{1,0:T(8,128)(2,1)S(1)} %get-tuple-element.46.rows, bf16[512,2304]{1,0:T(8,128)(2,1)S(1)} %get-tuple-element.47.refs_0_.refs_1_), custom_call_target="tpu_custom_call" | custom-call | flops 301989888 | tf_op jit(solution)/shard_map/project/pallas_call | solution.py:292
  26.9 0.6 %collective-permute-start.11 = (bf16[64,2304]{1,0:T(8,128)(2,1)S(1)}, bf16[64,2304]{1,0:T(8,128)(2,1)S(1)}, u32[]{:S(2)}, u32[]{:S(2)}) collective-permute-start(bf16[64,2304]{1,0:T(8,128)(2,1)S(1)} %get-tuple-element.53), channel_id=1, source_target_pairs={{0,1},{1,0},{2,3},{3,2},{4,5},{5,4},{6,7},{7,6},{8,9},{9,8},{10,11... | collective-permute-start | bytes 884744 | tf_op jit(solution)/shard_map/ppermute | solution.py:22
  27.5 0.7 %collective-permute-done.10.theirs = bf16[64,3072]{1,0:T(8,128)(2,1)S(1)} collective-permute-done((bf16[64,3072]{1,0:T(8,128)(2,1)S(1)}, bf16[64,3072]{1,0:T(8,128)(2,1)S(1)}, u32[]{:S(2)}, u32[]{:S(2)}) %collective-permute-start.10) | collective-permute-done | bytes 393248 | tf_op jit(solution)/shard_map/ppermute | solution.py:22
  28.1 0.1 add_up.2
  28.2 1.6 %collective-permute-start.16 = (bf16[64,3072]{1,0:T(8,128)(2,1)S(1)}, bf16[64,3072]{1,0:T(8,128)(2,1)S(1)}, u32[]{:S(2)}, u32[]{:S(2)}) collective-permute-start(bf16[64,3072]{1,0:T(8,128)(2,1)S(1)} %add_up.2), channel_id=1, source_target_pairs={{0,2},{1,3},{2,0},{3,1},{4,6},{5,7},{6,4},{7,5},{8,10},{9,11},{10,... | collective-permute-start | bytes 1179656 | tf_op jit(solution)/shard_map/ppermute | solution.py:22
  29.8 0.6 %collective-permute-start.12 = (bf16[64,2304]{1,0:T(8,128)(2,1)S(1)}, bf16[64,2304]{1,0:T(8,128)(2,1)S(1)}, u32[]{:S(2)}, u32[]{:S(2)}) collective-permute-start(bf16[64,2304]{1,0:T(8,128)(2,1)S(1)} %add_up.3), channel_id=1, source_target_pairs={{0,2},{1,3},{2,0},{3,1},{4,6},{5,7},{6,4},{7,5},{8,10},{9,11},{10,... | collective-permute-start | bytes 884744 | tf_op jit(solution)/shard_map/ppermute | solution.py:22
  30.4 0.9 %project.3 = (f32[64,5376]{1,0:T(8,128)S(1)}, bf16[64,1792]{1,0:T(8,128)(2,1)S(1)}, bf16[64,1792]{1,0:T(8,128)(2,1)S(1)}, bf16[64,1792]{1,0:T(8,128)(2,1)S(1)}) custom-call(bf16[128,512]{1,0:T(8,128)(2,1)S(1)} %get-tuple-element.54.rows, bf16[512,3072]{1,0:T(8,128)(2,1)S(1)} %get-tuple-element.33.weight.refs_0_, ...), custom_call_target="tpu_custom_call" | custom-call | flops 704643072 | tf_op jit(solution)/shard_map/project/pallas_call | solution.py:292
  31.4 0.5 %collective-permute-start.14 = (bf16[64,1792]{1,0:T(8,128)(2,1)S(1)}, bf16[64,1792]{1,0:T(8,128)(2,1)S(1)}, u32[]{:S(2)}, u32[]{:S(2)}) collective-permute-start(bf16[64,1792]{1,0:T(8,128)(2,1)S(1)} %get-tuple-element.57), channel_id=1, source_target_pairs={{0,1},{1,0},{2,3},{3,2},{4,5},{5,4},{6,7},{7,6},{8,9},{9,8},{10,11... | collective-permute-start | bytes 688136 | tf_op jit(solution)/shard_map/ppermute | solution.py:22
  31.9 0.1 collective-permute-start.15
  32.0 0.9 %collective-permute-done.13.refs_0_ = bf16[64,1792]{1,0:T(8,128)(2,1)S(1)} collective-permute-done((bf16[64,1792]{1,0:T(8,128)(2,1)S(1)}, bf16[64,1792]{1,0:T(8,128)(2,1)S(1)}, u32[]{:S(2)}, u32[]{:S(2)}) %collective-permute-start.13) | collective-permute-done | bytes 229408 | tf_op jit(solution)/shard_map/ppermute | solution.py:22
  32.9 0.3 collective-permute-done.14.refs_1_
  33.2 0.3 collective-permute-done.15.refs_2_
  33.6 6.7 %collective-permute-done.16.across = bf16[64,3072]{1,0:T(8,128)(2,1)S(1)} collective-permute-done((bf16[64,3072]{1,0:T(8,128)(2,1)S(1)}, bf16[64,3072]{1,0:T(8,128)(2,1)S(1)}, u32[]{:S(2)}, u32[]{:S(2)}) %collective-permute-start.16) | collective-permute-done | bytes 393248 | tf_op jit(solution)/shard_map/ppermute | solution.py:22
  40.2 0.9 %combine.2.refs_3_ = bf16[64,5376]{1,0:T(8,128)(2,1)} custom-call(f32[64,5376]{1,0:T(8,128)S(1)} %get-tuple-element.55.mine, bf16[64,3072]{1,0:T(8,128)(2,1)S(1)} %collective-permute-done.16.across, bf16[64,1792]{1,0:T(8,128)(2,1)S(1)} %collective-permute-done.13.refs_0_, bf16[64,1792]{1,0:T(8,128)(2,1)S(1)} %collective-permute-done.14.refs_1_, ...), custom_call_target="tpu_custom_call" | custom-call | tf_op jit(solution)/shard_map/combine/pallas_call | solution.py:339
  41.1 4.6 %collective-permute-done.12.across = bf16[64,2304]{1,0:T(8,128)(2,1)S(1)} collective-permute-done((bf16[64,2304]{1,0:T(8,128)(2,1)S(1)}, bf16[64,2304]{1,0:T(8,128)(2,1)S(1)}, u32[]{:S(2)}, u32[]{:S(2)}) %collective-permute-start.12) | collective-permute-done | bytes 294944 | tf_op jit(solution)/shard_map/ppermute | solution.py:22
  45.7 0.8 %combine.3 = bf16[64,5376]{1,0:T(8,128)(2,1)} custom-call(f32[64,5376]{1,0:T(8,128)S(1)} %get-tuple-element.55.mine, bf16[64,2304]{1,0:T(8,128)(2,1)S(1)} %collective-permute-done.12.across, bf16[64,1792]{1,0:T(8,128)(2,1)S(1)} %collective-permute-done.13.refs_0_, ...), custom_call_target="tpu_custom_call", output_to_operand_aliasing={{}: (5, {})} | custom-call | tf_op jit(solution)/shard_map/combine/pallas_call | solution.py:339
  (15 shorter events, 0.2 us)
Async XLA Ops:
  0.0 11.0 %collective-permute-start.2 = (bf16[256,256]{1,0:T(8,128)(2,1)}, bf16[256,256]{1,0:T(8,128)(2,1)S(1)}, u32[]{:S(2)}, u32[]{:S(2)}) collective-permute-start(bf16[256,256]{1,0:T(8,128)(2,1)} %keys_in.1), channel_id=1, source_target_pairs={{0,8},{8,16},{16,24},{24,0},{4,12},{12,20},{20,28},{28,4},{1,9},{9... | collective-permute-start | bytes 393224 | tf_op jit(solution)/shard_map/ppermute | solution.py:22
  3.0 9.9 %collective-permute-start.3 = (bf16[256,256]{1,0:T(8,128)(2,1)}, bf16[256,256]{1,0:T(8,128)(2,1)S(1)}, u32[]{:S(2)}, u32[]{:S(2)}) collective-permute-start(bf16[256,256]{1,0:T(8,128)(2,1)} %values_in.1), channel_id=1, source_target_pairs={{0,8},{8,16},{16,24},{24,0},{4,12},{12,20},{20,28},{28,4},{1,9},{9... | collective-permute-start | bytes 393224 | tf_op jit(solution)/shard_map/ppermute | solution.py:22
  4.6 9.8 %collective-permute-start.1 = (bf16[256,256]{1,0:T(8,128)(2,1)}, bf16[256,256]{1,0:T(8,128)(2,1)S(1)}, u32[]{:S(2)}, u32[]{:S(2)}) collective-permute-start(bf16[256,256]{1,0:T(8,128)(2,1)} %values_in.1), channel_id=1, source_target_pairs={{0,4},{4,0},{8,12},{12,8},{16,20},{20,16},{24,28},{28,24},{1,5},{5... | collective-permute-start | bytes 393224 | tf_op jit(solution)/shard_map/ppermute | solution.py:22
  6.1 8.8 %collective-permute-start.4 = (bf16[256,256]{1,0:T(8,128)(2,1)}, bf16[256,256]{1,0:T(8,128)(2,1)S(1)}, u32[]{:S(2)}, u32[]{:S(2)}) collective-permute-start(bf16[256,256]{1,0:T(8,128)(2,1)} %keys_in.1), channel_id=1, source_target_pairs={{0,16},{16,24},{24,8},{8,0},{4,20},{20,28},{28,12},{12,4},{1,17},{... | collective-permute-start | bytes 393224 | tf_op jit(solution)/shard_map/ppermute | solution.py:22
  7.4 9.1 %collective-permute-start = (bf16[256,256]{1,0:T(8,128)(2,1)}, bf16[256,256]{1,0:T(8,128)(2,1)S(1)}, u32[]{:S(2)}, u32[]{:S(2)}) collective-permute-start(bf16[256,256]{1,0:T(8,128)(2,1)} %keys_in.1), channel_id=1, source_target_pairs={{0,4},{4,0},{8,12},{12,8},{16,20},{20,16},{24,28},{28,24},{1,5},{5... | collective-permute-start | bytes 393224 | tf_op jit(solution)/shard_map/ppermute | solution.py:22
  7.7 0.7 %copy-start = (s32[16]{0:T(128)S(1)}, s32[16]{0:T(128)}, u32[]{:S(2)}) copy-start(s32[16]{0:T(128)} %docs.5) | copy-start | bytes 196
  8.3 2.7 %copy-start.1 = (bf16[256,256]{1,0:T(8,128)(2,1)S(1)}, bf16[256,256]{1,0:T(8,128)(2,1)}, u32[]{:S(2)}) copy-start(bf16[256,256]{1,0:T(8,128)(2,1)} %values_in.1) | copy-start | bytes 393220
  11.1 9.0 %collective-permute-start.5 = (bf16[256,256]{1,0:T(8,128)(2,1)S(1)}, bf16[256,256]{1,0:T(8,128)(2,1)S(1)}, u32[]{:S(2)}, u32[]{:S(2)}) collective-permute-start(bf16[256,256]{1,0:T(8,128)(2,1)S(1)} %copy-done.1), channel_id=1, source_target_pairs={{0,16},{16,24},{24,8},{8,0},{4,20},{20,28},{28,12},{12,4},{1,17},{... | collective-permute-start | bytes 393224 | tf_op jit(solution)/shard_map/ppermute | solution.py:22
  12.9 7.2 %collective-permute-start.6 = (bf16[256,256]{1,0:T(8,128)(2,1)S(1)}, bf16[256,256]{1,0:T(8,128)(2,1)S(1)}, u32[]{:S(2)}, u32[]{:S(2)}) collective-permute-start(bf16[256,256]{1,0:T(8,128)(2,1)S(1)} %collective-permute-done.2.refs_6_), channel_id=1, source_target_pairs={{0,4},{4,0},{8,12},{12,8},{16,20},{20,16},{24,28},{28,24},{1,5},{5... | collective-permute-start | bytes 393224 | tf_op jit(solution)/shard_map/ppermute | solution.py:22
  14.4 6.3 %collective-permute-start.7 = (bf16[256,256]{1,0:T(8,128)(2,1)S(1)}, bf16[256,256]{1,0:T(8,128)(2,1)S(1)}, u32[]{:S(2)}, u32[]{:S(2)}) collective-permute-start(bf16[256,256]{1,0:T(8,128)(2,1)S(1)} %collective-permute-done.3.refs_7_), channel_id=1, source_target_pairs={{0,4},{4,0},{8,12},{12,8},{16,20},{20,16},{24,28},{28,24},{1,5},{5... | collective-permute-start | bytes 393224 | tf_op jit(solution)/shard_map/ppermute | solution.py:22
  14.9 9.5 %collective-permute-start.8 = (bf16[256,256]{1,0:T(8,128)(2,1)S(1)}, bf16[256,256]{1,0:T(8,128)(2,1)S(1)}, u32[]{:S(2)}, u32[]{:S(2)}) collective-permute-start(bf16[256,256]{1,0:T(8,128)(2,1)S(1)} %collective-permute-done.4.refs_8_), channel_id=1, source_target_pairs={{0,4},{4,0},{8,12},{12,8},{16,20},{20,16},{24,28},{28,24},{1,5},{5... | collective-permute-start | bytes 393224 | tf_op jit(solution)/shard_map/ppermute | solution.py:22
  16.4 8.0 %collective-permute-start.9 = (bf16[256,256]{1,0:T(8,128)(2,1)S(1)}, bf16[256,256]{1,0:T(8,128)(2,1)S(1)}, u32[]{:S(2)}, u32[]{:S(2)}) collective-permute-start(bf16[256,256]{1,0:T(8,128)(2,1)S(1)} %collective-permute-done.1.refs_5_), channel_id=1, source_target_pairs={{0,16},{16,24},{24,8},{8,0},{4,20},{20,28},{28,12},{12,4},{1,17},{... | collective-permute-start | bytes 393224 | tf_op jit(solution)/shard_map/ppermute | solution.py:22
  26.3 1.8 %collective-permute-start.10 = (bf16[64,3072]{1,0:T(8,128)(2,1)S(1)}, bf16[64,3072]{1,0:T(8,128)(2,1)S(1)}, u32[]{:S(2)}, u32[]{:S(2)}) collective-permute-start(bf16[64,3072]{1,0:T(8,128)(2,1)S(1)} %get-tuple-element.51), channel_id=1, source_target_pairs={{0,1},{1,0},{2,3},{3,2},{4,5},{5,4},{6,7},{7,6},{8,9},{9,8},{10,11... | collective-permute-start | bytes 1179656 | tf_op jit(solution)/shard_map/ppermute | solution.py:22
  26.9 2.9 %collective-permute-start.11 = (bf16[64,2304]{1,0:T(8,128)(2,1)S(1)}, bf16[64,2304]{1,0:T(8,128)(2,1)S(1)}, u32[]{:S(2)}, u32[]{:S(2)}) collective-permute-start(bf16[64,2304]{1,0:T(8,128)(2,1)S(1)} %get-tuple-element.53), channel_id=1, source_target_pairs={{0,1},{1,0},{2,3},{3,2},{4,5},{5,4},{6,7},{7,6},{8,9},{9,8},{10,11... | collective-permute-start | bytes 884744 | tf_op jit(solution)/shard_map/ppermute | solution.py:22
  28.2 12.0 %collective-permute-start.16 = (bf16[64,3072]{1,0:T(8,128)(2,1)S(1)}, bf16[64,3072]{1,0:T(8,128)(2,1)S(1)}, u32[]{:S(2)}, u32[]{:S(2)}) collective-permute-start(bf16[64,3072]{1,0:T(8,128)(2,1)S(1)} %add_up.2), channel_id=1, source_target_pairs={{0,2},{1,3},{2,0},{3,1},{4,6},{5,7},{6,4},{7,5},{8,10},{9,11},{10,... | collective-permute-start | bytes 1179656 | tf_op jit(solution)/shard_map/ppermute | solution.py:22
  29.8 15.9 %collective-permute-start.12 = (bf16[64,2304]{1,0:T(8,128)(2,1)S(1)}, bf16[64,2304]{1,0:T(8,128)(2,1)S(1)}, u32[]{:S(2)}, u32[]{:S(2)}) collective-permute-start(bf16[64,2304]{1,0:T(8,128)(2,1)S(1)} %add_up.3), channel_id=1, source_target_pairs={{0,2},{1,3},{2,0},{3,1},{4,6},{5,7},{6,4},{7,5},{8,10},{9,11},{10,... | collective-permute-start | bytes 884744 | tf_op jit(solution)/shard_map/ppermute | solution.py:22
  31.4 1.6 %collective-permute-start.13 = (bf16[64,1792]{1,0:T(8,128)(2,1)S(1)}, bf16[64,1792]{1,0:T(8,128)(2,1)S(1)}, u32[]{:S(2)}, u32[]{:S(2)}) collective-permute-start(bf16[64,1792]{1,0:T(8,128)(2,1)S(1)} %get-tuple-element.56), channel_id=1, source_target_pairs={{0,1},{1,0},{2,3},{3,2},{4,5},{5,4},{6,7},{7,6},{8,9},{9,8},{10,11... | collective-permute-start | bytes 688136 | tf_op jit(solution)/shard_map/ppermute | solution.py:22
  31.4 1.8 %collective-permute-start.14 = (bf16[64,1792]{1,0:T(8,128)(2,1)S(1)}, bf16[64,1792]{1,0:T(8,128)(2,1)S(1)}, u32[]{:S(2)}, u32[]{:S(2)}) collective-permute-start(bf16[64,1792]{1,0:T(8,128)(2,1)S(1)} %get-tuple-element.57), channel_id=1, source_target_pairs={{0,1},{1,0},{2,3},{3,2},{4,5},{5,4},{6,7},{7,6},{8,9},{9,8},{10,11... | collective-permute-start | bytes 688136 | tf_op jit(solution)/shard_map/ppermute | solution.py:22
  31.9 1.6 %collective-permute-start.15 = (bf16[64,1792]{1,0:T(8,128)(2,1)S(1)}, bf16[64,1792]{1,0:T(8,128)(2,1)S(1)}, u32[]{:S(2)}, u32[]{:S(2)}) collective-permute-start(bf16[64,1792]{1,0:T(8,128)(2,1)S(1)} %get-tuple-element.58), channel_id=1, source_target_pairs={{0,1},{1,0},{2,3},{3,2},{4,5},{5,4},{6,7},{7,6},{8,9},{9,8},{10,11... | collective-permute-start | bytes 688136 | tf_op jit(solution)/shard_map/ppermute | solution.py:22

commit v3 on v2

--- a/solution.py
+++ b/solution.py
@@ -22,17 +22,9 @@
     return lax.ppermute(block, axis, pairs)
 
 
-def chunk_source(number, position, n_ctx):
-    first = n_ctx * 3 // 4
-    in_first = position < first
-    return (
-        (position, None),
-        (position ^ 1, position % 2 == 1),
-        (position - 2, in_first & (position >= 2)),
-        (position - 4, in_first & (position >= 4)),
-        ((position - 2) ^ 1, in_first & (position >= 2)),
-        ((position - 4) ^ 1, in_first & (position >= 4)),
-    )[number]
+def in_place(number, position, n_ctx):
+    away = {2: 2, 3: 4, 4: 2, 5: 4}[number]
+    return (position < n_ctx * 3 // 4) & (position >= away)
 
 
 BESIDE = ((0, 1), (2, 3), (4, 5), (6, 7))
@@ -48,29 +40,25 @@
     return [(ring[i], ring[(i + 1) % len(ring)]) for ring in rings for i in range(len(ring))]
 
 
-def score_blocks(docs, q, a, h, chunks, numbers):
+def score_blocks(doors, q, a, h, chunks, numbers):
     position = lax.axis_index("ctx")
     n_ctx = lax.axis_size("ctx")
     n_query = chunks[0][0].shape[0]
-    q_blocks = n_query // BLOCK
-    doc = docs[position * q_blocks + a]
     scores = []
     for (keys, _), c in zip(chunks, numbers):
         count = (a + 1) * BLOCK if c == 0 else n_query
         k = keys[:count, h * HEAD_SIZE : (h + 1) * HEAD_SIZE]
         s = lax.dot_general(q, k, (((1,), (1,)), ((), ())), preferred_element_type=jnp.float32)
-        source, there = chunk_source(c, position, n_ctx)
         for b in range(count // BLOCK):
             part = s[:, b * BLOCK : (b + 1) * BLOCK]
             if c == 0 and b == a:
                 row = lax.broadcasted_iota(jnp.int32, part.shape, 0) % BLOCK
                 col = lax.broadcasted_iota(jnp.int32, part.shape, 1)
                 part = jnp.where(row >= col, part, NEG)
+            elif c < 2:
+                part = part + doors(c, a, b)
             else:
-                seen = docs[jnp.maximum(source, 0) * q_blocks + b] == doc
-                if there is not None:
-                    seen = seen & there
-                part = part + jnp.where(seen, 0.0, NEG)
+                part = part + jnp.where(in_place(c, position, n_ctx), 0.0, NEG)
             scores.append(part)
     return scores
 
@@ -98,7 +86,7 @@
     return [slice((h * group + g) * HEAD_SIZE, (h * group + g + 1) * HEAD_SIZE) for g in range(group)]
 
 
-def absorb(numbers, docs, queries, chunks, before, after):
+def absorb(numbers, doors, queries, chunks, before, after):
     n_query = queries.shape[0]
     factor = SCALE * LOG2E
     parts = []
@@ -110,7 +98,7 @@
     scores = []
     for a, h, heads, _ in parts:
         q = jnp.concatenate([queries[a * BLOCK : (a + 1) * BLOCK, s] for s in heads], axis=0)
-        scores.append(score_blocks(docs, q, a, h, chunks, numbers))
+        scores.append(score_blocks(doors, q, a, h, chunks, numbers))
     peaks = [functools.reduce(jnp.maximum, s) for s in scores]
     peaks = [jnp.max(peak, axis=1, keepdims=True) * factor for peak in peaks]
     shrinks = None
@@ -146,32 +134,42 @@
     return list(zip(refs[0::2], refs[1::2]))
 
 
-def first_kernel(numbers, cut, docs, queries_in, keys_in, values_in, weight_in, *refs):
-    *state, queries, weight, keys, values, sems = refs
-    places = (
-        (queries_in, queries),
-        (keys_in, keys),
-        (values_in, values),
-        (weight_in.at[:, :cut], weight),
-    )
+def first_kernel(docs_in, queries_in, keys_in, values_in, *refs):
+    *state, queries, open_beside, docs, keys, values, sems = refs
+    places = ((docs_in, docs), (queries_in, queries), (keys_in, keys), (values_in, values))
     fetches = [pltpu.make_async_copy(a, b, sems.at[i]) for i, (a, b) in enumerate(places)]
     for fetch in fetches:
         fetch.start()
-    for fetch in fetches[:3]:
+    for fetch in fetches:
         fetch.wait()
-    absorb(numbers, docs, queries, [(keys, values)], None, store_state(state))
-    fetches[3].wait()
-
-
-def next_kernel(numbers, cut, docs, queries, *refs):
-    if cut is not None:
-        weight_in, *refs, weight, sem = refs
-        fetch = pltpu.make_async_copy(weight_in.at[:, cut:], weight, sem)
-        fetch.start()
+    position = lax.axis_index("ctx")
+    q_blocks = queries.shape[0] // BLOCK
+
+    def doors(number, a, b):
+        source = position if number == 0 else jnp.maximum(position - 1, 0)
+        seen = docs[source * q_blocks + b] == docs[position * q_blocks + a]
+        if number == 1:
+            seen = seen & (position % 2 == 1)
+        return jnp.where(seen, 0.0, NEG)
+
+    for a in range(q_blocks):
+        for b in range(q_blocks):
+            part = open_beside.at[a * 8 : (a + 1) * 8, b * BLOCK : (b + 1) * BLOCK]
+            part[...] = jnp.full(part.shape, doors(1, a, b), jnp.float32)
+    absorb((0,), doors, queries, [(keys, values)], None, store_state(state))
+
+
+def next_kernel(numbers, queries, open_beside, weight_in, *refs):
+    *refs, weight, sem = refs
+    fetch = pltpu.make_async_copy(weight_in, weight, sem)
+    fetch.start()
     pairs = 2 * len(numbers)
-    absorb(numbers, docs, queries, pairs_of(refs[3 : 3 + pairs]), refs[:3], store_state(refs[3 + pairs :]))
-    if cut is not None:
-        fetch.wait()
+
+    def doors(number, a, b):
+        return open_beside[a * 8 : a * 8 + 1, b * BLOCK : (b + 1) * BLOCK]
+
+    absorb(numbers, doors, queries, pairs_of(refs[3 : 3 + pairs]), refs[:3], store_state(refs[3 + pairs :]))
+    fetch.wait()
 
 
 def attend_cost(queries, numbers, fetched=0):
@@ -189,43 +187,49 @@
     return (pltpu.VMEM((rows, HEAD_SIZE), jnp.float32),) * 3
 
 
-def attend_first(docs, queries, keys, values, weight, cut):
-    part = pltpu.VMEM((weight.shape[0], cut), weight.dtype)
-    return pl.pallas_call(
-        functools.partial(first_kernel, (0,), cut),
-        out_shape=state_shapes(queries) + (pltpu.VMEM(queries.shape, queries.dtype), part),
-        in_specs=[SMEM, HBM, HBM, HBM, HBM],
+def attend_first(docs, queries, keys, values):
+    n_query = queries.shape[0]
+    return pl.pallas_call(
+        first_kernel,
+        out_shape=state_shapes(queries)
+        + (
+            pltpu.VMEM(queries.shape, queries.dtype),
+            pltpu.VMEM((8 * n_query // BLOCK, n_query), jnp.float32),
+        ),
+        in_specs=[HBM] * 4,
         out_specs=(VMEM,) * 5,
         scratch_shapes=[
+            pltpu.SMEM(docs.shape, docs.dtype),
             pltpu.VMEM(keys.shape, keys.dtype),
             pltpu.VMEM(values.shape, values.dtype),
             pltpu.SemaphoreType.DMA((4,)),
         ],
         compiler_params=LIMIT,
-        cost_estimate=attend_cost(queries, (0,), 2 * weight.size),
+        cost_estimate=attend_cost(queries, (0,)),
         name="attend_first",
-    )(docs, *[pltpu.with_memory_space_constraint(x, pltpu.HBM) for x in (queries, keys, values, weight)])
-
-
-def attend_next(docs, queries, state, chunks, numbers, weight=None, cut=None):
-    fetched, shapes, scratch = [], state_shapes(queries), []
-    if cut is not None:
-        fetched = [pltpu.with_memory_space_constraint(weight, pltpu.HBM)]
-        shapes += (pltpu.VMEM((weight.shape[0], weight.shape[1] - cut), weight.dtype),)
-        scratch = [pltpu.SemaphoreType.DMA]
-    return pl.pallas_call(
-        functools.partial(next_kernel, numbers, cut),
-        out_shape=shapes,
-        in_specs=[SMEM, VMEM] + [HBM] * len(fetched) + [VMEM] * (3 + 2 * len(chunks)),
-        out_specs=(VMEM,) * len(shapes),
-        scratch_shapes=scratch,
-        compiler_params=LIMIT,
-        cost_estimate=attend_cost(queries, numbers),
+    )(*[pltpu.with_memory_space_constraint(x, pltpu.HBM) for x in (docs, queries, keys, values)])
+
+
+def attend_next(queries, open_beside, weight, state, chunks, numbers):
+    return pl.pallas_call(
+        functools.partial(next_kernel, numbers),
+        out_shape=state_shapes(queries) + (pltpu.VMEM(weight.shape, weight.dtype),),
+        in_specs=[VMEM, VMEM, HBM] + [VMEM] * (3 + 2 * len(chunks)),
+        out_specs=(VMEM,) * 4,
+        scratch_shapes=[pltpu.SemaphoreType.DMA],
+        compiler_params=LIMIT,
+        cost_estimate=attend_cost(queries, numbers, 2 * weight.size),
         name="attend_next",
-    )(docs, queries, *fetched, *state, *[x for pair in chunks for x in pair])
-
-
-def last_kernel(numbers, docs, queries, weight, *refs):
+    )(
+        queries,
+        open_beside,
+        pltpu.with_memory_space_constraint(weight, pltpu.HBM),
+        *state,
+        *[x for pair in chunks for x in pair],
+    )
+
+
+def last_kernel(numbers, columns, queries, weight, *refs):
     pairs = 2 * len(numbers)
     chunks = pairs_of(refs[3 : 3 + pairs])
     far, near, mine, send, attended = refs[3 + pairs :]
@@ -237,29 +241,29 @@
             for g, head in enumerate(heads):
                 attended[a * BLOCK : (a + 1) * BLOCK, head] = result[g * BLOCK : (g + 1) * BLOCK]
 
-    absorb(numbers, docs, queries, chunks, refs[:3], after)
+    absorb(numbers, None, queries, chunks, refs[:3], after)
     place = lax.axis_index("head")
     share = queries.shape[0] // 4
     for half, owners in ((far, (place ^ 2, place ^ 3)), (near, (place, place ^ 1))):
         for i, owner in enumerate(owners):
             source = pl.ds(pl.multiple_of(owner * share, share), share)
             half[i * share : (i + 1) * share, :] = attended[source, :]
-    project_columns(far, [weight], mine, (send,))
-
-
-def attend_last(docs, queries, weight, state, chunks, numbers):
+    project_columns(far, weight, mine, (send,), *columns)
+
+
+def attend_last(queries, weight, state, chunks, numbers, columns):
     n_query, width = queries.shape
     half = jax.ShapeDtypeStruct((n_query // 2, width), jnp.bfloat16)
     return pl.pallas_call(
-        functools.partial(last_kernel, numbers),
-        out_shape=(half, half) + project_shapes(n_query // 4, weight.shape[1]),
-        in_specs=[SMEM] + [VMEM] * (5 + 2 * len(numbers)),
+        functools.partial(last_kernel, numbers, columns),
+        out_shape=(half, half) + project_shapes(n_query // 4, columns[1] - columns[0]),
+        in_specs=[VMEM] * (5 + 2 * len(numbers)),
         out_specs=(VMEM,) * 4,
         scratch_shapes=[pltpu.VMEM(queries.shape, jnp.bfloat16)],
         compiler_params=LIMIT,
         cost_estimate=attend_cost(queries, numbers),
         name="attend_last",
-    )(docs, queries, weight, *state, *[x for pair in chunks for x in pair])
+    )(queries, weight, *state, *[x for pair in chunks for x in pair])
 
 
 def project_shapes(rows, count, sends=1):
@@ -267,39 +271,35 @@
     return (jax.ShapeDtypeStruct((rows, count), jnp.float32),) + (send,) * sends
 
 
-def project_columns(rows, weights, mine, sends):
+def project_columns(rows, weight, mine, sends, start, end):
     share = rows.shape[0] // 2
     width = sends[0].shape[1]
-    ends = [0]
-    for weight in weights:
-        ends.append(ends[-1] + weight.shape[1])
-    stops = sorted(set(ends) | {i * width for i in range(len(sends) + 1)} | set(range(0, ends[-1], 768)))
-    for left, right in zip(stops[:-1], stops[1:]):
-        i = max(i for i in range(len(weights)) if ends[i] <= left)
-        columns = weights[i][:, left - ends[i] : right - ends[i]]
-        product = jnp.dot(rows[...], columns, preferred_element_type=jnp.float32)
-        mine[:, left:right] = product[:share]
-        send, at = sends[left // width], left // width * width
-        send[:, left - at : right - at] = product[share:].astype(send.dtype)
-
-
-def project_kernel(count, rows, *refs):
-    project_columns(rows, refs[:count], refs[count], refs[count + 1 :])
-
-
-def project(rows, weights, sends=1):
-    columns = sum(weight.shape[1] for weight in weights)
-    return pl.pallas_call(
-        functools.partial(project_kernel, len(weights)),
-        out_shape=project_shapes(rows.shape[0] // 2, columns, sends),
-        in_specs=[VMEM] * (1 + len(weights)),
+    for i, send in enumerate(sends):
+        for at in range(0, width, 768):
+            stop = min(at + 768, width)
+            columns = weight[:, start + i * width + at : start + i * width + stop]
+            product = jnp.dot(rows[...], columns, preferred_element_type=jnp.float32)
+            mine[:, i * width + at : i * width + stop] = product[:share]
+            send[:, at:stop] = product[share:].astype(send.dtype)
+
+
+def project_kernel(columns, rows, weight, mine, *sends):
+    project_columns(rows, weight, mine, sends, *columns)
+
+
+def project(rows, weight, columns, sends=1):
+    count = columns[1] - columns[0]
+    return pl.pallas_call(
+        functools.partial(project_kernel, columns),
+        out_shape=project_shapes(rows.shape[0] // 2, count, sends),
+        in_specs=[VMEM, VMEM],
         out_specs=(VMEM,) * (1 + sends),
         compiler_params=LIMIT,
         cost_estimate=pl.CostEstimate(
-            flops=2 * rows.shape[0] * rows.shape[1] * columns, bytes_accessed=0, transcendentals=0
+            flops=2 * rows.shape[0] * rows.shape[1] * count, bytes_accessed=0, transcendentals=0
         ),
         name="project",
-    )(rows, *weights)
+    )(rows, weight)
 
 
 def add_kernel(mine, theirs, out):
@@ -440,31 +440,25 @@
     if n_ctx == 8:
         by_two = [hop(x, "ctx", cycles(BY_TWO)) for x in (keys, values)]
         beside = [hop(x, "ctx", cycles(BESIDE)) for x in (keys, values)]
-        *state, fetched, weight_a = attend_first(doc_ids, queries, keys, values, out_weight, cut)
+        *state, fetched, open_beside = attend_first(doc_ids, queries, keys, values)
         swap_two = [hop(after(x, state[0]), "ctx", cycles(BESIDE)) for x in by_two]
-        four_keys = hop(keys, "ctx", cycles(BY_FOUR))
+        four_keys = hop(after(after(keys, beside[0]), state[0]), "ctx", cycles(BY_FOUR))
         four_values = hop(after(values, by_two[0]), "ctx", cycles(BY_FOUR))
         swap_four = [
             hop(four_keys, "ctx", cycles(BESIDE)),
             hop(after(beside[1], four_keys), "ctx", cycles(BY_FOUR)),
         ]
-        *state, weight_b = attend_next(
-            doc_ids,
-            fetched,
-            state,
-            [beside, by_two, (four_keys, four_values), swap_two],
-            (1, 2, 3, 4),
-            out_weight,
-            cut,
-        )
-        far, near, mine, send = attend_last(doc_ids, fetched, weight_a, state, [swap_four], (5,))
+        chunks = [beside, by_two, swap_two]
+        *state, weight = attend_next(fetched, open_beside, out_weight, state, chunks, (1, 2, 4))
+        chunks = [(four_keys, four_values), swap_four]
+        far, near, mine, send = attend_last(fetched, weight, state, chunks, (3, 5), (0, cut))
     else:
-        weight_a, weight_b = out_weight[:, :cut], out_weight[:, cut:]
+        weight = out_weight
         attended = ring_attention(queries, keys, values, doc_ids, n_ctx, position)
         far, near = part_rows(attended, place)
-        mine, send = project(far, [weight_a])
+        mine, send = project(far, weight, (0, cut))
     theirs = hop(send, "head", other_core)
-    later_mine, later_send = project(far, [weight_b])
+    later_mine, later_send = project(far, weight, (cut, columns))
     mine, later_mine = lax.optimization_barrier((mine, later_mine))
     first_sum = add_up(mine, theirs)
     first_part = hop(first_sum, "head", other_chip)
@@ -473,7 +467,7 @@
     later_sum = add_up(later_mine, later_theirs)
     second_part = hop(later_sum, "head", other_chip)
     near, later_sum = lax.optimization_barrier((near, later_sum))
-    mine, *sends = project(near, [weight_a, weight_b], 3)
+    mine, *sends = project(near, weight, (0, columns), 3)
     theirs = [hop(send, "head", other_core) for send in sends]
     out = combine(mine, theirs, first_part)
     return combine(mine, theirs, second_part, cut, out)

time: 46.7 us -> 44.8 us (0.959)
  waiting for transfers between devices: 14.1 us -> 17.4 us
  Pallas kernels: 11.6 us -> 8.97 us
  starting transfers between devices: 20.1 us -> 18.2 us
  local copies, waits for them, and re-layouts: 0.66 us -> 0 us
    ppermute x17, waiting for transfers between devices: 14.1 us -> 17.4 us  [hop(): return lax.ppermute(block, axis, pairs)]
    pallas_call x5, Pallas kernels: 9.74 us -> 7.17 us  [the longest x1 2.59 us: attend_next(): pl.pallas_call(functools.partial(next_kernel, numbers), out_shape=state_s...]
    ppermute x17, starting transfers between devices: 20.1 us -> 18.2 us  [hop(): return lax.ppermute(block, axis, pairs)]
    unnamed x4 -> x0, local copies, waits for them, and re-layouts: 0.66 us -> none
  transfers between devices with their start and end apart: 17 -> 17, of which waited for: 7 -> 10; matrix products, arithmetic and copies ran while one was open for 0% -> 0% of each run, Pallas kernels for 19% -> 15%
where the time goes in v3:
time: 44.8 us; the launch traced here: 44.6 us
  starting transfers between devices  18.2 us (41%)
  waiting for transfers between devices  17.4 us (39%)
  Pallas kernels  8.97 us (20%)
    ppermute x17, starting transfers between devices, hop(): return lax.ppermute(block, axis, pairs)  18.2 us
    ppermute x17, waiting for transfers between devices, hop(): return lax.ppermute(block, axis, pairs)  17.4 us
    pallas_call x1, Pallas kernels, attend_next(): pl.pallas_call(functools.partial(next_kernel, numbers), out_shape=state_s...  2.59 us
    pallas_call x2, Pallas kernels, combine(): pl.pallas_call(functools.partial(combine_kernel, at), out_shape=jax.Shape...  1.68 us
    pallas_call x1, Pallas kernels, attend_last(): pl.pallas_call(functools.partial(last_kernel, numbers, columns), out_shap...  1.61 us
    pallas_call x1, Pallas kernels, attend_first(): pl.pallas_call(first_kernel, out_shape=state_shapes(queries) + (pltpu.VME...  1.6 us
    pallas_call x2, Pallas kernels, project(): pl.pallas_call(functools.partial(project_kernel, columns), out_shape=proj...  1.36 us
  transfers between devices with their start and end apart: 17, of which 10 were waited for; matrix products, arithmetic and copies ran while one was open for 0% of the time, Pallas kernels for 15%

profile of v3, /device:TPU:0, one launch (start us, length us, event | category | flops | bytes accessed | tf_op | source)
XLA Modules:
  0.0 44.6 jit_solution(12425367419868515966)
XLA Ops:
  0.0 3.0 %collective-permute-start = (bf16[256,256]{1,0:T(8,128)(2,1)}, bf16[256,256]{1,0:T(8,128)(2,1)S(1)}, u32[]{:S(2)}, u32[]{:S(2)}) collective-permute-start(bf16[256,256]{1,0:T(8,128)(2,1)} %keys_in.1), channel_id=1, source_target_pairs={{0,4},{4,0},{8,12},{12,8},{16,20},{20,16},{24,28},{28,24},{1,5},{5... | collective-permute-start | bytes 393224 | tf_op jit(solution)/shard_map/ppermute | solution.py:22
  3.0 1.6 %collective-permute-start.2 = (bf16[256,256]{1,0:T(8,128)(2,1)}, bf16[256,256]{1,0:T(8,128)(2,1)S(1)}, u32[]{:S(2)}, u32[]{:S(2)}) collective-permute-start(bf16[256,256]{1,0:T(8,128)(2,1)} %keys_in.1), channel_id=1, source_target_pairs={{0,8},{8,16},{16,24},{24,0},{4,12},{12,20},{20,28},{28,4},{1,9},{9... | collective-permute-start | bytes 393224 | tf_op jit(solution)/shard_map/ppermute | solution.py:22
  4.5 1.6 %collective-permute-start.3 = (bf16[256,256]{1,0:T(8,128)(2,1)}, bf16[256,256]{1,0:T(8,128)(2,1)S(1)}, u32[]{:S(2)}, u32[]{:S(2)}) collective-permute-start(bf16[256,256]{1,0:T(8,128)(2,1)} %values_in.1), channel_id=1, source_target_pairs={{0,8},{8,16},{16,24},{24,0},{4,12},{12,20},{20,28},{28,4},{1,9},{9... | collective-permute-start | bytes 393224 | tf_op jit(solution)/shard_map/ppermute | solution.py:22
  6.1 0.5 %collective-permute-start.1 = (bf16[256,256]{1,0:T(8,128)(2,1)}, bf16[256,256]{1,0:T(8,128)(2,1)S(1)}, u32[]{:S(2)}, u32[]{:S(2)}) collective-permute-start(bf16[256,256]{1,0:T(8,128)(2,1)} %values_in.1), channel_id=1, source_target_pairs={{0,4},{4,0},{8,12},{12,8},{16,20},{20,16},{24,28},{28,24},{1,5},{5... | collective-permute-start | bytes 393224 | tf_op jit(solution)/shard_map/ppermute | solution.py:22
  6.6 1.6 %attend_first.1 = (f32[1024,128]{1,0:T(8,128)S(1)}, f32[1024,128]{1,0:T(8,128)S(1)}, f32[1024,128]{1,0:T(8,128)S(1)}, bf16[256,512]{1,0:T(8,128)(2,1)S(1)}, f32[16,256]{1,0:T(8,128)S(1)}) custom-call(s32[16]{0:T(128)} %docs_in.1, bf16[256,512]{1,0:T(8,128)(2,1)} %queries_in.1, bf16[256,256]{1,0:T(8,128)(2,1)} %keys_in.1, bf16[256,256]{1,0:T(8,128)(2,1)} %values_in.1), custom_call_target="tpu_custom_call" | custom-call | flops 134217728 | tf_op jit(solution)/shard_map/attend_first/pallas_call | solution.py:192
  8.2 1.5 %collective-permute-start.6 = (bf16[256,256]{1,0:T(8,128)(2,1)}, bf16[256,256]{1,0:T(8,128)(2,1)S(1)}, u32[]{:S(2)}, u32[]{:S(2)}) collective-permute-start(bf16[256,256]{1,0:T(8,128)(2,1)} %keys_in.1), channel_id=1, source_target_pairs={{0,16},{16,24},{24,8},{8,0},{4,20},{20,28},{28,12},{12,4},{1,17},{... | collective-permute-start | bytes 393224 | tf_op jit(solution)/shard_map/ppermute | solution.py:22
  9.8 1.7 %collective-permute-done.2.refs_5_ = bf16[256,256]{1,0:T(8,128)(2,1)S(1)} collective-permute-done((bf16[256,256]{1,0:T(8,128)(2,1)}, bf16[256,256]{1,0:T(8,128)(2,1)S(1)}, u32[]{:S(2)}, u32[]{:S(2)}) %collective-permute-start.2) | collective-permute-done | bytes 131104 | tf_op jit(solution)/shard_map/ppermute | solution.py:22
  11.5 0.7 %collective-permute-start.4 = (bf16[256,256]{1,0:T(8,128)(2,1)S(1)}, bf16[256,256]{1,0:T(8,128)(2,1)S(1)}, u32[]{:S(2)}, u32[]{:S(2)}) collective-permute-start(bf16[256,256]{1,0:T(8,128)(2,1)S(1)} %collective-permute-done.2.refs_5_), channel_id=1, source_target_pairs={{0,4},{4,0},{8,12},{12,8},{16,20},{20,16},{24,28},{28,24},{1,5},{5... | collective-permute-start | bytes 393224 | tf_op jit(solution)/shard_map/ppermute | solution.py:22
  12.2 1.8 %collective-permute-done.3.refs_6_ = bf16[256,256]{1,0:T(8,128)(2,1)S(1)} collective-permute-done((bf16[256,256]{1,0:T(8,128)(2,1)}, bf16[256,256]{1,0:T(8,128)(2,1)S(1)}, u32[]{:S(2)}, u32[]{:S(2)}) %collective-permute-start.3) | collective-permute-done | bytes 131104 | tf_op jit(solution)/shard_map/ppermute | solution.py:22
  13.9 3.8 %collective-permute-start.7 = (bf16[256,256]{1,0:T(8,128)(2,1)}, bf16[256,256]{1,0:T(8,128)(2,1)S(1)}, u32[]{:S(2)}, u32[]{:S(2)}) collective-permute-start(bf16[256,256]{1,0:T(8,128)(2,1)} %values_in.1), channel_id=1, source_target_pairs={{0,16},{16,24},{24,8},{8,0},{4,20},{20,28},{28,12},{12,4},{1,17},{... | collective-permute-start | bytes 393224 | tf_op jit(solution)/shard_map/ppermute | solution.py:22
  17.8 2.0 %collective-permute-start.8 = (bf16[256,256]{1,0:T(8,128)(2,1)S(1)}, bf16[256,256]{1,0:T(8,128)(2,1)S(1)}, u32[]{:S(2)}, u32[]{:S(2)}) collective-permute-start(bf16[256,256]{1,0:T(8,128)(2,1)S(1)} %collective-permute-done.6.refs_3_), channel_id=1, source_target_pairs={{0,4},{4,0},{8,12},{12,8},{16,20},{20,16},{24,28},{28,24},{1,5},{5... | collective-permute-start | bytes 393224 | tf_op jit(solution)/shard_map/ppermute | solution.py:22
  19.9 2.6 %attend_next.1 = (f32[1024,128]{1,0:T(8,128)S(1)}, f32[1024,128]{1,0:T(8,128)S(1)}, f32[1024,128]{1,0:T(8,128)S(1)}, bf16[512,5376]{1,0:T(8,128)(2,1)S(1)}) custom-call(bf16[256,512]{1,0:T(8,128)(2,1)S(1)} %get-tuple-element.34.queries, f32[16,256]{1,0:T(8,128)S(1)} %get-tuple-element.35.open_beside, bf16[512,5376]{1,0:T(8,128)(2,1)} %weight_in.1, ...), custom_call_target="tpu_custom_call" | custom-call | flops 402653184 | bytes 5505024 | tf_op jit(solution)/shard_map/attend_next/pallas_call | solution.py:214
  22.5 0.3 collective-permute-done.9.refs_6_
  22.7 0.1 collective-permute-done.8.refs_5_
  22.8 1.6 %attend_last.1 = (bf16[128,512]{1,0:T(8,128)(2,1)S(1)}, bf16[128,512]{1,0:T(8,128)(2,1)S(1)}, f32[64,3072]{1,0:T(8,128)S(1)}, bf16[64,3072]{1,0:T(8,128)(2,1)S(1)}) custom-call(bf16[256,512]{1,0:T(8,128)(2,1)S(1)} %get-tuple-element.34.queries, bf16[512,5376]{1,0:T(8,128)(2,1)S(1)} %get-tuple-element.41.weight, f32[1024,128]{1,0:T(8,128)S(1)} %get-tuple-element.42.refs_0_, ...), custom_call_target="tpu_custom_call" | custom-call | flops 268435456 | tf_op jit(solution)/shard_map/attend_last/pallas_call | solution.py:257
  24.4 0.1 collective-permute-start.10
  24.5 0.5 %project.2 = (f32[64,2304]{1,0:T(8,128)S(1)}, bf16[64,2304]{1,0:T(8,128)(2,1)S(1)}) custom-call(bf16[128,512]{1,0:T(8,128)(2,1)S(1)} %get-tuple-element.51.rows, bf16[512,5376]{1,0:T(8,128)(2,1)S(1)} %get-tuple-element.41.weight), custom_call_target="tpu_custom_call" | custom-call | flops 301989888 | tf_op jit(solution)/shard_map/project/pallas_call | solution.py:292
  25.0 0.6 %collective-permute-start.11 = (bf16[64,2304]{1,0:T(8,128)(2,1)S(1)}, bf16[64,2304]{1,0:T(8,128)(2,1)S(1)}, u32[]{:S(2)}, u32[]{:S(2)}) collective-permute-start(bf16[64,2304]{1,0:T(8,128)(2,1)S(1)} %get-tuple-element.57), channel_id=1, source_target_pairs={{0,1},{1,0},{2,3},{3,2},{4,5},{5,4},{6,7},{7,6},{8,9},{9,8},{10,11... | collective-permute-start | bytes 884744 | tf_op jit(solution)/shard_map/ppermute | solution.py:22
  25.5 0.7 %collective-permute-done.10.theirs = bf16[64,3072]{1,0:T(8,128)(2,1)S(1)} collective-permute-done((bf16[64,3072]{1,0:T(8,128)(2,1)S(1)}, bf16[64,3072]{1,0:T(8,128)(2,1)S(1)}, u32[]{:S(2)}, u32[]{:S(2)}) %collective-permute-start.10) | collective-permute-done | bytes 393248 | tf_op jit(solution)/shard_map/ppermute | solution.py:22
  26.3 1.6 %collective-permute-start.16 = (bf16[64,3072]{1,0:T(8,128)(2,1)S(1)}, bf16[64,3072]{1,0:T(8,128)(2,1)S(1)}, u32[]{:S(2)}, u32[]{:S(2)}) collective-permute-start(bf16[64,3072]{1,0:T(8,128)(2,1)S(1)} %add_up.2), channel_id=1, source_target_pairs={{0,2},{1,3},{2,0},{3,1},{4,6},{5,7},{6,4},{7,5},{8,10},{9,11},{10,... | collective-permute-start | bytes 1179656 | tf_op jit(solution)/shard_map/ppermute | solution.py:22
  27.9 0.6 %collective-permute-start.12 = (bf16[64,2304]{1,0:T(8,128)(2,1)S(1)}, bf16[64,2304]{1,0:T(8,128)(2,1)S(1)}, u32[]{:S(2)}, u32[]{:S(2)}) collective-permute-start(bf16[64,2304]{1,0:T(8,128)(2,1)S(1)} %add_up.3), channel_id=1, source_target_pairs={{0,2},{1,3},{2,0},{3,1},{4,6},{5,7},{6,4},{7,5},{8,10},{9,11},{10,... | collective-permute-start | bytes 884744 | tf_op jit(solution)/shard_map/ppermute | solution.py:22
  28.5 0.9 %project.3 = (f32[64,5376]{1,0:T(8,128)S(1)}, bf16[64,1792]{1,0:T(8,128)(2,1)S(1)}, bf16[64,1792]{1,0:T(8,128)(2,1)S(1)}, bf16[64,1792]{1,0:T(8,128)(2,1)S(1)}) custom-call(bf16[128,512]{1,0:T(8,128)(2,1)S(1)} %get-tuple-element.58.rows, bf16[512,5376]{1,0:T(8,128)(2,1)S(1)} %get-tuple-element.41.weight), custom_call_target="tpu_custom_call" | custom-call | flops 704643072 | tf_op jit(solution)/shard_map/project/pallas_call | solution.py:292
  29.4 0.1 collective-permute-start.13
  29.5 0.5 %collective-permute-start.14 = (bf16[64,1792]{1,0:T(8,128)(2,1)S(1)}, bf16[64,1792]{1,0:T(8,128)(2,1)S(1)}, u32[]{:S(2)}, u32[]{:S(2)}) collective-permute-start(bf16[64,1792]{1,0:T(8,128)(2,1)S(1)} %get-tuple-element.61), channel_id=1, source_target_pairs={{0,1},{1,0},{2,3},{3,2},{4,5},{5,4},{6,7},{7,6},{8,9},{9,8},{10,11... | collective-permute-start | bytes 688136 | tf_op jit(solution)/shard_map/ppermute | solution.py:22
  30.0 0.1 collective-permute-start.15
  30.0 0.9 %collective-permute-done.13.refs_0_ = bf16[64,1792]{1,0:T(8,128)(2,1)S(1)} collective-permute-done((bf16[64,1792]{1,0:T(8,128)(2,1)S(1)}, bf16[64,1792]{1,0:T(8,128)(2,1)S(1)}, u32[]{:S(2)}, u32[]{:S(2)}) %collective-permute-start.13) | collective-permute-done | bytes 229408 | tf_op jit(solution)/shard_map/ppermute | solution.py:22
  30.9 0.3 collective-permute-done.14.refs_1_
  31.3 0.3 collective-permute-done.15.refs_2_
  31.6 6.7 %collective-permute-done.16.across = bf16[64,3072]{1,0:T(8,128)(2,1)S(1)} collective-permute-done((bf16[64,3072]{1,0:T(8,128)(2,1)S(1)}, bf16[64,3072]{1,0:T(8,128)(2,1)S(1)}, u32[]{:S(2)}, u32[]{:S(2)}) %collective-permute-start.16) | collective-permute-done | bytes 393248 | tf_op jit(solution)/shard_map/ppermute | solution.py:22
  38.3 0.9 %combine.2.refs_3_ = bf16[64,5376]{1,0:T(8,128)(2,1)} custom-call(f32[64,5376]{1,0:T(8,128)S(1)} %get-tuple-element.59.mine, bf16[64,3072]{1,0:T(8,128)(2,1)S(1)} %collective-permute-done.16.across, bf16[64,1792]{1,0:T(8,128)(2,1)S(1)} %collective-permute-done.13.refs_0_, bf16[64,1792]{1,0:T(8,128)(2,1)S(1)} %collective-permute-done.14.refs_1_, ...), custom_call_target="tpu_custom_call" | custom-call | tf_op jit(solution)/shard_map/combine/pallas_call | solution.py:339
  39.2 4.6 %collective-permute-done.12.across = bf16[64,2304]{1,0:T(8,128)(2,1)S(1)} collective-permute-done((bf16[64,2304]{1,0:T(8,128)(2,1)S(1)}, bf16[64,2304]{1,0:T(8,128)(2,1)S(1)}, u32[]{:S(2)}, u32[]{:S(2)}) %collective-permute-start.12) | collective-permute-done | bytes 294944 | tf_op jit(solution)/shard_map/ppermute | solution.py:22
  43.8 0.8 %combine.3 = bf16[64,5376]{1,0:T(8,128)(2,1)} custom-call(f32[64,5376]{1,0:T(8,128)S(1)} %get-tuple-element.59.mine, bf16[64,2304]{1,0:T(8,128)(2,1)S(1)} %collective-permute-done.12.across, bf16[64,1792]{1,0:T(8,128)(2,1)S(1)} %collective-permute-done.13.refs_0_, ...), custom_call_target="tpu_custom_call", output_to_operand_aliasing={{}: (5, {})} | custom-call | tf_op jit(solution)/shard_map/combine/pallas_call | solution.py:339
  (11 shorter events, 0.2 us)
Async XLA Ops:
  0.0 8.2 %collective-permute-start = (bf16[256,256]{1,0:T(8,128)(2,1)}, bf16[256,256]{1,0:T(8,128)(2,1)S(1)}, u32[]{:S(2)}, u32[]{:S(2)}) collective-permute-start(bf16[256,256]{1,0:T(8,128)(2,1)} %keys_in.1), channel_id=1, source_target_pairs={{0,4},{4,0},{8,12},{12,8},{16,20},{20,16},{24,28},{28,24},{1,5},{5... | collective-permute-start | bytes 393224 | tf_op jit(solution)/shard_map/ppermute | solution.py:22
  3.0 8.5 %collective-permute-start.2 = (bf16[256,256]{1,0:T(8,128)(2,1)}, bf16[256,256]{1,0:T(8,128)(2,1)S(1)}, u32[]{:S(2)}, u32[]{:S(2)}) collective-permute-start(bf16[256,256]{1,0:T(8,128)(2,1)} %keys_in.1), channel_id=1, source_target_pairs={{0,8},{8,16},{16,24},{24,0},{4,12},{12,20},{20,28},{28,4},{1,9},{9... | collective-permute-start | bytes 393224 | tf_op jit(solution)/shard_map/ppermute | solution.py:22
  4.5 9.4 %collective-permute-start.3 = (bf16[256,256]{1,0:T(8,128)(2,1)}, bf16[256,256]{1,0:T(8,128)(2,1)S(1)}, u32[]{:S(2)}, u32[]{:S(2)}) collective-permute-start(bf16[256,256]{1,0:T(8,128)(2,1)} %values_in.1), channel_id=1, source_target_pairs={{0,8},{8,16},{16,24},{24,0},{4,12},{12,20},{20,28},{28,4},{1,9},{9... | collective-permute-start | bytes 393224 | tf_op jit(solution)/shard_map/ppermute | solution.py:22
  6.1 11.6 %collective-permute-start.1 = (bf16[256,256]{1,0:T(8,128)(2,1)}, bf16[256,256]{1,0:T(8,128)(2,1)S(1)}, u32[]{:S(2)}, u32[]{:S(2)}) collective-permute-start(bf16[256,256]{1,0:T(8,128)(2,1)} %values_in.1), channel_id=1, source_target_pairs={{0,4},{4,0},{8,12},{12,8},{16,20},{20,16},{24,28},{28,24},{1,5},{5... | collective-permute-start | bytes 393224 | tf_op jit(solution)/shard_map/ppermute | solution.py:22
  8.2 9.5 %collective-permute-start.6 = (bf16[256,256]{1,0:T(8,128)(2,1)}, bf16[256,256]{1,0:T(8,128)(2,1)S(1)}, u32[]{:S(2)}, u32[]{:S(2)}) collective-permute-start(bf16[256,256]{1,0:T(8,128)(2,1)} %keys_in.1), channel_id=1, source_target_pairs={{0,16},{16,24},{24,8},{8,0},{4,20},{20,28},{28,12},{12,4},{1,17},{... | collective-permute-start | bytes 393224 | tf_op jit(solution)/shard_map/ppermute | solution.py:22
  11.5 8.4 %collective-permute-start.4 = (bf16[256,256]{1,0:T(8,128)(2,1)S(1)}, bf16[256,256]{1,0:T(8,128)(2,1)S(1)}, u32[]{:S(2)}, u32[]{:S(2)}) collective-permute-start(bf16[256,256]{1,0:T(8,128)(2,1)S(1)} %collective-permute-done.2.refs_5_), channel_id=1, source_target_pairs={{0,4},{4,0},{8,12},{12,8},{16,20},{20,16},{24,28},{28,24},{1,5},{5... | collective-permute-start | bytes 393224 | tf_op jit(solution)/shard_map/ppermute | solution.py:22
  13.9 5.9 %collective-permute-start.5 = (bf16[256,256]{1,0:T(8,128)(2,1)S(1)}, bf16[256,256]{1,0:T(8,128)(2,1)S(1)}, u32[]{:S(2)}, u32[]{:S(2)}) collective-permute-start(bf16[256,256]{1,0:T(8,128)(2,1)S(1)} %collective-permute-done.3.refs_6_), channel_id=1, source_target_pairs={{0,4},{4,0},{8,12},{12,8},{16,20},{20,16},{24,28},{28,24},{1,5},{5... | collective-permute-start | bytes 393224 | tf_op jit(solution)/shard_map/ppermute | solution.py:22
  13.9 8.5 %collective-permute-start.7 = (bf16[256,256]{1,0:T(8,128)(2,1)}, bf16[256,256]{1,0:T(8,128)(2,1)S(1)}, u32[]{:S(2)}, u32[]{:S(2)}) collective-permute-start(bf16[256,256]{1,0:T(8,128)(2,1)} %values_in.1), channel_id=1, source_target_pairs={{0,16},{16,24},{24,8},{8,0},{4,20},{20,28},{28,12},{12,4},{1,17},{... | collective-permute-start | bytes 393224 | tf_op jit(solution)/shard_map/ppermute | solution.py:22
  17.8 5.0 %collective-permute-start.9 = (bf16[256,256]{1,0:T(8,128)(2,1)S(1)}, bf16[256,256]{1,0:T(8,128)(2,1)S(1)}, u32[]{:S(2)}, u32[]{:S(2)}) collective-permute-start(bf16[256,256]{1,0:T(8,128)(2,1)S(1)} %collective-permute-done.1.refs_4_), channel_id=1, source_target_pairs={{0,16},{16,24},{24,8},{8,0},{4,20},{20,28},{28,12},{12,4},{1,17},{... | collective-permute-start | bytes 393224 | tf_op jit(solution)/shard_map/ppermute | solution.py:22
  17.8 5.0 %collective-permute-start.8 = (bf16[256,256]{1,0:T(8,128)(2,1)S(1)}, bf16[256,256]{1,0:T(8,128)(2,1)S(1)}, u32[]{:S(2)}, u32[]{:S(2)}) collective-permute-start(bf16[256,256]{1,0:T(8,128)(2,1)S(1)} %collective-permute-done.6.refs_3_), channel_id=1, source_target_pairs={{0,4},{4,0},{8,12},{12,8},{16,20},{20,16},{24,28},{28,24},{1,5},{5... | collective-permute-start | bytes 393224 | tf_op jit(solution)/shard_map/ppermute | solution.py:22
  24.4 1.8 %collective-permute-start.10 = (bf16[64,3072]{1,0:T(8,128)(2,1)S(1)}, bf16[64,3072]{1,0:T(8,128)(2,1)S(1)}, u32[]{:S(2)}, u32[]{:S(2)}) collective-permute-start(bf16[64,3072]{1,0:T(8,128)(2,1)S(1)} %get-tuple-element.55), channel_id=1, source_target_pairs={{0,1},{1,0},{2,3},{3,2},{4,5},{5,4},{6,7},{7,6},{8,9},{9,8},{10,11... | collective-permute-start | bytes 1179656 | tf_op jit(solution)/shard_map/ppermute | solution.py:22
  25.0 2.9 %collective-permute-start.11 = (bf16[64,2304]{1,0:T(8,128)(2,1)S(1)}, bf16[64,2304]{1,0:T(8,128)(2,1)S(1)}, u32[]{:S(2)}, u32[]{:S(2)}) collective-permute-start(bf16[64,2304]{1,0:T(8,128)(2,1)S(1)} %get-tuple-element.57), channel_id=1, source_target_pairs={{0,1},{1,0},{2,3},{3,2},{4,5},{5,4},{6,7},{7,6},{8,9},{9,8},{10,11... | collective-permute-start | bytes 884744 | tf_op jit(solution)/shard_map/ppermute | solution.py:22
  26.3 12.0 %collective-permute-start.16 = (bf16[64,3072]{1,0:T(8,128)(2,1)S(1)}, bf16[64,3072]{1,0:T(8,128)(2,1)S(1)}, u32[]{:S(2)}, u32[]{:S(2)}) collective-permute-start(bf16[64,3072]{1,0:T(8,128)(2,1)S(1)} %add_up.2), channel_id=1, source_target_pairs={{0,2},{1,3},{2,0},{3,1},{4,6},{5,7},{6,4},{7,5},{8,10},{9,11},{10,... | collective-permute-start | bytes 1179656 | tf_op jit(solution)/shard_map/ppermute | solution.py:22
  27.9 15.9 %collective-permute-start.12 = (bf16[64,2304]{1,0:T(8,128)(2,1)S(1)}, bf16[64,2304]{1,0:T(8,128)(2,1)S(1)}, u32[]{:S(2)}, u32[]{:S(2)}) collective-permute-start(bf16[64,2304]{1,0:T(8,128)(2,1)S(1)} %add_up.3), channel_id=1, source_target_pairs={{0,2},{1,3},{2,0},{3,1},{4,6},{5,7},{6,4},{7,5},{8,10},{9,11},{10,... | collective-permute-start | bytes 884744 | tf_op jit(solution)/shard_map/ppermute | solution.py:22
  29.4 1.6 %collective-permute-start.13 = (bf16[64,1792]{1,0:T(8,128)(2,1)S(1)}, bf16[64,1792]{1,0:T(8,128)(2,1)S(1)}, u32[]{:S(2)}, u32[]{:S(2)}) collective-permute-start(bf16[64,1792]{1,0:T(8,128)(2,1)S(1)} %get-tuple-element.60), channel_id=1, source_target_pairs={{0,1},{1,0},{2,3},{3,2},{4,5},{5,4},{6,7},{7,6},{8,9},{9,8},{10,11... | collective-permute-start | bytes 688136 | tf_op jit(solution)/shard_map/ppermute | solution.py:22
  29.5 1.8 %collective-permute-start.14 = (bf16[64,1792]{1,0:T(8,128)(2,1)S(1)}, bf16[64,1792]{1,0:T(8,128)(2,1)S(1)}, u32[]{:S(2)}, u32[]{:S(2)}) collective-permute-start(bf16[64,1792]{1,0:T(8,128)(2,1)S(1)} %get-tuple-element.61), channel_id=1, source_target_pairs={{0,1},{1,0},{2,3},{3,2},{4,5},{5,4},{6,7},{7,6},{8,9},{9,8},{10,11... | collective-permute-start | bytes 688136 | tf_op jit(solution)/shard_map/ppermute | solution.py:22
  30.0 1.6 %collective-permute-start.15 = (bf16[64,1792]{1,0:T(8,128)(2,1)S(1)}, bf16[64,1792]{1,0:T(8,128)(2,1)S(1)}, u32[]{:S(2)}, u32[]{:S(2)}) collective-permute-start(bf16[64,1792]{1,0:T(8,128)(2,1)S(1)} %get-tuple-element.62), channel_id=1, source_target_pairs={{0,1},{1,0},{2,3},{3,2},{4,5},{5,4},{6,7},{7,6},{8,9},{9,8},{10,11... | collective-permute-start | bytes 688136 | tf_op jit(solution)/shard_map/ppermute | solution.py:22

commit v4 on v3

--- a/solution.py
+++ b/solution.py
@@ -28,8 +28,8 @@
 
 
 BESIDE = ((0, 1), (2, 3), (4, 5), (6, 7))
-BY_TWO = ((0, 2, 4, 6), (1, 3, 5, 7))
-BY_FOUR = ((0, 4, 6, 2), (1, 5, 7, 3))
+BY_TWO = ((0, 2, 4), (1, 3, 5), (6,), (7,))
+BY_FOUR = ((0, 4), (1, 5), (2,), (3,), (6,), (7,))
 
 
 def after(x, event):
@@ -442,16 +442,13 @@
         beside = [hop(x, "ctx", cycles(BESIDE)) for x in (keys, values)]
         *state, fetched, open_beside = attend_first(doc_ids, queries, keys, values)
         swap_two = [hop(after(x, state[0]), "ctx", cycles(BESIDE)) for x in by_two]
-        four_keys = hop(after(after(keys, beside[0]), state[0]), "ctx", cycles(BY_FOUR))
-        four_values = hop(after(values, by_two[0]), "ctx", cycles(BY_FOUR))
-        swap_four = [
-            hop(four_keys, "ctx", cycles(BESIDE)),
-            hop(after(beside[1], four_keys), "ctx", cycles(BY_FOUR)),
-        ]
-        chunks = [beside, by_two, swap_two]
-        *state, weight = attend_next(fetched, open_beside, out_weight, state, chunks, (1, 2, 4))
-        chunks = [(four_keys, four_values), swap_four]
-        far, near, mine, send = attend_last(fetched, weight, state, chunks, (3, 5), (0, cut))
+        by_four = [after(after(x, beside[0]), state[0]) for x in (keys, values)]
+        by_four = [hop(x, "ctx", cycles(BY_FOUR)) for x in by_four]
+        beside_four = [hop(x, "ctx", cycles(BY_FOUR)) for x in beside]
+        chunks = [beside, by_two, by_four]
+        *state, weight = attend_next(fetched, open_beside, out_weight, state, chunks, (1, 2, 3))
+        chunks = [swap_two, beside_four]
+        far, near, mine, send = attend_last(fetched, weight, state, chunks, (4, 5), (0, cut))
     else:
         weight = out_weight
         attended = ring_attention(queries, keys, values, doc_ids, n_ctx, position)

time: 44.8 us -> 54.2 us (1.21)
  starting transfers between devices: 18.2 us -> 29.5 us
  waiting for transfers between devices: 17.4 us -> 15.2 us
    ppermute x17, starting transfers between devices: 18.2 us -> 29.5 us  [hop(): return lax.ppermute(block, axis, pairs)]
    ppermute x17, waiting for transfers between devices: 17.4 us -> 15.2 us  [hop(): return lax.ppermute(block, axis, pairs)]
  transfers between devices with their start and end apart: 17 -> 17, of which waited for: 10 -> 7; matrix products, arithmetic and copies ran while one was open for 0% -> 0% of each run, Pallas kernels for 15% -> 12%
where the time goes in v4:
time: 54.2 us; the launch traced here: 53.9 us
  starting transfers between devices  29.5 us (54%)
  waiting for transfers between devices  15.2 us (28%)
  Pallas kernels  8.97 us (17%)
    ppermute x17, starting transfers between devices, hop(): return lax.ppermute(block, axis, pairs)  29.5 us
    ppermute x17, waiting for transfers between devices, hop(): return lax.ppermute(block, axis, pairs)  15.2 us
    pallas_call x1, Pallas kernels, attend_next(): pl.pallas_call(functools.partial(next_kernel, numbers), out_shape=state_s...  2.59 us
    pallas_call x2, Pallas kernels, combine(): pl.pallas_call(functools.partial(combine_kernel, at), out_shape=jax.Shape...  1.68 us
    pallas_call x1, Pallas kernels, attend_first(): pl.pallas_call(first_kernel, out_shape=state_shapes(queries) + (pltpu.VME...  1.61 us
    pallas_call x1, Pallas kernels, attend_last(): pl.pallas_call(functools.partial(last_kernel, numbers, columns), out_shap...  1.6 us
    pallas_call x2, Pallas kernels, project(): pl.pallas_call(functools.partial(project_kernel, columns), out_shape=proj...  1.36 us
  transfers between devices with their start and end apart: 17, of which 7 were waited for; matrix products, arithmetic and copies ran while one was open for 0% of the time, Pallas kernels for 12%

profile of v4, /device:TPU:0, one launch (start us, length us, event | category | flops | bytes accessed | tf_op | source)
XLA Modules:
  0.0 53.9 jit_solution(17257521900093206618)
XLA Ops:
  0.0 3.0 %collective-permute-start = (bf16[256,256]{1,0:T(8,128)(2,1)}, bf16[256,256]{1,0:T(8,128)(2,1)S(1)}, u32[]{:S(2)}, u32[]{:S(2)}) collective-permute-start(bf16[256,256]{1,0:T(8,128)(2,1)} %keys_in.1), channel_id=1, source_target_pairs={{0,4},{4,0},{8,12},{12,8},{16,20},{20,16},{24,28},{28,24},{1,5},{5... | collective-permute-start | bytes 393224 | tf_op jit(solution)/shard_map/ppermute | solution.py:22
  3.0 3.5 %collective-permute-start.2 = (bf16[256,256]{1,0:T(8,128)(2,1)}, bf16[256,256]{1,0:T(8,128)(2,1)S(1)}, u32[]{:S(2)}, u32[]{:S(2)}) collective-permute-start(bf16[256,256]{1,0:T(8,128)(2,1)} %keys_in.1), channel_id=1, source_target_pairs={{0,8},{8,16},{16,0},{4,12},{12,20},{20,4},{24,24},{28,28},{1,9},{9... | collective-permute-start | bytes 393224 | tf_op jit(solution)/shard_map/ppermute | solution.py:22
  6.5 0.6 %collective-permute-start.1 = (bf16[256,256]{1,0:T(8,128)(2,1)}, bf16[256,256]{1,0:T(8,128)(2,1)S(1)}, u32[]{:S(2)}, u32[]{:S(2)}) collective-permute-start(bf16[256,256]{1,0:T(8,128)(2,1)} %values_in.1), channel_id=1, source_target_pairs={{0,4},{4,0},{8,12},{12,8},{16,20},{20,16},{24,28},{28,24},{1,5},{5... | collective-permute-start | bytes 393224 | tf_op jit(solution)/shard_map/ppermute | solution.py:22
  7.0 3.5 %collective-permute-start.3 = (bf16[256,256]{1,0:T(8,128)(2,1)}, bf16[256,256]{1,0:T(8,128)(2,1)S(1)}, u32[]{:S(2)}, u32[]{:S(2)}) collective-permute-start(bf16[256,256]{1,0:T(8,128)(2,1)} %values_in.1), channel_id=1, source_target_pairs={{0,8},{8,16},{16,0},{4,12},{12,20},{20,4},{24,24},{28,28},{1,9},{9... | collective-permute-start | bytes 393224 | tf_op jit(solution)/shard_map/ppermute | solution.py:22
  10.5 1.6 %attend_first.1 = (f32[1024,128]{1,0:T(8,128)S(1)}, f32[1024,128]{1,0:T(8,128)S(1)}, f32[1024,128]{1,0:T(8,128)S(1)}, bf16[256,512]{1,0:T(8,128)(2,1)S(1)}, f32[16,256]{1,0:T(8,128)S(1)}) custom-call(s32[16]{0:T(128)} %docs_in.1, bf16[256,512]{1,0:T(8,128)(2,1)} %queries_in.1, bf16[256,256]{1,0:T(8,128)(2,1)} %keys_in.1, bf16[256,256]{1,0:T(8,128)(2,1)} %values_in.1), custom_call_target="tpu_custom_call" | custom-call | flops 134217728 | tf_op jit(solution)/shard_map/attend_first/pallas_call | solution.py:192
  12.1 3.3 %collective-permute-start.4 = (bf16[256,256]{1,0:T(8,128)(2,1)}, bf16[256,256]{1,0:T(8,128)(2,1)S(1)}, u32[]{:S(2)}, u32[]{:S(2)}) collective-permute-start(bf16[256,256]{1,0:T(8,128)(2,1)} %keys_in.1), channel_id=1, source_target_pairs={{0,16},{16,0},{4,20},{20,4},{8,8},{12,12},{24,24},{28,28},{1,17},{... | collective-permute-start | bytes 393224 | tf_op jit(solution)/shard_map/ppermute | solution.py:22
  15.4 3.5 %collective-permute-start.5 = (bf16[256,256]{1,0:T(8,128)(2,1)}, bf16[256,256]{1,0:T(8,128)(2,1)S(1)}, u32[]{:S(2)}, u32[]{:S(2)}) collective-permute-start(bf16[256,256]{1,0:T(8,128)(2,1)} %values_in.1), channel_id=1, source_target_pairs={{0,16},{16,0},{4,20},{20,4},{8,8},{12,12},{24,24},{28,28},{1,17},{... | collective-permute-start | bytes 393224 | tf_op jit(solution)/shard_map/ppermute | solution.py:22
  18.9 1.6 %collective-permute-start.6 = (bf16[256,256]{1,0:T(8,128)(2,1)S(1)}, bf16[256,256]{1,0:T(8,128)(2,1)S(1)}, u32[]{:S(2)}, u32[]{:S(2)}) collective-permute-start(bf16[256,256]{1,0:T(8,128)(2,1)S(1)} %collective-permute-done.2.refs_5_), channel_id=1, source_target_pairs={{0,4},{4,0},{8,12},{12,8},{16,20},{20,16},{24,28},{28,24},{1,5},{5... | collective-permute-start | bytes 393224 | tf_op jit(solution)/shard_map/ppermute | solution.py:22
  20.5 0.5 collective-permute-start.7
  21.0 3.2 %collective-permute-start.8 = (bf16[256,256]{1,0:T(8,128)(2,1)S(1)}, bf16[256,256]{1,0:T(8,128)(2,1)S(1)}, u32[]{:S(2)}, u32[]{:S(2)}) collective-permute-start(bf16[256,256]{1,0:T(8,128)(2,1)S(1)} %collective-permute-done.refs_3_), channel_id=1, source_target_pairs={{0,16},{16,0},{4,20},{20,4},{8,8},{12,12},{24,24},{28,28},{1,17},{... | collective-permute-start | bytes 393224 | tf_op jit(solution)/shard_map/ppermute | solution.py:22
  24.3 3.5 %collective-permute-start.9 = (bf16[256,256]{1,0:T(8,128)(2,1)S(1)}, bf16[256,256]{1,0:T(8,128)(2,1)S(1)}, u32[]{:S(2)}, u32[]{:S(2)}) collective-permute-start(bf16[256,256]{1,0:T(8,128)(2,1)S(1)} %collective-permute-done.1.refs_4_), channel_id=1, source_target_pairs={{0,16},{16,0},{4,20},{20,4},{8,8},{12,12},{24,24},{28,28},{1,17},{... | collective-permute-start | bytes 393224 | tf_op jit(solution)/shard_map/ppermute | solution.py:22
  27.8 2.6 %attend_next.1 = (f32[1024,128]{1,0:T(8,128)S(1)}, f32[1024,128]{1,0:T(8,128)S(1)}, f32[1024,128]{1,0:T(8,128)S(1)}, bf16[512,5376]{1,0:T(8,128)(2,1)S(1)}) custom-call(bf16[256,512]{1,0:T(8,128)(2,1)S(1)} %get-tuple-element.34.queries, f32[16,256]{1,0:T(8,128)S(1)} %get-tuple-element.35.open_beside, bf16[512,5376]{1,0:T(8,128)(2,1)} %weight_in.1, ...), custom_call_target="tpu_custom_call" | custom-call | flops 402653184 | bytes 5505024 | tf_op jit(solution)/shard_map/attend_next/pallas_call | solution.py:214
  30.4 1.6 %collective-permute-done.9.refs_6_ = bf16[256,256]{1,0:T(8,128)(2,1)S(1)} collective-permute-done((bf16[256,256]{1,0:T(8,128)(2,1)S(1)}, bf16[256,256]{1,0:T(8,128)(2,1)S(1)}, u32[]{:S(2)}, u32[]{:S(2)}) %collective-permute-start.9) | collective-permute-done | bytes 131104 | tf_op jit(solution)/shard_map/ppermute | solution.py:22
  32.0 1.6 %attend_last.1 = (bf16[128,512]{1,0:T(8,128)(2,1)S(1)}, bf16[128,512]{1,0:T(8,128)(2,1)S(1)}, f32[64,3072]{1,0:T(8,128)S(1)}, bf16[64,3072]{1,0:T(8,128)(2,1)S(1)}) custom-call(bf16[256,512]{1,0:T(8,128)(2,1)S(1)} %get-tuple-element.34.queries, bf16[512,5376]{1,0:T(8,128)(2,1)S(1)} %get-tuple-element.43.weight, f32[1024,128]{1,0:T(8,128)S(1)} %get-tuple-element.44.refs_0_, ...), custom_call_target="tpu_custom_call" | custom-call | flops 268435456 | tf_op jit(solution)/shard_map/attend_last/pallas_call | solution.py:257
  33.6 0.1 collective-permute-start.10
  33.7 0.5 project.2
  34.2 0.6 %collective-permute-start.11 = (bf16[64,2304]{1,0:T(8,128)(2,1)S(1)}, bf16[64,2304]{1,0:T(8,128)(2,1)S(1)}, u32[]{:S(2)}, u32[]{:S(2)}) collective-permute-start(bf16[64,2304]{1,0:T(8,128)(2,1)S(1)} %get-tuple-element.57), channel_id=1, source_target_pairs={{0,1},{1,0},{2,3},{3,2},{4,5},{5,4},{6,7},{7,6},{8,9},{9,8},{10,11... | collective-permute-start | bytes 884744 | tf_op jit(solution)/shard_map/ppermute | solution.py:22
  34.8 0.7 %collective-permute-done.10.theirs = bf16[64,3072]{1,0:T(8,128)(2,1)S(1)} collective-permute-done((bf16[64,3072]{1,0:T(8,128)(2,1)S(1)}, bf16[64,3072]{1,0:T(8,128)(2,1)S(1)}, u32[]{:S(2)}, u32[]{:S(2)}) %collective-permute-start.10) | collective-permute-done | bytes 393248 | tf_op jit(solution)/shard_map/ppermute | solution.py:22
  35.4 0.1 add_up.2
  35.5 1.6 %collective-permute-start.16 = (bf16[64,3072]{1,0:T(8,128)(2,1)S(1)}, bf16[64,3072]{1,0:T(8,128)(2,1)S(1)}, u32[]{:S(2)}, u32[]{:S(2)}) collective-permute-start(bf16[64,3072]{1,0:T(8,128)(2,1)S(1)} %add_up.2), channel_id=1, source_target_pairs={{0,2},{1,3},{2,0},{3,1},{4,6},{5,7},{6,4},{7,5},{8,10},{9,11},{10,... | collective-permute-start | bytes 1179656 | tf_op jit(solution)/shard_map/ppermute | solution.py:22
  37.1 0.6 %collective-permute-start.12 = (bf16[64,2304]{1,0:T(8,128)(2,1)S(1)}, bf16[64,2304]{1,0:T(8,128)(2,1)S(1)}, u32[]{:S(2)}, u32[]{:S(2)}) collective-permute-start(bf16[64,2304]{1,0:T(8,128)(2,1)S(1)} %add_up.3), channel_id=1, source_target_pairs={{0,2},{1,3},{2,0},{3,1},{4,6},{5,7},{6,4},{7,5},{8,10},{9,11},{10,... | collective-permute-start | bytes 884744 | tf_op jit(solution)/shard_map/ppermute | solution.py:22
  37.7 0.9 %project.3 = (f32[64,5376]{1,0:T(8,128)S(1)}, bf16[64,1792]{1,0:T(8,128)(2,1)S(1)}, bf16[64,1792]{1,0:T(8,128)(2,1)S(1)}, bf16[64,1792]{1,0:T(8,128)(2,1)S(1)}) custom-call(bf16[128,512]{1,0:T(8,128)(2,1)S(1)} %get-tuple-element.58.rows, bf16[512,5376]{1,0:T(8,128)(2,1)S(1)} %get-tuple-element.43.weight), custom_call_target="tpu_custom_call" | custom-call | flops 704643072 | tf_op jit(solution)/shard_map/project/pallas_call | solution.py:292
  38.6 0.1 collective-permute-start.13
  38.7 0.5 collective-permute-start.14
  39.2 0.1 collective-permute-start.15
  39.3 0.9 %collective-permute-done.13.refs_0_ = bf16[64,1792]{1,0:T(8,128)(2,1)S(1)} collective-permute-done((bf16[64,1792]{1,0:T(8,128)(2,1)S(1)}, bf16[64,1792]{1,0:T(8,128)(2,1)S(1)}, u32[]{:S(2)}, u32[]{:S(2)}) %collective-permute-start.13) | collective-permute-done | bytes 229408 | tf_op jit(solution)/shard_map/ppermute | solution.py:22
  40.2 0.3 collective-permute-done.14.refs_1_
  40.5 0.3 collective-permute-done.15.refs_2_
  40.8 6.7 %collective-permute-done.16.across = bf16[64,3072]{1,0:T(8,128)(2,1)S(1)} collective-permute-done((bf16[64,3072]{1,0:T(8,128)(2,1)S(1)}, bf16[64,3072]{1,0:T(8,128)(2,1)S(1)}, u32[]{:S(2)}, u32[]{:S(2)}) %collective-permute-start.16) | collective-permute-done | bytes 393248 | tf_op jit(solution)/shard_map/ppermute | solution.py:22
  47.5 0.9 %combine.2.refs_3_ = bf16[64,5376]{1,0:T(8,128)(2,1)} custom-call(f32[64,5376]{1,0:T(8,128)S(1)} %get-tuple-element.59.mine, bf16[64,3072]{1,0:T(8,128)(2,1)S(1)} %collective-permute-done.16.across, bf16[64,1792]{1,0:T(8,128)(2,1)S(1)} %collective-permute-done.13.refs_0_, bf16[64,1792]{1,0:T(8,128)(2,1)S(1)} %collective-permute-done.14.refs_1_, ...), custom_call_target="tpu_custom_call" | custom-call | tf_op jit(solution)/shard_map/combine/pallas_call | solution.py:339
  48.4 4.6 %collective-permute-done.12.across = bf16[64,2304]{1,0:T(8,128)(2,1)S(1)} collective-permute-done((bf16[64,2304]{1,0:T(8,128)(2,1)S(1)}, bf16[64,2304]{1,0:T(8,128)(2,1)S(1)}, u32[]{:S(2)}, u32[]{:S(2)}) %collective-permute-start.12) | collective-permute-done | bytes 294944 | tf_op jit(solution)/shard_map/ppermute | solution.py:22
  53.0 0.8 %combine.3 = bf16[64,5376]{1,0:T(8,128)(2,1)} custom-call(f32[64,5376]{1,0:T(8,128)S(1)} %get-tuple-element.59.mine, bf16[64,2304]{1,0:T(8,128)(2,1)S(1)} %collective-permute-done.12.across, bf16[64,1792]{1,0:T(8,128)(2,1)S(1)} %collective-permute-done.13.refs_0_, ...), custom_call_target="tpu_custom_call", output_to_operand_aliasing={{}: (5, {})} | custom-call | tf_op jit(solution)/shard_map/combine/pallas_call | solution.py:339
  (11 shorter events, 0.1 us)
Async XLA Ops:
  0.0 12.1 %collective-permute-start = (bf16[256,256]{1,0:T(8,128)(2,1)}, bf16[256,256]{1,0:T(8,128)(2,1)S(1)}, u32[]{:S(2)}, u32[]{:S(2)}) collective-permute-start(bf16[256,256]{1,0:T(8,128)(2,1)} %keys_in.1), channel_id=1, source_target_pairs={{0,4},{4,0},{8,12},{12,8},{16,20},{20,16},{24,28},{28,24},{1,5},{5... | collective-permute-start | bytes 393224 | tf_op jit(solution)/shard_map/ppermute | solution.py:22
  3.0 15.9 %collective-permute-start.2 = (bf16[256,256]{1,0:T(8,128)(2,1)}, bf16[256,256]{1,0:T(8,128)(2,1)S(1)}, u32[]{:S(2)}, u32[]{:S(2)}) collective-permute-start(bf16[256,256]{1,0:T(8,128)(2,1)} %keys_in.1), channel_id=1, source_target_pairs={{0,8},{8,16},{16,0},{4,12},{12,20},{20,4},{24,24},{28,28},{1,9},{9... | collective-permute-start | bytes 393224 | tf_op jit(solution)/shard_map/ppermute | solution.py:22
  6.5 14.6 %collective-permute-start.1 = (bf16[256,256]{1,0:T(8,128)(2,1)}, bf16[256,256]{1,0:T(8,128)(2,1)S(1)}, u32[]{:S(2)}, u32[]{:S(2)}) collective-permute-start(bf16[256,256]{1,0:T(8,128)(2,1)} %values_in.1), channel_id=1, source_target_pairs={{0,4},{4,0},{8,12},{12,8},{16,20},{20,16},{24,28},{28,24},{1,5},{5... | collective-permute-start | bytes 393224 | tf_op jit(solution)/shard_map/ppermute | solution.py:22
  7.0 13.5 %collective-permute-start.3 = (bf16[256,256]{1,0:T(8,128)(2,1)}, bf16[256,256]{1,0:T(8,128)(2,1)S(1)}, u32[]{:S(2)}, u32[]{:S(2)}) collective-permute-start(bf16[256,256]{1,0:T(8,128)(2,1)} %values_in.1), channel_id=1, source_target_pairs={{0,8},{8,16},{16,0},{4,12},{12,20},{20,4},{24,24},{28,28},{1,9},{9... | collective-permute-start | bytes 393224 | tf_op jit(solution)/shard_map/ppermute | solution.py:22
  12.1 12.1 %collective-permute-start.4 = (bf16[256,256]{1,0:T(8,128)(2,1)}, bf16[256,256]{1,0:T(8,128)(2,1)S(1)}, u32[]{:S(2)}, u32[]{:S(2)}) collective-permute-start(bf16[256,256]{1,0:T(8,128)(2,1)} %keys_in.1), channel_id=1, source_target_pairs={{0,16},{16,0},{4,20},{20,4},{8,8},{12,12},{24,24},{28,28},{1,17},{... | collective-permute-start | bytes 393224 | tf_op jit(solution)/shard_map/ppermute | solution.py:22
  15.4 12.4 %collective-permute-start.5 = (bf16[256,256]{1,0:T(8,128)(2,1)}, bf16[256,256]{1,0:T(8,128)(2,1)S(1)}, u32[]{:S(2)}, u32[]{:S(2)}) collective-permute-start(bf16[256,256]{1,0:T(8,128)(2,1)} %values_in.1), channel_id=1, source_target_pairs={{0,16},{16,0},{4,20},{20,4},{8,8},{12,12},{24,24},{28,28},{1,17},{... | collective-permute-start | bytes 393224 | tf_op jit(solution)/shard_map/ppermute | solution.py:22
  18.9 11.5 %collective-permute-start.6 = (bf16[256,256]{1,0:T(8,128)(2,1)S(1)}, bf16[256,256]{1,0:T(8,128)(2,1)S(1)}, u32[]{:S(2)}, u32[]{:S(2)}) collective-permute-start(bf16[256,256]{1,0:T(8,128)(2,1)S(1)} %collective-permute-done.2.refs_5_), channel_id=1, source_target_pairs={{0,4},{4,0},{8,12},{12,8},{16,20},{20,16},{24,28},{28,24},{1,5},{5... | collective-permute-start | bytes 393224 | tf_op jit(solution)/shard_map/ppermute | solution.py:22
  20.5 9.9 %collective-permute-start.7 = (bf16[256,256]{1,0:T(8,128)(2,1)S(1)}, bf16[256,256]{1,0:T(8,128)(2,1)S(1)}, u32[]{:S(2)}, u32[]{:S(2)}) collective-permute-start(bf16[256,256]{1,0:T(8,128)(2,1)S(1)} %collective-permute-done.3.refs_6_), channel_id=1, source_target_pairs={{0,4},{4,0},{8,12},{12,8},{16,20},{20,16},{24,28},{28,24},{1,5},{5... | collective-permute-start | bytes 393224 | tf_op jit(solution)/shard_map/ppermute | solution.py:22
  21.0 9.4 %collective-permute-start.8 = (bf16[256,256]{1,0:T(8,128)(2,1)S(1)}, bf16[256,256]{1,0:T(8,128)(2,1)S(1)}, u32[]{:S(2)}, u32[]{:S(2)}) collective-permute-start(bf16[256,256]{1,0:T(8,128)(2,1)S(1)} %collective-permute-done.refs_3_), channel_id=1, source_target_pairs={{0,16},{16,0},{4,20},{20,4},{8,8},{12,12},{24,24},{28,28},{1,17},{... | collective-permute-start | bytes 393224 | tf_op jit(solution)/shard_map/ppermute | solution.py:22
  24.3 7.8 %collective-permute-start.9 = (bf16[256,256]{1,0:T(8,128)(2,1)S(1)}, bf16[256,256]{1,0:T(8,128)(2,1)S(1)}, u32[]{:S(2)}, u32[]{:S(2)}) collective-permute-start(bf16[256,256]{1,0:T(8,128)(2,1)S(1)} %collective-permute-done.1.refs_4_), channel_id=1, source_target_pairs={{0,16},{16,0},{4,20},{20,4},{8,8},{12,12},{24,24},{28,28},{1,17},{... | collective-permute-start | bytes 393224 | tf_op jit(solution)/shard_map/ppermute | solution.py:22
  33.6 1.8 %collective-permute-start.10 = (bf16[64,3072]{1,0:T(8,128)(2,1)S(1)}, bf16[64,3072]{1,0:T(8,128)(2,1)S(1)}, u32[]{:S(2)}, u32[]{:S(2)}) collective-permute-start(bf16[64,3072]{1,0:T(8,128)(2,1)S(1)} %get-tuple-element.55), channel_id=1, source_target_pairs={{0,1},{1,0},{2,3},{3,2},{4,5},{5,4},{6,7},{7,6},{8,9},{9,8},{10,11... | collective-permute-start | bytes 1179656 | tf_op jit(solution)/shard_map/ppermute | solution.py:22
  34.2 2.9 %collective-permute-start.11 = (bf16[64,2304]{1,0:T(8,128)(2,1)S(1)}, bf16[64,2304]{1,0:T(8,128)(2,1)S(1)}, u32[]{:S(2)}, u32[]{:S(2)}) collective-permute-start(bf16[64,2304]{1,0:T(8,128)(2,1)S(1)} %get-tuple-element.57), channel_id=1, source_target_pairs={{0,1},{1,0},{2,3},{3,2},{4,5},{5,4},{6,7},{7,6},{8,9},{9,8},{10,11... | collective-permute-start | bytes 884744 | tf_op jit(solution)/shard_map/ppermute | solution.py:22
  35.5 12.0 %collective-permute-start.16 = (bf16[64,3072]{1,0:T(8,128)(2,1)S(1)}, bf16[64,3072]{1,0:T(8,128)(2,1)S(1)}, u32[]{:S(2)}, u32[]{:S(2)}) collective-permute-start(bf16[64,3072]{1,0:T(8,128)(2,1)S(1)} %add_up.2), channel_id=1, source_target_pairs={{0,2},{1,3},{2,0},{3,1},{4,6},{5,7},{6,4},{7,5},{8,10},{9,11},{10,... | collective-permute-start | bytes 1179656 | tf_op jit(solution)/shard_map/ppermute | solution.py:22
  37.1 15.9 %collective-permute-start.12 = (bf16[64,2304]{1,0:T(8,128)(2,1)S(1)}, bf16[64,2304]{1,0:T(8,128)(2,1)S(1)}, u32[]{:S(2)}, u32[]{:S(2)}) collective-permute-start(bf16[64,2304]{1,0:T(8,128)(2,1)S(1)} %add_up.3), channel_id=1, source_target_pairs={{0,2},{1,3},{2,0},{3,1},{4,6},{5,7},{6,4},{7,5},{8,10},{9,11},{10,... | collective-permute-start | bytes 884744 | tf_op jit(solution)/shard_map/ppermute | solution.py:22
  38.6 1.6 %collective-permute-start.13 = (bf16[64,1792]{1,0:T(8,128)(2,1)S(1)}, bf16[64,1792]{1,0:T(8,128)(2,1)S(1)}, u32[]{:S(2)}, u32[]{:S(2)}) collective-permute-start(bf16[64,1792]{1,0:T(8,128)(2,1)S(1)} %get-tuple-element.60), channel_id=1, source_target_pairs={{0,1},{1,0},{2,3},{3,2},{4,5},{5,4},{6,7},{7,6},{8,9},{9,8},{10,11... | collective-permute-start | bytes 688136 | tf_op jit(solution)/shard_map/ppermute | solution.py:22
  38.7 1.8 %collective-permute-start.14 = (bf16[64,1792]{1,0:T(8,128)(2,1)S(1)}, bf16[64,1792]{1,0:T(8,128)(2,1)S(1)}, u32[]{:S(2)}, u32[]{:S(2)}) collective-permute-start(bf16[64,1792]{1,0:T(8,128)(2,1)S(1)} %get-tuple-element.61), channel_id=1, source_target_pairs={{0,1},{1,0},{2,3},{3,2},{4,5},{5,4},{6,7},{7,6},{8,9},{9,8},{10,11... | collective-permute-start | bytes 688136 | tf_op jit(solution)/shard_map/ppermute | solution.py:22
  39.2 1.6 %collective-permute-start.15 = (bf16[64,1792]{1,0:T(8,128)(2,1)S(1)}, bf16[64,1792]{1,0:T(8,128)(2,1)S(1)}, u32[]{:S(2)}, u32[]{:S(2)}) collective-permute-start(bf16[64,1792]{1,0:T(8,128)(2,1)S(1)} %get-tuple-element.62), channel_id=1, source_target_pairs={{0,1},{1,0},{2,3},{3,2},{4,5},{5,4},{6,7},{7,6},{8,9},{9,8},{10,11... | collective-permute-start | bytes 688136 | tf_op jit(solution)/shard_map/ppermute | solution.py:22

commit v5 on v4

--- a/solution.py
+++ b/solution.py
@@ -28,8 +28,8 @@
 
 
 BESIDE = ((0, 1), (2, 3), (4, 5), (6, 7))
-BY_TWO = ((0, 2, 4), (1, 3, 5), (6,), (7,))
-BY_FOUR = ((0, 4), (1, 5), (2,), (3,), (6,), (7,))
+BY_TWO = ((0, 2, 4, 6), (1, 3, 5, 7))
+BY_FOUR = ((0, 4, 6, 2), (1, 5, 7, 3))
 
 
 def after(x, event):

time: 54.2 us -> 49.7 us (0.917)
  starting transfers between devices: 29.5 us -> 24.4 us
  waiting for transfers between devices: 15.2 us -> 16 us
    ppermute x17, starting transfers between devices: 29.5 us -> 24.4 us  [hop(): return lax.ppermute(block, axis, pairs)]
    ppermute x17, waiting for transfers between devices: 15.2 us -> 16 us  [hop(): return lax.ppermute(block, axis, pairs)]
  transfers between devices with their start and end apart: 17 -> 17, of which waited for: 7 -> 8; matrix products, arithmetic and copies ran while one was open for 0% -> 0% of each run, Pallas kernels for 12% -> 13%
where the time goes in v5:
time: 49.7 us; the launch traced here: 49.6 us
  starting transfers between devices  24.4 us (49%)
  waiting for transfers between devices  16 us (32%)
  Pallas kernels  8.96 us (18%)
    ppermute x17, starting transfers between devices, hop(): return lax.ppermute(block, axis, pairs)  24.4 us
    ppermute x17, waiting for transfers between devices, hop(): return lax.ppermute(block, axis, pairs)  16 us
    pallas_call x1, Pallas kernels, attend_next(): pl.pallas_call(functools.partial(next_kernel, numbers), out_shape=state_s...  2.59 us
    pallas_call x2, Pallas kernels, combine(): pl.pallas_call(functools.partial(combine_kernel, at), out_shape=jax.Shape...  1.68 us
    pallas_call x1, Pallas kernels, attend_last(): pl.pallas_call(functools.partial(last_kernel, numbers, columns), out_shap...  1.6 us
    pallas_call x1, Pallas kernels, attend_first(): pl.pallas_call(first_kernel, out_shape=state_shapes(queries) + (pltpu.VME...  1.6 us
    pallas_call x2, Pallas kernels, project(): pl.pallas_call(functools.partial(project_kernel, columns), out_shape=proj...  1.36 us
  transfers between devices with their start and end apart: 17, of which 8 were waited for; matrix products, arithmetic and copies ran while one was open for 0% of the time, Pallas kernels for 13%

profile of v5, /device:TPU:0, one launch (start us, length us, event | category | flops | bytes accessed | tf_op | source)
XLA Modules:
  0.0 49.6 jit_solution(7882424140869773467)
XLA Ops:
  0.0 3.0 %collective-permute-start = (bf16[256,256]{1,0:T(8,128)(2,1)}, bf16[256,256]{1,0:T(8,128)(2,1)S(1)}, u32[]{:S(2)}, u32[]{:S(2)}) collective-permute-start(bf16[256,256]{1,0:T(8,128)(2,1)} %keys_in.1), channel_id=1, source_target_pairs={{0,4},{4,0},{8,12},{12,8},{16,20},{20,16},{24,28},{28,24},{1,5},{5... | collective-permute-start | bytes 393224 | tf_op jit(solution)/shard_map/ppermute | solution.py:22
  3.0 1.6 %collective-permute-start.2 = (bf16[256,256]{1,0:T(8,128)(2,1)}, bf16[256,256]{1,0:T(8,128)(2,1)S(1)}, u32[]{:S(2)}, u32[]{:S(2)}) collective-permute-start(bf16[256,256]{1,0:T(8,128)(2,1)} %keys_in.1), channel_id=1, source_target_pairs={{0,8},{8,16},{16,24},{24,0},{4,12},{12,20},{20,28},{28,4},{1,9},{9... | collective-permute-start | bytes 393224 | tf_op jit(solution)/shard_map/ppermute | solution.py:22
  4.5 0.5 %collective-permute-start.1 = (bf16[256,256]{1,0:T(8,128)(2,1)}, bf16[256,256]{1,0:T(8,128)(2,1)S(1)}, u32[]{:S(2)}, u32[]{:S(2)}) collective-permute-start(bf16[256,256]{1,0:T(8,128)(2,1)} %values_in.1), channel_id=1, source_target_pairs={{0,4},{4,0},{8,12},{12,8},{16,20},{20,16},{24,28},{28,24},{1,5},{5... | collective-permute-start | bytes 393224 | tf_op jit(solution)/shard_map/ppermute | solution.py:22
  5.1 1.6 %collective-permute-start.3 = (bf16[256,256]{1,0:T(8,128)(2,1)}, bf16[256,256]{1,0:T(8,128)(2,1)S(1)}, u32[]{:S(2)}, u32[]{:S(2)}) collective-permute-start(bf16[256,256]{1,0:T(8,128)(2,1)} %values_in.1), channel_id=1, source_target_pairs={{0,8},{8,16},{16,24},{24,0},{4,12},{12,20},{20,28},{28,4},{1,9},{9... | collective-permute-start | bytes 393224 | tf_op jit(solution)/shard_map/ppermute | solution.py:22
  6.6 1.6 %attend_first.1 = (f32[1024,128]{1,0:T(8,128)S(1)}, f32[1024,128]{1,0:T(8,128)S(1)}, f32[1024,128]{1,0:T(8,128)S(1)}, bf16[256,512]{1,0:T(8,128)(2,1)S(1)}, f32[16,256]{1,0:T(8,128)S(1)}) custom-call(s32[16]{0:T(128)} %docs_in.1, bf16[256,512]{1,0:T(8,128)(2,1)} %queries_in.1, bf16[256,256]{1,0:T(8,128)(2,1)} %keys_in.1, bf16[256,256]{1,0:T(8,128)(2,1)} %values_in.1), custom_call_target="tpu_custom_call" | custom-call | flops 134217728 | tf_op jit(solution)/shard_map/attend_first/pallas_call | solution.py:192
  8.2 1.5 %collective-permute-start.4 = (bf16[256,256]{1,0:T(8,128)(2,1)}, bf16[256,256]{1,0:T(8,128)(2,1)S(1)}, u32[]{:S(2)}, u32[]{:S(2)}) collective-permute-start(bf16[256,256]{1,0:T(8,128)(2,1)} %keys_in.1), channel_id=1, source_target_pairs={{0,16},{16,24},{24,8},{8,0},{4,20},{20,28},{28,12},{12,4},{1,17},{... | collective-permute-start | bytes 393224 | tf_op jit(solution)/shard_map/ppermute | solution.py:22
  9.8 2.4 %collective-permute-start.5 = (bf16[256,256]{1,0:T(8,128)(2,1)}, bf16[256,256]{1,0:T(8,128)(2,1)S(1)}, u32[]{:S(2)}, u32[]{:S(2)}) collective-permute-start(bf16[256,256]{1,0:T(8,128)(2,1)} %values_in.1), channel_id=1, source_target_pairs={{0,16},{16,24},{24,8},{8,0},{4,20},{20,28},{28,12},{12,4},{1,17},{... | collective-permute-start | bytes 393224 | tf_op jit(solution)/shard_map/ppermute | solution.py:22
  12.2 1.5 %collective-permute-start.6 = (bf16[256,256]{1,0:T(8,128)(2,1)S(1)}, bf16[256,256]{1,0:T(8,128)(2,1)S(1)}, u32[]{:S(2)}, u32[]{:S(2)}) collective-permute-start(bf16[256,256]{1,0:T(8,128)(2,1)S(1)} %collective-permute-done.2.refs_5_), channel_id=1, source_target_pairs={{0,4},{4,0},{8,12},{12,8},{16,20},{20,16},{24,28},{28,24},{1,5},{5... | collective-permute-start | bytes 393224 | tf_op jit(solution)/shard_map/ppermute | solution.py:22
  13.7 0.2 collective-permute-done.3.refs_6_
  13.9 0.3 collective-permute-start.7
  14.2 8.5 %collective-permute-start.8 = (bf16[256,256]{1,0:T(8,128)(2,1)S(1)}, bf16[256,256]{1,0:T(8,128)(2,1)S(1)}, u32[]{:S(2)}, u32[]{:S(2)}) collective-permute-start(bf16[256,256]{1,0:T(8,128)(2,1)S(1)} %collective-permute-done.refs_3_), channel_id=1, source_target_pairs={{0,16},{16,24},{24,8},{8,0},{4,20},{20,28},{28,12},{12,4},{1,17},{... | collective-permute-start | bytes 393224 | tf_op jit(solution)/shard_map/ppermute | solution.py:22
  22.8 2.6 %attend_next.1 = (f32[1024,128]{1,0:T(8,128)S(1)}, f32[1024,128]{1,0:T(8,128)S(1)}, f32[1024,128]{1,0:T(8,128)S(1)}, bf16[512,5376]{1,0:T(8,128)(2,1)S(1)}) custom-call(bf16[256,512]{1,0:T(8,128)(2,1)S(1)} %get-tuple-element.34.queries, f32[16,256]{1,0:T(8,128)S(1)} %get-tuple-element.35.open_beside, bf16[512,5376]{1,0:T(8,128)(2,1)} %weight_in.1, ...), custom_call_target="tpu_custom_call" | custom-call | flops 402653184 | bytes 5505024 | tf_op jit(solution)/shard_map/attend_next/pallas_call | solution.py:214
  25.5 2.3 %collective-permute-done.9.refs_6_ = bf16[256,256]{1,0:T(8,128)(2,1)S(1)} collective-permute-done((bf16[256,256]{1,0:T(8,128)(2,1)S(1)}, bf16[256,256]{1,0:T(8,128)(2,1)S(1)}, u32[]{:S(2)}, u32[]{:S(2)}) %collective-permute-start.9) | collective-permute-done | bytes 131104 | tf_op jit(solution)/shard_map/ppermute | solution.py:22
  27.7 1.6 %attend_last.1 = (bf16[128,512]{1,0:T(8,128)(2,1)S(1)}, bf16[128,512]{1,0:T(8,128)(2,1)S(1)}, f32[64,3072]{1,0:T(8,128)S(1)}, bf16[64,3072]{1,0:T(8,128)(2,1)S(1)}) custom-call(bf16[256,512]{1,0:T(8,128)(2,1)S(1)} %get-tuple-element.34.queries, bf16[512,5376]{1,0:T(8,128)(2,1)S(1)} %get-tuple-element.43.weight, f32[1024,128]{1,0:T(8,128)S(1)} %get-tuple-element.44.refs_0_, ...), custom_call_target="tpu_custom_call" | custom-call | flops 268435456 | tf_op jit(solution)/shard_map/attend_last/pallas_call | solution.py:257
  29.4 0.1 collective-permute-start.10
  29.4 0.5 project.2
  29.9 0.6 %collective-permute-start.11 = (bf16[64,2304]{1,0:T(8,128)(2,1)S(1)}, bf16[64,2304]{1,0:T(8,128)(2,1)S(1)}, u32[]{:S(2)}, u32[]{:S(2)}) collective-permute-start(bf16[64,2304]{1,0:T(8,128)(2,1)S(1)} %get-tuple-element.57), channel_id=1, source_target_pairs={{0,1},{1,0},{2,3},{3,2},{4,5},{5,4},{6,7},{7,6},{8,9},{9,8},{10,11... | collective-permute-start | bytes 884744 | tf_op jit(solution)/shard_map/ppermute | solution.py:22
  30.5 0.7 %collective-permute-done.10.theirs = bf16[64,3072]{1,0:T(8,128)(2,1)S(1)} collective-permute-done((bf16[64,3072]{1,0:T(8,128)(2,1)S(1)}, bf16[64,3072]{1,0:T(8,128)(2,1)S(1)}, u32[]{:S(2)}, u32[]{:S(2)}) %collective-permute-start.10) | collective-permute-done | bytes 393248 | tf_op jit(solution)/shard_map/ppermute | solution.py:22
  31.1 0.1 add_up.2
  31.2 1.6 %collective-permute-start.16 = (bf16[64,3072]{1,0:T(8,128)(2,1)S(1)}, bf16[64,3072]{1,0:T(8,128)(2,1)S(1)}, u32[]{:S(2)}, u32[]{:S(2)}) collective-permute-start(bf16[64,3072]{1,0:T(8,128)(2,1)S(1)} %add_up.2), channel_id=1, source_target_pairs={{0,2},{1,3},{2,0},{3,1},{4,6},{5,7},{6,4},{7,5},{8,10},{9,11},{10,... | collective-permute-start | bytes 1179656 | tf_op jit(solution)/shard_map/ppermute | solution.py:22
  32.8 0.6 %collective-permute-start.12 = (bf16[64,2304]{1,0:T(8,128)(2,1)S(1)}, bf16[64,2304]{1,0:T(8,128)(2,1)S(1)}, u32[]{:S(2)}, u32[]{:S(2)}) collective-permute-start(bf16[64,2304]{1,0:T(8,128)(2,1)S(1)} %add_up.3), channel_id=1, source_target_pairs={{0,2},{1,3},{2,0},{3,1},{4,6},{5,7},{6,4},{7,5},{8,10},{9,11},{10,... | collective-permute-start | bytes 884744 | tf_op jit(solution)/shard_map/ppermute | solution.py:22
  33.4 0.9 %project.3 = (f32[64,5376]{1,0:T(8,128)S(1)}, bf16[64,1792]{1,0:T(8,128)(2,1)S(1)}, bf16[64,1792]{1,0:T(8,128)(2,1)S(1)}, bf16[64,1792]{1,0:T(8,128)(2,1)S(1)}) custom-call(bf16[128,512]{1,0:T(8,128)(2,1)S(1)} %get-tuple-element.58.rows, bf16[512,5376]{1,0:T(8,128)(2,1)S(1)} %get-tuple-element.43.weight), custom_call_target="tpu_custom_call" | custom-call | flops 704643072 | tf_op jit(solution)/shard_map/project/pallas_call | solution.py:292
  34.3 0.1 collective-permute-start.13
  34.4 0.5 %collective-permute-start.14 = (bf16[64,1792]{1,0:T(8,128)(2,1)S(1)}, bf16[64,1792]{1,0:T(8,128)(2,1)S(1)}, u32[]{:S(2)}, u32[]{:S(2)}) collective-permute-start(bf16[64,1792]{1,0:T(8,128)(2,1)S(1)} %get-tuple-element.61), channel_id=1, source_target_pairs={{0,1},{1,0},{2,3},{3,2},{4,5},{5,4},{6,7},{7,6},{8,9},{9,8},{10,11... | collective-permute-start | bytes 688136 | tf_op jit(solution)/shard_map/ppermute | solution.py:22
  34.9 0.1 collective-permute-start.15
  35.0 0.9 %collective-permute-done.13.refs_0_ = bf16[64,1792]{1,0:T(8,128)(2,1)S(1)} collective-permute-done((bf16[64,1792]{1,0:T(8,128)(2,1)S(1)}, bf16[64,1792]{1,0:T(8,128)(2,1)S(1)}, u32[]{:S(2)}, u32[]{:S(2)}) %collective-permute-start.13) | collective-permute-done | bytes 229408 | tf_op jit(solution)/shard_map/ppermute | solution.py:22
  35.9 0.3 collective-permute-done.14.refs_1_
  36.2 0.3 collective-permute-done.15.refs_2_
  36.5 6.7 %collective-permute-done.16.across = bf16[64,3072]{1,0:T(8,128)(2,1)S(1)} collective-permute-done((bf16[64,3072]{1,0:T(8,128)(2,1)S(1)}, bf16[64,3072]{1,0:T(8,128)(2,1)S(1)}, u32[]{:S(2)}, u32[]{:S(2)}) %collective-permute-start.16) | collective-permute-done | bytes 393248 | tf_op jit(solution)/shard_map/ppermute | solution.py:22
  43.2 0.9 %combine.2.refs_3_ = bf16[64,5376]{1,0:T(8,128)(2,1)} custom-call(f32[64,5376]{1,0:T(8,128)S(1)} %get-tuple-element.59.mine, bf16[64,3072]{1,0:T(8,128)(2,1)S(1)} %collective-permute-done.16.across, bf16[64,1792]{1,0:T(8,128)(2,1)S(1)} %collective-permute-done.13.refs_0_, bf16[64,1792]{1,0:T(8,128)(2,1)S(1)} %collective-permute-done.14.refs_1_, ...), custom_call_target="tpu_custom_call" | custom-call | tf_op jit(solution)/shard_map/combine/pallas_call | solution.py:339
  44.1 4.6 %collective-permute-done.12.across = bf16[64,2304]{1,0:T(8,128)(2,1)S(1)} collective-permute-done((bf16[64,2304]{1,0:T(8,128)(2,1)S(1)}, bf16[64,2304]{1,0:T(8,128)(2,1)S(1)}, u32[]{:S(2)}, u32[]{:S(2)}) %collective-permute-start.12) | collective-permute-done | bytes 294944 | tf_op jit(solution)/shard_map/ppermute | solution.py:22
  48.8 0.8 %combine.3 = bf16[64,5376]{1,0:T(8,128)(2,1)} custom-call(f32[64,5376]{1,0:T(8,128)S(1)} %get-tuple-element.59.mine, bf16[64,2304]{1,0:T(8,128)(2,1)S(1)} %collective-permute-done.12.across, bf16[64,1792]{1,0:T(8,128)(2,1)S(1)} %collective-permute-done.13.refs_0_, ...), custom_call_target="tpu_custom_call", output_to_operand_aliasing={{}: (5, {})} | custom-call | tf_op jit(solution)/shard_map/combine/pallas_call | solution.py:339
  (11 shorter events, 0.1 us)
Async XLA Ops:
  0.0 8.2 %collective-permute-start = (bf16[256,256]{1,0:T(8,128)(2,1)}, bf16[256,256]{1,0:T(8,128)(2,1)S(1)}, u32[]{:S(2)}, u32[]{:S(2)}) collective-permute-start(bf16[256,256]{1,0:T(8,128)(2,1)} %keys_in.1), channel_id=1, source_target_pairs={{0,4},{4,0},{8,12},{12,8},{16,20},{20,16},{24,28},{28,24},{1,5},{5... | collective-permute-start | bytes 393224 | tf_op jit(solution)/shard_map/ppermute | solution.py:22
  3.0 9.2 %collective-permute-start.2 = (bf16[256,256]{1,0:T(8,128)(2,1)}, bf16[256,256]{1,0:T(8,128)(2,1)S(1)}, u32[]{:S(2)}, u32[]{:S(2)}) collective-permute-start(bf16[256,256]{1,0:T(8,128)(2,1)} %keys_in.1), channel_id=1, source_target_pairs={{0,8},{8,16},{16,24},{24,0},{4,12},{12,20},{20,28},{28,4},{1,9},{9... | collective-permute-start | bytes 393224 | tf_op jit(solution)/shard_map/ppermute | solution.py:22
  4.5 9.7 %collective-permute-start.1 = (bf16[256,256]{1,0:T(8,128)(2,1)}, bf16[256,256]{1,0:T(8,128)(2,1)S(1)}, u32[]{:S(2)}, u32[]{:S(2)}) collective-permute-start(bf16[256,256]{1,0:T(8,128)(2,1)} %values_in.1), channel_id=1, source_target_pairs={{0,4},{4,0},{8,12},{12,8},{16,20},{20,16},{24,28},{28,24},{1,5},{5... | collective-permute-start | bytes 393224 | tf_op jit(solution)/shard_map/ppermute | solution.py:22
  5.1 8.9 %collective-permute-start.3 = (bf16[256,256]{1,0:T(8,128)(2,1)}, bf16[256,256]{1,0:T(8,128)(2,1)S(1)}, u32[]{:S(2)}, u32[]{:S(2)}) collective-permute-start(bf16[256,256]{1,0:T(8,128)(2,1)} %values_in.1), channel_id=1, source_target_pairs={{0,8},{8,16},{16,24},{24,0},{4,12},{12,20},{20,28},{28,4},{1,9},{9... | collective-permute-start | bytes 393224 | tf_op jit(solution)/shard_map/ppermute | solution.py:22
  8.2 14.5 %collective-permute-start.4 = (bf16[256,256]{1,0:T(8,128)(2,1)}, bf16[256,256]{1,0:T(8,128)(2,1)S(1)}, u32[]{:S(2)}, u32[]{:S(2)}) collective-permute-start(bf16[256,256]{1,0:T(8,128)(2,1)} %keys_in.1), channel_id=1, source_target_pairs={{0,16},{16,24},{24,8},{8,0},{4,20},{20,28},{28,12},{12,4},{1,17},{... | collective-permute-start | bytes 393224 | tf_op jit(solution)/shard_map/ppermute | solution.py:22
  9.8 13.1 %collective-permute-start.5 = (bf16[256,256]{1,0:T(8,128)(2,1)}, bf16[256,256]{1,0:T(8,128)(2,1)S(1)}, u32[]{:S(2)}, u32[]{:S(2)}) collective-permute-start(bf16[256,256]{1,0:T(8,128)(2,1)} %values_in.1), channel_id=1, source_target_pairs={{0,16},{16,24},{24,8},{8,0},{4,20},{20,28},{28,12},{12,4},{1,17},{... | collective-permute-start | bytes 393224 | tf_op jit(solution)/shard_map/ppermute | solution.py:22
  12.2 13.2 %collective-permute-start.6 = (bf16[256,256]{1,0:T(8,128)(2,1)S(1)}, bf16[256,256]{1,0:T(8,128)(2,1)S(1)}, u32[]{:S(2)}, u32[]{:S(2)}) collective-permute-start(bf16[256,256]{1,0:T(8,128)(2,1)S(1)} %collective-permute-done.2.refs_5_), channel_id=1, source_target_pairs={{0,4},{4,0},{8,12},{12,8},{16,20},{20,16},{24,28},{28,24},{1,5},{5... | collective-permute-start | bytes 393224 | tf_op jit(solution)/shard_map/ppermute | solution.py:22
  13.9 11.5 %collective-permute-start.7 = (bf16[256,256]{1,0:T(8,128)(2,1)S(1)}, bf16[256,256]{1,0:T(8,128)(2,1)S(1)}, u32[]{:S(2)}, u32[]{:S(2)}) collective-permute-start(bf16[256,256]{1,0:T(8,128)(2,1)S(1)} %collective-permute-done.3.refs_6_), channel_id=1, source_target_pairs={{0,4},{4,0},{8,12},{12,8},{16,20},{20,16},{24,28},{28,24},{1,5},{5... | collective-permute-start | bytes 393224 | tf_op jit(solution)/shard_map/ppermute | solution.py:22
  14.2 11.2 %collective-permute-start.8 = (bf16[256,256]{1,0:T(8,128)(2,1)S(1)}, bf16[256,256]{1,0:T(8,128)(2,1)S(1)}, u32[]{:S(2)}, u32[]{:S(2)}) collective-permute-start(bf16[256,256]{1,0:T(8,128)(2,1)S(1)} %collective-permute-done.refs_3_), channel_id=1, source_target_pairs={{0,16},{16,24},{24,8},{8,0},{4,20},{20,28},{28,12},{12,4},{1,17},{... | collective-permute-start | bytes 393224 | tf_op jit(solution)/shard_map/ppermute | solution.py:22
  22.8 5.0 %collective-permute-start.9 = (bf16[256,256]{1,0:T(8,128)(2,1)S(1)}, bf16[256,256]{1,0:T(8,128)(2,1)S(1)}, u32[]{:S(2)}, u32[]{:S(2)}) collective-permute-start(bf16[256,256]{1,0:T(8,128)(2,1)S(1)} %collective-permute-done.1.refs_4_), channel_id=1, source_target_pairs={{0,16},{16,24},{24,8},{8,0},{4,20},{20,28},{28,12},{12,4},{1,17},{... | collective-permute-start | bytes 393224 | tf_op jit(solution)/shard_map/ppermute | solution.py:22
  29.4 1.8 %collective-permute-start.10 = (bf16[64,3072]{1,0:T(8,128)(2,1)S(1)}, bf16[64,3072]{1,0:T(8,128)(2,1)S(1)}, u32[]{:S(2)}, u32[]{:S(2)}) collective-permute-start(bf16[64,3072]{1,0:T(8,128)(2,1)S(1)} %get-tuple-element.55), channel_id=1, source_target_pairs={{0,1},{1,0},{2,3},{3,2},{4,5},{5,4},{6,7},{7,6},{8,9},{9,8},{10,11... | collective-permute-start | bytes 1179656 | tf_op jit(solution)/shard_map/ppermute | solution.py:22
  29.9 2.9 %collective-permute-start.11 = (bf16[64,2304]{1,0:T(8,128)(2,1)S(1)}, bf16[64,2304]{1,0:T(8,128)(2,1)S(1)}, u32[]{:S(2)}, u32[]{:S(2)}) collective-permute-start(bf16[64,2304]{1,0:T(8,128)(2,1)S(1)} %get-tuple-element.57), channel_id=1, source_target_pairs={{0,1},{1,0},{2,3},{3,2},{4,5},{5,4},{6,7},{7,6},{8,9},{9,8},{10,11... | collective-permute-start | bytes 884744 | tf_op jit(solution)/shard_map/ppermute | solution.py:22
  31.2 12.0 %collective-permute-start.16 = (bf16[64,3072]{1,0:T(8,128)(2,1)S(1)}, bf16[64,3072]{1,0:T(8,128)(2,1)S(1)}, u32[]{:S(2)}, u32[]{:S(2)}) collective-permute-start(bf16[64,3072]{1,0:T(8,128)(2,1)S(1)} %add_up.2), channel_id=1, source_target_pairs={{0,2},{1,3},{2,0},{3,1},{4,6},{5,7},{6,4},{7,5},{8,10},{9,11},{10,... | collective-permute-start | bytes 1179656 | tf_op jit(solution)/shard_map/ppermute | solution.py:22
  32.8 15.9 %collective-permute-start.12 = (bf16[64,2304]{1,0:T(8,128)(2,1)S(1)}, bf16[64,2304]{1,0:T(8,128)(2,1)S(1)}, u32[]{:S(2)}, u32[]{:S(2)}) collective-permute-start(bf16[64,2304]{1,0:T(8,128)(2,1)S(1)} %add_up.3), channel_id=1, source_target_pairs={{0,2},{1,3},{2,0},{3,1},{4,6},{5,7},{6,4},{7,5},{8,10},{9,11},{10,... | collective-permute-start | bytes 884744 | tf_op jit(solution)/shard_map/ppermute | solution.py:22
  34.3 1.6 %collective-permute-start.13 = (bf16[64,1792]{1,0:T(8,128)(2,1)S(1)}, bf16[64,1792]{1,0:T(8,128)(2,1)S(1)}, u32[]{:S(2)}, u32[]{:S(2)}) collective-permute-start(bf16[64,1792]{1,0:T(8,128)(2,1)S(1)} %get-tuple-element.60), channel_id=1, source_target_pairs={{0,1},{1,0},{2,3},{3,2},{4,5},{5,4},{6,7},{7,6},{8,9},{9,8},{10,11... | collective-permute-start | bytes 688136 | tf_op jit(solution)/shard_map/ppermute | solution.py:22
  34.4 1.8 %collective-permute-start.14 = (bf16[64,1792]{1,0:T(8,128)(2,1)S(1)}, bf16[64,1792]{1,0:T(8,128)(2,1)S(1)}, u32[]{:S(2)}, u32[]{:S(2)}) collective-permute-start(bf16[64,1792]{1,0:T(8,128)(2,1)S(1)} %get-tuple-element.61), channel_id=1, source_target_pairs={{0,1},{1,0},{2,3},{3,2},{4,5},{5,4},{6,7},{7,6},{8,9},{9,8},{10,11... | collective-permute-start | bytes 688136 | tf_op jit(solution)/shard_map/ppermute | solution.py:22
  34.9 1.6 %collective-permute-start.15 = (bf16[64,1792]{1,0:T(8,128)(2,1)S(1)}, bf16[64,1792]{1,0:T(8,128)(2,1)S(1)}, u32[]{:S(2)}, u32[]{:S(2)}) collective-permute-start(bf16[64,1792]{1,0:T(8,128)(2,1)S(1)} %get-tuple-element.62), channel_id=1, source_target_pairs={{0,1},{1,0},{2,3},{3,2},{4,5},{5,4},{6,7},{7,6},{8,9},{9,8},{10,11... | collective-permute-start | bytes 688136 | tf_op jit(solution)/shard_map/ppermute | solution.py:22
